TPU v7x, 32 devices: a whole 2x2x4 slice. The times are simulated.
32 devices in a mesh: mem: 4 (over x, core), tile: 8 (over z, y).
Axes of the slice: x: 2, y: 2, z: 4, core: 2. Of those that a mesh axis runs over, the one named last changes fastest.
Arguments:
- latents: float32 [24, 256], P('mem'), may hold values from -6 to 6
- basis: bfloat16 [256, 2, 128, 512], P(None, None, 'tile'), may hold values from -0.375 to 0.375
- conv_in: bfloat16 [9, 64], replicated, may hold values from -2 to 2
- conv_mid: bfloat16 [9, 64, 64], replicated, may hold values from -0.25 to 0.25
- conv_out: bfloat16 [64], replicated, may hold values from -0.75 to 0.75
- pressure_prev: float32 [2, 128, 512], P(None, 'tile'), may hold values from -6 to 6
- source: float32 [2, 128, 512], P(None, 'tile'), may hold values from -6 to 6
- perf_cells: int32 [384, 8], replicated, may hold values from 0 to 131071
- perf_count: int32 [384], replicated, may hold values from 1 to 8
- obs_perturbed: float32 [24, 384], replicated, may hold values from -6 to 6
- obs_error: float32 [384], replicated, may hold values from 0.2 to 2
Outputs:
- pressure: float32 [24, 2, 128, 512], P(None, None, 'tile', 'mem')
- well_data: float32 [24, 384], replicated
- latents_new: float32 [24, 256], P('mem')
All inputs are finite; a program needn't handle non-finite values.
Results may differ from a plain program's by a relative error of at most 0.0055.
Values may be sent and summed in bfloat16 or wider, within the bound.
No kernel may reach another device: no remote copies, remote signals or barrier semaphores. Data moves between devices by JAX's collectives and lax.ppermute only.
A program may use at most 128 MiB of HBM per device.

v0:
```python
import math

import jax
import jax.numpy as jnp
from jax import lax
from jax.sharding import PartitionSpec as P

SWEEPS = 2


storage_coef = 1.0


def extended(cells, sides, width):
    for axis, dim in sides:
        count = lax.axis_size(axis)
        ends = count - 1
        head = lax.slice_in_dim(cells, 0, width, axis=dim)
        tail = lax.slice_in_dim(cells, cells.shape[dim] - width, cells.shape[dim], axis=dim)
        cells = jnp.concatenate(
            [
                lax.ppermute(tail, axis, [(i, (i + 1) % count) for i in range(ends)]),
                cells,
                lax.ppermute(head, axis, [((i + 1) % count, i) for i in range(ends)]),
            ],
            axis=dim,
        )
    return cells


def lift(field, conv_in):
    rows = field.shape[1] - 2
    width = field.shape[2]
    padded = jnp.pad(field, ((0, 0), (0, 0), (1, 1)))
    total = jnp.zeros((field.shape[0], conv_in.shape[1], rows, width), jnp.float32)
    for tap in range(9):
        part = padded[:, tap // 3 : tap // 3 + rows, tap % 3 : tap % 3 + width]
        total = total + conv_in[tap].astype(jnp.float32)[None, :, None, None] * part[:, None]
    return jax.nn.relu(total).astype(jnp.bfloat16)


def mix(lifted, field, conv_mid, conv_out):
    rows = field.shape[1]
    width = field.shape[2]
    padded = jnp.pad(lifted, ((0, 0), (0, 0), (0, 0), (1, 1)))
    total = jnp.zeros((field.shape[0], conv_mid.shape[1], rows, width), jnp.float32)
    for tap in range(9):
        part = padded[:, :, tap // 3 : tap // 3 + rows, tap % 3 : tap % 3 + width]
        total = total + jnp.einsum(
            "oc,zcxy->zoxy", conv_mid[tap], part, preferred_element_type=jnp.float32
        )
    deep = jax.nn.relu(total)
    return field + jnp.einsum("c,zcxy->zxy", conv_out.astype(jnp.float32), deep)


def neighbours(wide):
    zpad = jnp.pad(wide, ((0, 0), (1, 1), (0, 0), (0, 0)))
    return [
        zpad[:, 1:-1, 2:, 1:-1],
        zpad[:, 1:-1, :-2, 1:-1],
        zpad[:, 1:-1, 1:-1, 2:],
        zpad[:, 1:-1, 1:-1, :-2],
        zpad[:, 2:, 1:-1, 1:-1],
        zpad[:, :-2, 1:-1, 1:-1],
    ]


def well_terms(perm, press, perf_cells, perf_count, row_start, col_start, grid_rows, grid_cols):
    members = perm.shape[0]
    rows = perm.shape[2]
    width = perm.shape[3]
    wells = perf_cells.shape[0]
    slots = perf_cells.shape[1]
    ids = perf_cells.reshape(-1)
    layer_of = ids // (grid_rows * grid_cols)
    rest = ids % (grid_rows * grid_cols)
    row_local = rest // grid_cols - row_start
    col_local = rest % grid_cols - col_start
    inside = (row_local >= 0) & (row_local < rows) & (col_local >= 0) & (col_local < width)
    local_ids = jnp.where(inside, layer_of * rows * width + row_local * width + col_local, 0)
    used = (jnp.arange(slots)[None, :] < perf_count[:, None]).reshape(-1) & inside
    weight = used.astype(jnp.float32)
    perm_at = jnp.take(perm.reshape(members, -1), local_ids, axis=1) * weight[None, :]
    press_at = jnp.take(press.reshape(members, -1), local_ids, axis=1)
    numer = jnp.sum((perm_at * press_at).reshape(members, wells, slots), axis=2)
    weight_sum = jnp.sum(perm_at.reshape(members, wells, slots), axis=2)
    return (numer, weight_sum)


def body(
    latents,
    basis,
    conv_in,
    conv_mid,
    conv_out,
    pressure_prev,
    source,
    perf_cells,
    perf_count,
    obs_perturbed,
    obs_error,
):
    mem_dev = latents.shape[0]
    layers = basis.shape[1]
    rows = basis.shape[2]
    width = basis.shape[3]
    tile_at = lax.axis_index("tile")
    mem_at = lax.axis_index("mem")
    grid_rows = rows * lax.axis_size("tile")
    flat_basis = basis.reshape(basis.shape[0], -1)
    field = jnp.dot(latents.astype(jnp.bfloat16), flat_basis, preferred_element_type=jnp.float32)
    field = field.reshape(mem_dev, layers, rows, width)
    wide = extended(field, (("tile", 2),), 1)
    lifted = lax.map(lambda single: lift(single, conv_in), wide)
    lifted_wide = extended(lifted, (("tile", 3),), 1)
    log_perm = lax.map(lambda pair: mix(pair[0], pair[1], conv_mid, conv_out), (lifted_wide, field))
    base_full = storage_coef * pressure_prev + source
    log_tiles = lax.all_to_all(log_perm, "mem", split_axis=3, concat_axis=0, tiled=True)
    cols = log_tiles.shape[3]
    perm = jnp.exp(log_tiles)
    base = lax.dynamic_slice_in_dim(base_full, mem_at * cols, cols, 2)
    prev_local = lax.dynamic_slice_in_dim(pressure_prev, mem_at * cols, cols, 2)
    perm_wide = extended(perm, (("mem", 3), ("tile", 2)), 1)
    conduct = [2.0 * perm * other / (perm + other) for other in neighbours(perm_wide)]
    denom = storage_coef + sum(conduct)
    press = jnp.broadcast_to(prev_local, perm.shape)
    for sweep in range(SWEEPS):
        press_wide = extended(press, (("mem", 3), ("tile", 2)), 1)
        acc = base[None] + sum((cval * nval for cval, nval in zip(conduct, neighbours(press_wide))))
        press = acc / denom
    numer, weight_sum = well_terms(
        perm,
        press,
        perf_cells,
        perf_count,
        tile_at * rows,
        mem_at * cols,
        grid_rows,
        cols * lax.axis_size("mem"),
    )
    members = press.shape[0]
    numer, weight_sum = lax.psum((numer, weight_sum), ("mem", "tile"))
    well_data = numer / weight_sum
    scale = 2.0 * obs_error
    centred = well_data - jnp.mean(well_data, axis=0, keepdims=True)
    scaled = centred / (math.sqrt(members - 1) * scale[None, :])
    innov = (obs_perturbed - well_data) / scale[None, :]
    gram = jnp.eye(members, dtype=jnp.float32) + jnp.dot(
        scaled, scaled.T, precision=lax.Precision.HIGHEST
    )
    cross = jnp.dot(scaled, innov.T, precision=lax.Precision.HIGHEST)
    factor = jnp.linalg.cholesky(gram)
    weights = jax.scipy.linalg.cho_solve((factor, True), cross)
    every = lax.all_gather(latents, "mem", axis=0, tiled=True)
    spread = (every - jnp.mean(every, axis=0, keepdims=True)) / math.sqrt(members - 1)
    own_weights = lax.dynamic_slice_in_dim(weights, mem_at * mem_dev, mem_dev, 1)
    latents_new = latents + jnp.dot(own_weights.T, spread, precision=lax.Precision.HIGHEST)
    return (press, well_data, latents_new)


def solution(mesh):
    return jax.shard_map(
        body,
        mesh=mesh,
        in_specs=(
            P("mem", None),
            P(None, None, "tile", None),
            P(),
            P(),
            P(),
            P(None, "tile", None),
            P(None, "tile", None),
            P(),
            P(),
            P(),
            P(),
        ),
        out_specs=(P(None, None, "tile", "mem"), P(), P("mem", None)),
        check_vma=False,
    )
```

profile of v0, /device:TPU:0, one launch (start us, length us, event | category | flops | bytes accessed | tf_op | source)
XLA Modules:
  0.0 630.6 jit_solution(1429464906320155200)
XLA Ops:
  7.2 15.4 %copy.59 = bf16[32,8,32,512]{3,1,2,0:T(8,128)(2,1)} copy(bf16[32,8,32,512]{3,2,1,0:T(8,128)(2,1)} %bitcast.226) | data formatting | bytes 16777216
  22.6 11.9 %copy.29 = bf16[16384,256]{1,0:T(8,128)(2,1)} copy(bf16[16384,256]{0,1:T(8,128)(2,1)} %bitcast.222) | data formatting | bytes 16777216 | tf_op jit(solution)/shard_map/dot_general | solution.py:111
  34.5 5.6 fusion.110
  40.1 4.9 collective-permute-start
  46.6 4.2 collective-permute-done.1
  50.9 35.6 %while.24 = (s32[]{:T(128)}, bf16[6,2,64,16,512]{4,2,3,1,0:T(8,128)(2,1)}, bf16[9,64]{1,0:T(8,128)(2,1)S(1)}, f32[6,2,18,512]{3,0,2,1:T(8,128)S(1)}, s32[]{:T(128)}) while((s32[]{:T(128)}, bf16[6,2,64,16,512]{4,2,3,1,0:T(8,128)(2,1)}, bf16[9,64]{1,0:T(8,128)(2,1)S(1)}, f32[6,2,18,512]{3,0,2,1:T(8,128)S(1)}, s32[]{:T(128)}) %tuple.105), condition=%wide.region_1.2_spmd, body=%wide.region_0.1_spmd.sunk | while | flops 19923520 | bytes 8067265 | solution.py:114
  89.3 4.4 collective-permute-start.2
  101.9 24.2 %collective-permute-done.2 = bf16[6,2,64,1,512]{4,2,3,1,0:T(8,128)(2,1)S(1)} collective-permute-done((bf16[6,2,64,1,512]{4,2,3,1,0:T(8,128)(2,1)}, bf16[6,2,64,1,512]{4,2,3,1,0:T(8,128)(2,1)S(1)}, u32[]{:S(2)}, u32[]{:S(2)}) %collective-permute-start.2) | collective-permute-done | bytes 786464 | tf_op jit(solution)/shard_map/ppermute | solution.py:22
  126.1 10.3 %pad_maximum_fusion = bf16[6,2,64,18,512]{4,2,3,1,0:T(8,128)(2,1)} fusion(bf16[6,2,64,1,512]{4,2,3,1,0:T(8,128)(2,1)S(1)} %collective-permute-done.3, bf16[6,2,64,16,512]{4,2,3,1,0:T(8,128)(2,1)} %get-tuple-element.134, bf16[6,2,64,1,512]{4,2,3,1,0:T(8,128)(2,1)S(1)} %collective-permute-done.2), kind=kLoop, calls=%fused_computation.83 | loop fusion | flops 14155776 | bytes 28311552 | tf_op jit(solution)/shard_map/concatenate | solution.py:20
  136.5 224.6 %while.25 = (s32[]{:T(128)}, f32[6,2,16,512]{3,2,1,0:T(8,128)S(1)}, f32[6,2,16,512]{3,0,2,1:T(8,128)S(1)}, bf16[6,2,64,18,512]{4,2,3,1,0:T(8,128)(2,1)}, bf16[9,...) while((s32[]{:T(128)}, f32[6,2,16,512]{3,2,1,0:T(8,128)S(1)}, ...), condition=%wide.region_3.4_spmd, body=%wide.region_2.3_spmd.sunk | while | flops 1219510272 | bytes 92815952 | solution.py:116
  160.4 13.4 %fusion.170 = f32[1,2,16,512]{3,0,2,1:T(1,128)S(1)} fusion(f32[2,16,512,64]{2,3,1,0:T(8,128)} %fusion.162, f32[2,16,512,64]{2,3,1,0:T(8,128)} %fusion.163, f32[2,16,512,64]{2,3,1,0:T(8,128)} %fusion.164, f32[2,16,512,64]{2,3,1,0:T(8,128)} %fusion.165, f32[2,16,512,64]{2,3,1,0:T(8,128)} %fusion.166, f32[2,16,512,64]{2,3,1,0:T(8,128)} %fusion.167, ...), kind=kOutput, calls=%fused_computation.21.clone.1 | convolution fusion | flops 145752064 | bytes 35996160 | tf_op jit(solution)/shard_map/while/body/eval_jaxpr/c,zcxy->zxy/dot_general | solution.py:53
  197.8 13.4 %fusion.170 = f32[1,2,16,512]{3,0,2,1:T(1,128)S(1)} fusion(f32[2,16,512,64]{2,3,1,0:T(8,128)} %fusion.162, f32[2,16,512,64]{2,3,1,0:T(8,128)} %fusion.163, f32[2,16,512,64]{2,3,1,0:T(8,128)} %fusion.164, f32[2,16,512,64]{2,3,1,0:T(8,128)} %fusion.165, f32[2,16,512,64]{2,3,1,0:T(8,128)} %fusion.166, f32[2,16,512,64]{2,3,1,0:T(8,128)} %fusion.167, ...), kind=kOutput, calls=%fused_computation.21.clone.1 | convolution fusion | flops 145752064 | bytes 35996160 | tf_op jit(solution)/shard_map/while/body/eval_jaxpr/c,zcxy->zxy/dot_general | solution.py:53
  235.2 13.4 %fusion.170 = f32[1,2,16,512]{3,0,2,1:T(1,128)S(1)} fusion(f32[2,16,512,64]{2,3,1,0:T(8,128)} %fusion.162, f32[2,16,512,64]{2,3,1,0:T(8,128)} %fusion.163, f32[2,16,512,64]{2,3,1,0:T(8,128)} %fusion.164, f32[2,16,512,64]{2,3,1,0:T(8,128)} %fusion.165, f32[2,16,512,64]{2,3,1,0:T(8,128)} %fusion.166, f32[2,16,512,64]{2,3,1,0:T(8,128)} %fusion.167, ...), kind=kOutput, calls=%fused_computation.21.clone.1 | convolution fusion | flops 145752064 | bytes 35996160 | tf_op jit(solution)/shard_map/while/body/eval_jaxpr/c,zcxy->zxy/dot_general | solution.py:53
  272.7 13.4 %fusion.170 = f32[1,2,16,512]{3,0,2,1:T(1,128)S(1)} fusion(f32[2,16,512,64]{2,3,1,0:T(8,128)} %fusion.162, f32[2,16,512,64]{2,3,1,0:T(8,128)} %fusion.163, f32[2,16,512,64]{2,3,1,0:T(8,128)} %fusion.164, f32[2,16,512,64]{2,3,1,0:T(8,128)} %fusion.165, f32[2,16,512,64]{2,3,1,0:T(8,128)} %fusion.166, f32[2,16,512,64]{2,3,1,0:T(8,128)} %fusion.167, ...), kind=kOutput, calls=%fused_computation.21.clone.1 | convolution fusion | flops 145752064 | bytes 35996160 | tf_op jit(solution)/shard_map/while/body/eval_jaxpr/c,zcxy->zxy/dot_general | solution.py:53
  310.1 13.4 %fusion.170 = f32[1,2,16,512]{3,0,2,1:T(1,128)S(1)} fusion(f32[2,16,512,64]{2,3,1,0:T(8,128)} %fusion.162, f32[2,16,512,64]{2,3,1,0:T(8,128)} %fusion.163, f32[2,16,512,64]{2,3,1,0:T(8,128)} %fusion.164, f32[2,16,512,64]{2,3,1,0:T(8,128)} %fusion.165, f32[2,16,512,64]{2,3,1,0:T(8,128)} %fusion.166, f32[2,16,512,64]{2,3,1,0:T(8,128)} %fusion.167, ...), kind=kOutput, calls=%fused_computation.21.clone.1 | convolution fusion | flops 145752064 | bytes 35996160 | tf_op jit(solution)/shard_map/while/body/eval_jaxpr/c,zcxy->zxy/dot_general | solution.py:53
  347.6 13.4 %fusion.170 = f32[1,2,16,512]{3,0,2,1:T(1,128)S(1)} fusion(f32[2,16,512,64]{2,3,1,0:T(8,128)} %fusion.162, f32[2,16,512,64]{2,3,1,0:T(8,128)} %fusion.163, f32[2,16,512,64]{2,3,1,0:T(8,128)} %fusion.164, f32[2,16,512,64]{2,3,1,0:T(8,128)} %fusion.165, f32[2,16,512,64]{2,3,1,0:T(8,128)} %fusion.166, f32[2,16,512,64]{2,3,1,0:T(8,128)} %fusion.167, ...), kind=kOutput, calls=%fused_computation.21.clone.1 | convolution fusion | flops 145752064 | bytes 35996160 | tf_op jit(solution)/shard_map/while/body/eval_jaxpr/c,zcxy->zxy/dot_general | solution.py:53
  363.2 5.0 reshape.341
  368.2 3.5 all-to-all-start
  371.6 8.3 %all-reduce.8.cloned.1.call-start = ((), (), s32[]{:S(2)}) async-start(), calls=%async_computation.1 | async-start | bytes 786432 | tf_op jit(solution)/shard_map/psum | solution.py:142
  384.1 4.2 reshape.342
  391.6 3.9 copy.36
  400.7 4.3 collective-permute-start.11
  406.7 4.5 collective-permute-start.10
  414.4 3.3 collective-permute-done.6
  418.4 4.8 fusion.71
  427.2 5.2 collective-permute-done.13
  434.0 5.4 collective-permute-start.15
  439.5 9.8 %all-gather = f32[4,6,256]{2,1,0:T(8,128)S(1)} all-gather(f32[1,6,256]{2,1,0:T(8,128)S(1)} %bitcast.227), channel_id=1, replica_groups=mesh['mem'=4,'tile'=8] {'mem'}, dimensions={0}, use_global_device_ids=true | all-gather | bytes 30720 | tf_op jit(solution)/shard_map/all_gather | solution.py:154
  451.8 10.8 %gather_fusion = f32[3072,24]{1,0:T(8,128)} fusion(f32[24,4096]{0,1:T(8,128)S(1)} %copy.38, s32[3072]{0:T(1024)S(1)} %broadcast_clamp_fusion), kind=kCustom, calls=%fused_computation.clone | custom fusion | bytes 602112 | tf_op jit(solution)/shard_map/jit(_take)/gather | solution.py:83
  468.4 10.8 %gather_fusion.1 = f32[3072,24]{1,0:T(8,128)} fusion(f32[24,4096]{0,1:T(8,128)S(1)} %bitcast.225, s32[3072]{0:T(1024)S(1)} %broadcast_clamp_fusion), kind=kCustom, calls=%fused_computation.1.clone | custom fusion | bytes 602112 | tf_op jit(solution)/shard_map/jit(_take)/gather | solution.py:84
  479.2 4.6 bitcast_reduce_fusion
  484.0 129.5 %all-reduce.8.cloned.1.call-done = (f32[24,384]{0,1:T(8,128)}, f32[24,384]{0,1:T(8,128)}) async-done(((f32[24,384]{0,1:T(8,128)}, f32[24,384]{0,1:T(8,128)}), (f32[24,384]{0,1:T(8,128)}, f32[24,384]{0,1:T(8,128)})) %all-reduce.8.cloned.1.call-update) | async-done | bytes 73744 | tf_op jit(solution)/shard_map/psum | solution.py:142
  (231 shorter events, 235.7 us)
Async XLA Ops:
  22.6 11.9 %copy-start.12 = (f32[6,256]{1,0:T(8,128)S(1)}, f32[6,256]{1,0:T(8,128)}, u32[]{:S(2)}) copy-start(f32[6,256]{1,0:T(8,128)} %param.17) | copy-start | bytes 18436
  34.5 16.4 %copy-start.11 = (bf16[9,64]{1,0:T(8,128)(2,1)S(1)}, bf16[9,64]{1,0:T(8,128)(2,1)}, u32[]{:S(2)}) copy-start(bf16[9,64]{1,0:T(8,128)(2,1)} %param.19) | copy-start | bytes 3460
  40.1 6.5 %collective-permute-start = (f32[6,2,1,512]{3,0,2,1:T(8,128)S(1)}, f32[6,2,1,512]{3,0,2,1:T(8,128)S(1)}, u32[]{:S(2)}, u32[]{:S(2)}) collective-permute-start(f32[6,2,1,512]{3,0,2,1:T(8,128)S(1)} %get-tuple-element.228), channel_id=1, source_target_pairs={{0,1},{1,2},{2,3},{3,4},{4,5},{5,6},{6,7},{8,9},{9,10},{10,11},{11... | collective-permute-start | bytes 73736 | tf_op jit(solution)/shard_map/ppermute | solution.py:22
  45.0 5.8 collective-permute-start.1
  86.6 13.6 %copy-start.22 = (s32[384,8]{0,1:T(8,128)S(1)}, s32[384,8]{0,1:T(8,128)}, u32[]{:S(2)}) copy-start(s32[384,8]{0,1:T(8,128)} %param.24) | copy-start | bytes 36868
  86.6 14.5 %copy-start.24 = (s32[384]{0:T(512)S(1)}, s32[384]{0:T(512)}, u32[]{:S(2)}) copy-start(s32[384]{0:T(512)} %param.25) | copy-start | bytes 4612
  89.3 36.8 %collective-permute-start.2 = (bf16[6,2,64,1,512]{4,2,3,1,0:T(8,128)(2,1)}, bf16[6,2,64,1,512]{4,2,3,1,0:T(8,128)(2,1)S(1)}, u32[]{:S(2)}, u32[]{:S(2)}) collective-permute-start(bf16[6,2,64,1,512]{4,2,3,1,0:T(8,128)(2,1)} %get-tuple-element.220), channel_id=1, source_target_pairs={{0,1},{1,2},{2,3},{3,4},{4,5},{5,6},{6,7},{8,9},{9,10},{10,11},{11... | collective-permute-start | bytes 2359304 | tf_op jit(solution)/shard_map/ppermute | solution.py:22
  93.7 32.5 %collective-permute-start.3 = (bf16[6,2,64,1,512]{4,2,3,1,0:T(8,128)(2,1)}, bf16[6,2,64,1,512]{4,2,3,1,0:T(8,128)(2,1)S(1)}, u32[]{:S(2)}, u32[]{:S(2)}) collective-permute-start(bf16[6,2,64,1,512]{4,2,3,1,0:T(8,128)(2,1)} %get-tuple-element.221), channel_id=1, source_target_pairs={{1,0},{2,1},{3,2},{4,3},{5,4},{6,5},{7,6},{9,8},{10,9},{11,10},{12... | collective-permute-start | bytes 2359304 | tf_op jit(solution)/shard_map/ppermute | solution.py:24
  96.0 303.1 %collective-permute-start.7 = (f32[24,2,16,1]{3,2,1,0:T(8,128)}, f32[24,2,16,1]{3,2,1,0:T(8,128)}, u32[]{:S(2)}, u32[]{:S(2)}) collective-permute-start(f32[24,2,16,1]{3,2,1,0:T(8,128)} %broadcast_in_dim.48), channel_id=1, source_target_pairs={{0,8},{8,16},{16,24},{1,9},{9,17},{17,25},{2,10},{10,18},{18,26},{... | collective-permute-start | bytes 9224 | tf_op jit(solution)/shard_map/ppermute | solution.py:22
  98.9 300.2 %collective-permute-start.8 = (f32[24,2,16,1]{3,2,1,0:T(8,128)}, f32[24,2,16,1]{3,2,1,0:T(8,128)}, u32[]{:S(2)}, u32[]{:S(2)}) collective-permute-start(f32[24,2,16,1]{3,2,1,0:T(8,128)} %broadcast_in_dim.50), channel_id=1, source_target_pairs={{8,0},{16,8},{24,16},{9,1},{17,9},{25,17},{10,2},{18,10},{26,18},{... | collective-permute-start | bytes 9224 | tf_op jit(solution)/shard_map/ppermute | solution.py:24
  101.9 34.6 %copy-start.3 = (bf16[9,64,64]{2,1,0:T(8,128)(2,1)S(1)}, bf16[9,64,64]{2,1,0:T(8,128)(2,1)}, u32[]{:S(2)}) copy-start(bf16[9,64,64]{2,1,0:T(8,128)(2,1)} %param.20) | copy-start | bytes 221188
  101.9 34.6 %copy-start.20 = (bf16[64]{0:T(256)(128)(2,1)S(1)}, bf16[64]{0:T(256)(128)(2,1)}, u32[]{:S(2)}) copy-start(bf16[64]{0:T(256)(128)(2,1)} %param.21) | copy-start | bytes 388
  363.1 18.1 %copy-start.15 = (s32[3072]{0:T(1024)S(1)}, s32[3072]{0:T(1024)}, u32[]{:S(2)}) copy-start(s32[3072]{0:T(1024)} %reshape.290) | copy-start | bytes 36868
  363.2 18.1 %copy-start.23 = (pred[3072]{0:T(1024)(128)(4,1)S(1)}, pred[3072]{0:T(1024)(128)(4,1)}, u32[]{:S(2)}) copy-start(pred[3072]{0:T(1024)(128)(4,1)} %lt.76) | copy-start | bytes 9220
  368.2 13.8 %all-to-all-start = ((f32[4,1,24576]{2,1,0:T(1,128)}), f32[4,1,24576]{2,1,0:T(1,128)S(1)}, u32[]{:S(2)}, u32[]{:S(2)}) async-start(f32[4,1,24576]{2,1,0:T(1,128)} %reshape.341), calls=%async_computation | async-start | bytes 786432 | tf_op jit(solution)/shard_map/all_to_all | solution.py:118
  371.6 241.9 %all-reduce.8.cloned.1.call-start = ((), (), s32[]{:S(2)}) async-start(), calls=%async_computation.1 | async-start | bytes 786432 | tf_op jit(solution)/shard_map/psum | solution.py:142
  395.6 10.7 %collective-permute-start.4 = (f32[24,2,16,1]{3,2,1,0:T(8,128)S(1)}, f32[24,2,16,1]{3,2,1,0:T(8,128)S(1)}, u32[]{:S(2)}, u32[]{:S(2)}) collective-permute-start(f32[24,2,16,1]{3,2,1,0:T(8,128)S(1)} %get-tuple-element.232), channel_id=1, source_target_pairs={{0,8},{8,16},{16,24},{1,9},{9,17},{17,25},{2,10},{10,18},{18,26},{... | collective-permute-start | bytes 9224 | tf_op jit(solution)/shard_map/ppermute | solution.py:22
  397.8 8.6 %collective-permute-start.5 = (f32[24,2,16,1]{3,2,1,0:T(8,128)S(1)}, f32[24,2,16,1]{3,2,1,0:T(8,128)S(1)}, u32[]{:S(2)}, u32[]{:S(2)}) collective-permute-start(f32[24,2,16,1]{3,2,1,0:T(8,128)S(1)} %get-tuple-element.233), channel_id=1, source_target_pairs={{8,0},{16,8},{24,16},{9,1},{17,9},{25,17},{10,2},{18,10},{26,18},{... | collective-permute-start | bytes 9224 | tf_op jit(solution)/shard_map/ppermute | solution.py:24
  400.7 11.9 %collective-permute-start.11 = (f32[24,2,1,130]{3,2,1,0:T(1,128)S(1)}, f32[24,2,1,130]{3,2,1,0:T(1,128)S(1)}, u32[]{:S(2)}, u32[]{:S(2)}) collective-permute-start(f32[24,2,1,130]{3,2,1,0:T(1,128)S(1)} %get-tuple-element.226), channel_id=1, source_target_pairs={{0,1},{1,2},{2,3},{3,4},{4,5},{5,6},{6,7},{8,9},{9,10},{10,11},{11... | collective-permute-start | bytes 74888 | tf_op jit(solution)/shard_map/ppermute | solution.py:22
  405.0 7.6 %collective-permute-start.9 = (f32[24,2,1,130]{3,2,1,0:T(1,128)S(1)}, f32[24,2,1,130]{3,2,1,0:T(1,128)S(1)}, u32[]{:S(2)}, u32[]{:S(2)}) collective-permute-start(f32[24,2,1,130]{3,2,1,0:T(1,128)S(1)} %get-tuple-element.227), channel_id=1, source_target_pairs={{1,0},{2,1},{3,2},{4,3},{5,4},{6,5},{7,6},{9,8},{10,9},{11,10},{12... | collective-permute-start | bytes 74888 | tf_op jit(solution)/shard_map/ppermute | solution.py:24
  406.4 12.0 %copy-start.1 = (f32[24,2,16,1]{3,2,1,0:T(8,128)}, f32[24,2,16,1]{3,2,1,0:T(8,128)S(1)}, u32[]{:S(2)}) copy-start(f32[24,2,16,1]{3,2,1,0:T(8,128)S(1)} %collective-permute-done.5) | copy-start | bytes 9220
  406.7 7.6 %collective-permute-start.10 = (f32[24,2,1,130]{3,2,1,0:T(1,128)S(1)}, f32[24,2,1,130]{3,2,1,0:T(1,128)S(1)}, u32[]{:S(2)}, u32[]{:S(2)}) collective-permute-start(f32[24,2,1,130]{3,2,1,0:T(1,128)S(1)} %get-tuple-element.224), channel_id=1, source_target_pairs={{0,1},{1,2},{2,3},{3,4},{4,5},{5,6},{6,7},{8,9},{9,10},{10,11},{11... | collective-permute-start | bytes 74888 | tf_op jit(solution)/shard_map/ppermute | solution.py:22
  411.3 6.4 %collective-permute-start.6 = (f32[24,2,1,130]{3,2,1,0:T(1,128)S(1)}, f32[24,2,1,130]{3,2,1,0:T(1,128)S(1)}, u32[]{:S(2)}, u32[]{:S(2)}) collective-permute-start(f32[24,2,1,130]{3,2,1,0:T(1,128)S(1)} %get-tuple-element.225), channel_id=1, source_target_pairs={{1,0},{2,1},{3,2},{4,3},{5,4},{6,5},{7,6},{9,8},{10,9},{11,10},{12... | collective-permute-start | bytes 74888 | tf_op jit(solution)/shard_map/ppermute | solution.py:24
  423.2 16.3 %copy-start.25 = (f32[384]{0:T(512)S(1)}, f32[384]{0:T(512)}, u32[]{:S(2)}) copy-start(f32[384]{0:T(512)} %param.27) | copy-start | bytes 4612
  423.2 16.4 %copy-start.13 = (f32[6,256]{1,0:T(8,128)S(1)}, f32[6,256]{1,0:T(8,128)}, u32[]{:S(2)}) copy-start(f32[6,256]{1,0:T(8,128)} %param.17) | copy-start | bytes 18436
  423.4 3.8 collective-permute-start.12
  425.8 6.5 %collective-permute-start.13 = (f32[24,2,16,1]{3,2,1,0:T(8,128)S(1)}, f32[24,2,16,1]{3,2,1,0:T(8,128)S(1)}, u32[]{:S(2)}, u32[]{:S(2)}) collective-permute-start(f32[24,2,16,1]{3,2,1,0:T(8,128)S(1)} %get-tuple-element.231), channel_id=1, source_target_pairs={{8,0},{16,8},{24,16},{9,1},{17,9},{25,17},{10,2},{18,10},{26,18},{... | collective-permute-start | bytes 9224 | tf_op jit(solution)/shard_map/ppermute | solution.py:24
  427.2 22.2 %copy-start.4 = (f32[24,2,16,1]{3,2,1,0:T(8,128)}, f32[24,2,16,1]{3,2,1,0:T(8,128)S(1)}, u32[]{:S(2)}) copy-start(f32[24,2,16,1]{3,2,1,0:T(8,128)S(1)} %collective-permute-done.12) | copy-start | bytes 9220
  432.4 17.0 %copy-start.6 = (f32[24,2,16,1]{3,2,1,0:T(8,128)}, f32[24,2,16,1]{3,2,1,0:T(8,128)S(1)}, u32[]{:S(2)}) copy-start(f32[24,2,16,1]{3,2,1,0:T(8,128)S(1)} %collective-permute-done.13) | copy-start | bytes 9220
  432.7 29.9 %collective-permute-start.14 = (f32[24,2,1,130]{3,2,1,0:T(1,128)S(1)}, f32[24,2,1,130]{3,2,1,0:T(1,128)S(1)}, u32[]{:S(2)}, u32[]{:S(2)}) collective-permute-start(f32[24,2,1,130]{3,2,1,0:T(1,128)S(1)} %get-tuple-element.223), channel_id=1, source_target_pairs={{1,0},{2,1},{3,2},{4,3},{5,4},{6,5},{7,6},{9,8},{10,9},{11,10},{12... | collective-permute-start | bytes 74888 | tf_op jit(solution)/shard_map/ppermute | solution.py:24
  434.0 28.6 %collective-permute-start.15 = (f32[24,2,1,130]{3,2,1,0:T(1,128)S(1)}, f32[24,2,1,130]{3,2,1,0:T(1,128)S(1)}, u32[]{:S(2)}, u32[]{:S(2)}) collective-permute-start(f32[24,2,1,130]{3,2,1,0:T(1,128)S(1)} %get-tuple-element.222), channel_id=1, source_target_pairs={{0,1},{1,2},{2,3},{3,4},{4,5},{5,6},{6,7},{8,9},{9,10},{10,11},{11... | collective-permute-start | bytes 74888 | tf_op jit(solution)/shard_map/ppermute | solution.py:22
  467.7 11.5 %copy-start.8 = (f32[24,2,16,128]{3,2,1,0:T(8,128)}, f32[24,2,16,128]{3,2,1,0:T(8,128)S(1)}, u32[]{:S(2)}) copy-start(f32[24,2,16,128]{3,2,1,0:T(8,128)S(1)} %fusion.60) | copy-start | bytes 1179652
  (12 other events, 67.0 us)
Sparse Core Ops, SparseCore 0:
  484.0 129.4 all-reduce.7
where the time goes:
time: 638 us; the launch traced here: 631 us
  matrix products  221 us (35%)
  waiting for transfers between devices  166 us (26%)
  local copies, waits for them, and re-layouts  107 us (17%)
  other arithmetic  58.8 us (9%)
  starting transfers between devices  52.5 us (8%)
  between operations  14.9 us (2%)
  blocking collectives  9.76 us (2%)
    dot_general x48, matrix products, mix(): jnp.einsum('oc,zcxy->zoxy', conv_mid[tap], part, preferred_element_type=j...  132 us
    psum x1, waiting for transfers between devices, body(): numer, weight_sum = lax.psum((numer, weight_sum), ('mem', 'tile'))  129 us
    dot_general x6, matrix products, mix(): return field + jnp.einsum('c,zcxy->zxy', conv_out.astype(jnp.float32), deep)  80.6 us
    ppermute x8, starting transfers between devices, extended(): lax.ppermute(tail, axis, [(i, (i + 1) % count) for i in range(ends)])  30.1 us
    unnamed x59, local copies, waits for them, and re-layouts  25.7 us
    ppermute x8, waiting for transfers between devices, extended(): lax.ppermute(tail, axis, [(i, (i + 1) % count) for i in range(ends)])  24.2 us
    convert_element_type x6, other arithmetic, lift(): return jax.nn.relu(total).astype(jnp.bfloat16)  18.8 us
    concatenate x8, other arithmetic, extended(): jnp.concatenate([lax.ppermute(tail, axis, [(i, (i + 1) % count) for i in...  17 us
  transfers between devices with their start and end apart: 18, of which 5 were waited for; matrix products, arithmetic and copies ran while one was open for 44% of the time, Pallas kernels for 0%

commit v1 on v0

v1 whole, which is shorter than its diff:
```python
import functools
import math

import jax
import jax.numpy as jnp
from jax import lax
from jax.experimental import pallas as pl
from jax.experimental.pallas import tpu as pltpu
from jax.sharding import PartitionSpec as P

SWEEPS = 2
HALO = 4
RING = 24
LIFT_BLOCKS = 11
MIX_BLOCKS = 10
SEG = 16
BF = jnp.bfloat16
F32 = jnp.float32
VMEM = pl.BlockSpec(memory_space=pltpu.VMEM)
SMEM = pl.BlockSpec(memory_space=pltpu.SMEM)


def iota(shape, dim):
    return lax.broadcasted_iota(jnp.int32, shape, dim)


def field_kernel(lat_ref, basis_ref, prev_ref, src_ref, field_ref, low_ref, high_ref):
    step = pl.program_id(0)
    comps, layers, rows, width = basis_ref.shape
    members, total = lat_ref.shape
    span = comps * rows

    @pl.when(step == 0)
    def _():
        field_ref[...] = jnp.zeros_like(field_ref)

    pick = (iota((total, span), 0) == step * comps + iota((total, span), 1) // rows).astype(BF)
    spread = jnp.dot(lat_ref[...].astype(BF), pick, preferred_element_type=F32)
    own = iota((rows, span), 0) == iota((rows, span), 1) % rows
    left = jnp.where(own[None], spread[:, None, :], 0.0).astype(BF).reshape(members * rows, span)
    for z in range(layers):
        right = basis_ref[:, z].reshape(span, width)
        part = jnp.dot(left, right, preferred_element_type=F32)
        field_ref[z] = field_ref[z] + part.reshape(members, rows, width)

    @pl.when(step == pl.num_programs(0) - 1)
    def _():
        tiles = [field_ref.at[z, m] for z in range(layers) for m in range(members)]
        tiles += [prev_ref.at[z] for z in range(layers)] + [src_ref.at[z] for z in range(layers)]
        first = iota((8, width), 0) < HALO
        for pair in range(len(tiles) // 2):
            even, odd = tiles[2 * pair], tiles[2 * pair + 1]
            low_ref[pair] = jnp.where(first, even[0:8], pltpu.roll(odd[0:8], HALO, 0))
            high_ref[pair] = jnp.where(first, pltpu.roll(odd[rows - 8 : rows], HALO, 0), even[rows - 8 : rows])


def field_of(latents, basis, prev, src):
    total, layers, rows, width = basis.shape
    members = latents.shape[0]
    comps = 32
    pairs = (layers * members + 2 * layers) // 2
    whole = lambda shape: pl.BlockSpec(shape, lambda s: (0,) * len(shape))
    return pl.pallas_call(
        field_kernel,
        grid=(total // comps,),
        in_specs=[
            whole(latents.shape),
            pl.BlockSpec((comps, layers, rows, width), lambda s: (s, 0, 0, 0)),
            whole(prev.shape),
            whole(src.shape),
        ],
        out_specs=[
            whole((layers, members, rows, width)),
            whole((pairs, 8, width)),
            whole((pairs, 8, width)),
        ],
        out_shape=[
            jax.ShapeDtypeStruct((layers, members, rows, width), F32),
            jax.ShapeDtypeStruct((pairs, 8, width), F32),
            jax.ShapeDtypeStruct((pairs, 8, width), F32),
        ],
        compiler_params=pltpu.CompilerParams(vmem_limit_bytes=24 * 2**20),
    )(latents, basis, prev, src)


def block_row(block, half):
    return jnp.where(block == 0, jnp.where(half == 0, 18, -3), 2 * block - HALO + half)


def prep_kernel(grid_rows, rows, tile_ref, taps_ref, mid_ref, win_ref, wmix_ref):
    tile = tile_ref[0]
    shape = taps_ref.shape
    kinds = jnp.where(iota(shape, 0) >> 4 == iota(shape, 1) >> 6, taps_ref[...].astype(F32), 0.0).astype(BF)
    k, j = iota((256, 64), 0), iota((256, 64), 1)
    offset, ring = k >> 6, k & 31
    place, tap = j >> 4, j & 15
    xx, yy = place >> 1, place & 1
    a = ((tap * 11) >> 5) - 1
    b = tap - 3 * (a + 1) - 1
    fits = (tap < 9) & (offset == yy + b + 1)
    for block in range(LIFT_BLOCKS):
        if block == 0:
            row = jnp.where(xx == 0, 18, -3)
        else:
            row = 2 * block - HALO + xx
        near = row + a
        near = jnp.where(near < 0, near + RING, near)
        grid_row = tile * rows + row
        pick = fits & (ring == near) & (grid_row >= 0) & (grid_row < grid_rows)
        win_ref[block] = jnp.dot(jnp.where(pick, 1.0, 0.0).astype(BF), kinds, preferred_element_type=F32).astype(BF)
    o, n = iota((64, 256), 0), iota((64, 256), 1)
    placed = []
    for place_out in range(4):
        put = n == (o >> 5) * 128 + place_out * 32 + (o & 31)
        placed.append(jnp.dot(mid_ref[...], jnp.where(put, 1.0, 0.0).astype(BF), preferred_element_type=F32))
    for kind in range(4):
        side, over = kind & 1, kind >> 1
        for place_in in range(4):
            xi, yi = place_in >> 1, place_in & 1
            total = jnp.zeros((64, 256), F32)
            for place_out in range(4):
                xo, yo = place_out >> 1, place_out & 1
                dx = xi - xo + (0 if not over else (2 if xi == 0 else -2))
                dy = yi - yo + (0 if not side else (2 if yi == 0 else -2))
                if abs(dx) <= 1 and abs(dy) <= 1:
                    t = 3 * (dx + 1) + dy + 1
                    total = total + placed[place_out][64 * t : 64 * t + 64]
            at = 256 * kind + 64 * place_in
            wmix_ref[at : at + 64, :] = total.astype(BF)


def prep(tile_at, grid_rows, rows, conv_in, conv_mid):
    taps = jnp.tile(jnp.pad(conv_in, ((0, 7), (0, 0))), (4, 4))
    mid = jnp.transpose(conv_mid, (0, 2, 1)).reshape(-1, conv_mid.shape[1])
    return pl.pallas_call(
        functools.partial(prep_kernel, grid_rows, rows),
        in_specs=[SMEM, VMEM, VMEM],
        out_specs=[VMEM, VMEM],
        out_shape=[
            jax.ShapeDtypeStruct((LIFT_BLOCKS, 256, 256), BF),
            jax.ShapeDtypeStruct((1024, 256), BF),
        ],
        compiler_params=pltpu.CompilerParams(vmem_limit_bytes=24 * 2**20),
        cost_estimate=pl.CostEstimate(flops=400_000_000, bytes_accessed=4_000_000, transcendentals=0),
    )(tile_at, taps, mid)


def ring_tile(group, up_ref, down_ref):
    pair = group // 2
    up, down = up_ref[pair], down_ref[pair]
    first = iota(up.shape, 0) < HALO
    return jnp.where(first, up, down), pltpu.roll(jnp.where(first, down, up), HALO, 0)


def decode_kernel(
    grid_rows,
    tile_ref,
    field_ref,
    down_ref,
    up_ref,
    prev_ref,
    src_ref,
    win_ref,
    wmix_ref,
    out_ref,
    sel_ref,
    col_ref,
    press_ref,
    sums_ref,
    f_scr,
    t_scr,
    pt_scr,
    lift_scr,
    side_scr,
    deep_scr,
    wout_scr,
    v_scr,
):
    layers, members, rows, width = field_ref.shape
    groups = layers * members
    steps = width // (2 * SEG)
    block_rows = width // 2
    tile = tile_ref[0]

    def load(pair, _):
        up, down = up_ref[pair], down_ref[pair]
        first = iota(up.shape, 0) < HALO
        thirds = (jnp.where(first, up, down), pltpu.roll(jnp.where(first, down, up), HALO, 0))
        for half in range(2):
            group = 2 * pair + half
            own = field_ref[group // members, lax.rem(group, members)]
            f = jnp.concatenate([own, thirds[half]], axis=0)
            f_scr[group] = f
            hi = f.astype(BF).astype(F32)
            lo = f - hi
            zero = jnp.zeros((32 - RING, width), F32)
            edge = iota((RING, width), 1) == 0
            hi_left = jnp.where(edge, 0.0, pltpu.roll(hi, 1, 1))
            lo_left = jnp.where(edge, 0.0, pltpu.roll(lo, 1, 1))
            tall = jnp.concatenate([hi_left, zero, lo_left, zero, hi, zero, lo, zero], axis=0).T
            t_scr[0:width, :] = tall
            end = pltpu.roll(tall[width - 8 : width], 64, 1)
            end = jnp.where(iota(end.shape, 1) < 64, end, 0.0)
            t_scr[width : width + 8, :] = pltpu.roll(end, 1, 0)
            for q in range(steps + 1):
                part = t_scr[pl.ds(2 * q, SEG, stride=2 * steps), :].astype(BF)
                if q < steps:
                    pt_scr[pl.ds(pl.multiple_of(group * block_rows + q * SEG, SEG), SEG), 0:128] = part
                if q > 0:
                    pt_scr[pl.ds(pl.multiple_of(group * block_rows + (q - 1) * SEG, SEG), SEG), 128:256] = part
        return 0

    lax.fori_loop(0, groups // 2, load, 0)

    chunk = 4 * block_rows
    chunks = groups * block_rows // chunk

    def lift(t, _):
        block, part = t // chunks, lax.rem(t, chunks)
        at = pl.multiple_of(part * chunk, chunk)
        wide = jnp.dot(pt_scr[pl.ds(at, chunk), :], win_ref[block], preferred_element_type=F32)
        wide = jnp.maximum(wide, 0.0)
        tight = wide.astype(BF)
        lift_scr[block, pl.ds(at, chunk), :] = tight
        right = iota((SEG, 256), 1) & 64 == 0
        row = iota((SEG, 256), 0)
        for i in range(chunk // block_rows):
            base = i * block_rows
            last = base + block_rows - SEG
            after = jnp.where(row < SEG - 1, pltpu.roll(wide[base : base + SEG], SEG - 1, 0), 0.0)
            before = jnp.where(row > 0, pltpu.roll(wide[last : last + SEG], 1, 0), 0.0)
            for q in range(steps):
                r = base + q * SEG
                nxt = after if q == steps - 1 else wide[r + SEG : r + 2 * SEG]
                prv = before if q == 0 else wide[r - SEG : r]
                side_scr[block, pl.ds(pl.multiple_of(at + r, SEG), SEG), :] = jnp.where(right, nxt, prv).astype(BF)
        return 0

    lax.fori_loop(0, LIFT_BLOCKS * chunks, lift, 0)

    gain0, gain1 = out_ref[0:1, :], out_ref[1:2, :]

    def mix(t, _):
        block, part = t // chunks + 1, lax.rem(t, chunks)
        above = block - 1
        below = jnp.where(block == LIFT_BLOCKS - 1, 0, block + 1)
        at = pl.ds(pl.multiple_of(part * chunk, chunk), chunk)
        x = jnp.concatenate(
            [
                lift_scr[block, at, :],
                side_scr[block, at, :],
                lift_scr[below, at, 0:128],
                lift_scr[above, at, 128:256],
                side_scr[below, at, 0:128],
                side_scr[above, at, 128:256],
            ],
            axis=1,
        )
        deep = jnp.maximum(jnp.dot(x, wmix_ref[...], preferred_element_type=F32), 0.0)
        deep_scr[block - 1, at, :] = (deep[:, :128] * gain0 + deep[:, 128:] * gain1).astype(BF)
        return 0

    lax.fori_loop(0, MIX_BLOCKS * chunks, mix, 0)

    k, n = iota(wout_scr.shape, 0), iota(wout_scr.shape, 1)
    place = (k & 127) >> 5
    row = 2 * ((k >> 7) + 1) - HALO + (place >> 1)
    row = jnp.where(row < 0, row + RING, row)
    wout_scr[...] = jnp.where(n == (place & 1) * 32 + row, 1.0, 0.0).astype(BF)

    def collect(pair, _):
        at = pl.ds(pl.multiple_of(pair * 2 * block_rows, 2 * block_rows), 2 * block_rows)
        x = jnp.concatenate([deep_scr[j, at, :] for j in range(MIX_BLOCKS)], axis=1)
        both = jnp.dot(x, wout_scr[...], preferred_element_type=F32)
        both = both[:block_rows] + pltpu.roll(both[block_rows:], 64, 1)
        for q in range(steps):
            part = both[q * SEG : (q + 1) * SEG]
            t_scr[pl.ds(2 * q, SEG, stride=2 * steps), :] = part
            t_scr[pl.ds(2 * q + 1, SEG, stride=2 * steps), :] = part
        flat = t_scr[0:width, :].T
        even = iota((RING, width), 1) & 1 == 0
        for half in range(2):
            s = 64 * half
            f_scr[2 * pair + half] = f_scr[2 * pair + half] + jnp.where(
                even, flat[s : s + RING], flat[s + 32 : s + 32 + RING]
            )
        return 0

    lax.fori_loop(0, groups // 2, collect, 0)

    full = (RING, width)
    ring = iota(full, 0)
    grid_row = tile * rows + jnp.where(ring < rows + HALO, ring, ring - RING)
    inside = (grid_row >= 0) & (grid_row < grid_rows)
    joined = (grid_row >= 0) & (grid_row < grid_rows - 1)
    not_last = iota(full, 1) < width - 1

    def ring_of(ref, group, z):
        pair = group // 2
        up, down = up_ref[pair], down_ref[pair]
        first = iota(up.shape, 0) < HALO
        if group % 2 == 0:
            third = jnp.where(first, up, down)
        else:
            third = pltpu.roll(jnp.where(first, down, up), HALO, 0)
        return jnp.concatenate([ref[z], third], axis=0)

    def row_next(v):
        return pltpu.roll(v, RING - 1, 0)

    def row_prev(v):
        return pltpu.roll(v, 1, 0)

    def col_next(v):
        return pltpu.roll(v, width - 1, 1)

    def col_prev(v):
        return pltpu.roll(v, 1, 1)

    start = [ring_of(prev_ref, groups + z, z) for z in range(layers)]
    base = [start[z] + ring_of(src_ref, groups + layers + z, z) for z in range(layers)]
    around = [[f(start[z]) for f in (row_next, row_prev, col_next, col_prev)] for z in range(layers)]

    def flow(p, q):
        return 2.0 * p * q / (p + q)

    def sweep(member, _):
        perm = [jnp.where(inside, jnp.exp(f_scr[z * members + member]), 1.0) for z in range(layers)]
        between = jnp.where(inside, flow(perm[0], perm[1]), 0.0)
        faces, scale = [], []
        for z in range(layers):
            below = jnp.where(joined, flow(perm[z], row_next(perm[z])), 0.0)
            right = jnp.where(not_last, flow(perm[z], col_next(perm[z])), 0.0)
            right = jnp.where(inside, right, 0.0)
            face = (below, row_prev(below), right, col_prev(right))
            faces.append(face)
            scale.append(1.0 / (1.0 + between + face[0] + face[1] + face[2] + face[3]))
        press, near = start, around
        for turn in range(SWEEPS):
            if turn > 0:
                near = [[f(press[z]) for f in (row_next, row_prev, col_next, col_prev)] for z in range(layers)]
            press = [
                (base[z] + between * press[1 - z] + sum(c * v for c, v in zip(faces[z], near[z]))) * scale[z]
                for z in range(layers)
            ]
        cols = press_ref.shape[4]
        for z in range(layers):
            for d in range(press_ref.shape[0]):
                press_ref[d, member, z] = press[z][:rows, d * cols : (d + 1) * cols]
            weight = perm[z][:rows]
            for kind, value in enumerate((weight * press[z][:rows], weight)):
                hi = value.astype(BF)
                lo = (value - hi.astype(F32)).astype(BF)
                for part, piece in enumerate((hi, lo)):
                    at = (((kind * 2 + part) * members + member) * layers + z) * rows
                    v_scr[pl.ds(pl.multiple_of(at, rows), rows), :] = piece
        return 0

    lax.fori_loop(0, members, sweep, 0)

    slots, wells = sel_ref.shape
    cells = layers * rows
    sums = jnp.zeros((4 * members, wells), F32)
    for slot in range(slots):
        here = iota((width, wells), 0) == col_ref[slot : slot + 1, :]
        got = jnp.dot(v_scr[...], jnp.where(here, 1.0, 0.0).astype(BF), preferred_element_type=F32)
        mine = iota((cells, wells), 0) == sel_ref[slot : slot + 1, :]
        picked = jnp.where(mine[None], got.reshape(4 * members, cells, wells), 0.0)
        sums = sums + jnp.sum(picked, axis=1)
    sums_ref[0:members] = sums[0:members] + sums[members : 2 * members]
    sums_ref[members : 2 * members] = sums[2 * members : 3 * members] + sums[3 * members :]


def decode(parts, tile_at, grid_rows, field, down, up, prev, src, win, wmix, gains, sel, col):
    layers, members, rows, width = field.shape
    groups = layers * members
    total = groups * width // 2
    wells = sel.shape[1]
    return pl.pallas_call(
        functools.partial(decode_kernel, grid_rows),
        in_specs=[SMEM] + [VMEM] * 10,
        out_specs=[VMEM, VMEM],
        out_shape=[
            jax.ShapeDtypeStruct((parts, members, layers, rows, width // parts), F32),
            jax.ShapeDtypeStruct((2 * members, wells), F32),
        ],
        scratch_shapes=[
            pltpu.VMEM((groups, RING, width), F32),
            pltpu.VMEM((width + 8, 128), F32),
            pltpu.VMEM((total, 256), BF),
            pltpu.VMEM((LIFT_BLOCKS, total, 256), BF),
            pltpu.VMEM((LIFT_BLOCKS, total, 256), BF),
            pltpu.VMEM((MIX_BLOCKS, total, 128), BF),
            pltpu.VMEM((MIX_BLOCKS * 128, 128), BF),
            pltpu.VMEM((4 * groups * rows, width), BF),
        ],
        compiler_params=pltpu.CompilerParams(vmem_limit_bytes=60 * 2**20),
    )(tile_at, field, down, up, prev, src, win, wmix, gains, sel, col)


def update_kernel(mem_ref, wd_refs, lat_refs, obs_ref, err_ref, data_ref, new_ref, wd_scr, lat_scr, step_scr):
    count = len(wd_refs)
    own, wells = wd_refs[0].shape
    members = count * own
    mem = mem_ref[0]
    for k in range(count):
        source = lax.rem(mem + count - k, count)
        wd_scr[source] = wd_refs[k][...]
        lat_scr[source] = lat_refs[k][...]
    data = jnp.concatenate([wd_scr[k] for k in range(count)], axis=0)
    every = jnp.concatenate([lat_scr[k] for k in range(count)], axis=0)
    data_ref[...] = data
    scale = 2.0 * err_ref[...]
    root = math.sqrt(members - 1)
    scaled = (data - jnp.mean(data, axis=0, keepdims=True)) / (root * scale)
    innov = (obs_ref[...] - data) / scale
    dims = (((1,), (1,)), ((), ()))
    exact = lax.Precision.HIGHEST
    eye = (iota((members, members), 0) == iota((members, members), 1)).astype(F32)
    gram = eye + lax.dot_general(scaled, scaled, dims, precision=exact, preferred_element_type=F32)
    cross = lax.dot_general(innov, scaled, dims, precision=exact, preferred_element_type=F32)
    right = (every - jnp.mean(every, axis=0, keepdims=True)) / root
    place = iota((members, 1), 0)
    for k in range(members):
        inverse = 1.0 / gram[k : k + 1, k : k + 1]
        factor = jnp.where(place == k, 0.0, gram[:, k : k + 1])
        gram_row = gram[k : k + 1, :] * inverse
        right_row = right[k : k + 1, :] * inverse
        gram = jnp.where(place == k, gram_row, gram - factor * gram_row)
        right = jnp.where(place == k, right_row, right - factor * right_row)
    new = every + jnp.dot(cross, right, precision=exact, preferred_element_type=F32)
    for k in range(count):
        step_scr[k] = new[k * own : (k + 1) * own]
    new_ref[...] = step_scr[mem]


def update(mem_at, wds, lats, obs, err):
    count = len(wds)
    own, wells = wds[0].shape
    width = lats[0].shape[1]

    def kernel(mem_ref, *refs):
        update_kernel(mem_ref, refs[:count], refs[count : 2 * count], *refs[2 * count :])

    return pl.pallas_call(
        kernel,
        in_specs=[SMEM] + [VMEM] * (2 * count + 2),
        out_specs=[VMEM, VMEM],
        out_shape=[
            jax.ShapeDtypeStruct((count * own, wells), F32),
            jax.ShapeDtypeStruct((own, width), F32),
        ],
        scratch_shapes=[
            pltpu.VMEM((count, own, wells), F32),
            pltpu.VMEM((count, own, width), F32),
            pltpu.VMEM((count, own, width), F32),
        ],
        compiler_params=pltpu.CompilerParams(vmem_limit_bytes=24 * 2**20),
    )(mem_at, *wds, *lats, obs, err)


def gathered(own, axis):
    count = lax.axis_size(axis)
    return [own] + [
        lax.ppermute(own, axis, [(i, (i + k) % count) for i in range(count)]) for k in range(1, count)
    ]


def summed(own, axis):
    count = lax.axis_size(axis)
    if count & (count - 1):
        return lax.psum(own, axis)
    k = 1
    while k < count:
        own = own + lax.ppermute(own, axis, [(i, i ^ k) for i in range(count)])
        k *= 2
    return own


def body(
    latents,
    basis,
    conv_in,
    conv_mid,
    conv_out,
    pressure_prev,
    source,
    perf_cells,
    perf_count,
    obs_perturbed,
    obs_error,
):
    members = latents.shape[0]
    layers, rows, width = basis.shape[1:]
    tiles = lax.axis_size("tile")
    parts = lax.axis_size("mem")
    grid_rows = rows * tiles
    tile_at = lax.axis_index("tile")
    tile_vec = tile_at.astype(jnp.int32).reshape(1)
    mem_vec = lax.axis_index("mem").astype(jnp.int32).reshape(1)

    field, low, high = field_of(latents, basis, pressure_prev, source)
    down = lax.ppermute(high, "tile", [(i, i + 1) for i in range(tiles - 1)])
    up = lax.ppermute(low, "tile", [(i + 1, i) for i in range(tiles - 1)])
    lats = gathered(latents, "mem")

    win, wmix = prep(tile_vec, grid_rows, rows, conv_in, conv_mid)
    gains = jnp.tile(conv_out.astype(F32).reshape(2, 32), (1, 4))
    ids = perf_cells.T
    slots = ids.shape[0]
    layer_at = ids // (grid_rows * width)
    rest = ids % (grid_rows * width)
    row_at = rest // width - tile_at * rows
    used = (jnp.arange(slots)[:, None] < perf_count[None, :]) & (row_at >= 0) & (row_at < rows)
    sel = jnp.where(used, layer_at * rows + row_at, -1)
    col = rest % width

    press, sums = decode(
        parts, tile_vec, grid_rows, field, down, up, pressure_prev, source, win, wmix, gains, sel, col
    )
    swapped = lax.all_to_all(press, "mem", 0, 0)
    sums = summed(sums, "tile")
    wds = gathered(sums[:members] / sums[members:], "mem")
    data, new = update(mem_vec, wds, lats, obs_perturbed, obs_error.reshape(1, -1))
    return (swapped.reshape((parts * members,) + swapped.shape[2:]), data, new)


def solution(mesh):
    return jax.shard_map(
        body,
        mesh=mesh,
        in_specs=(
            P("mem", None),
            P(None, None, "tile", None),
            P(),
            P(),
            P(),
            P(None, "tile", None),
            P(None, "tile", None),
            P(),
            P(),
            P(),
            P(),
        ),
        out_specs=(P(None, None, "tile", "mem"), P(), P("mem", None)),
        check_vma=False,
    )
```

time: 638 us -> 101 us (0.16); the launches traced: 631 us -> 100 us
  matrix products: 221 us -> 0 us
  waiting for transfers between devices: 166 us -> 9.92 us
  local copies, waits for them, and re-layouts: 107 us -> 10.9 us
  other arithmetic: 58.8 us -> 1.4 us
  Pallas kernels: 0 us -> 56.5 us
  starting transfers between devices: 52.5 us -> 21 us
  between operations: 14.9 us -> 0.83 us
  blocking collectives: 9.76 us -> 0 us
    dot_general x58 -> x0, matrix products: 221 us -> none  [the longest x48 132 us: mix(): jnp.einsum('oc,zcxy->zoxy', conv_mid[tap], part, preferred_element_type=j...]
    psum x1 -> x0, waiting for transfers between devices: 129 us -> none  [body(): numer, weight_sum = lax.psum((numer, weight_sum), ('mem', 'tile'))]
    pallas_call x0 -> x4, Pallas kernels: none -> 56.5 us  [the longest x1 49 us: decode(): pl.pallas_call(functools.partial(decode_kernel, grid_rows), in_specs=[SME...]
    ppermute x16 -> x11, waiting for transfers between devices: 37 us -> 9.92 us  [the longest x3 5.64 us: summed(): own = own + lax.ppermute(own, axis, [(i, i ^ k) for i in range(count)])]
    ppermute x16 -> x11, starting transfers between devices: 40.7 us -> 17.5 us  [the longest x3 7.51 us: summed(): own = own + lax.ppermute(own, axis, [(i, i ^ k) for i in range(count)])]
    gather x2 -> x0, local copies, waits for them, and re-layouts: 21.7 us -> none  [the longest x1 10.8 us: well_terms(): press_at = jnp.take(press.reshape(members, -1), local_ids, axis=1)]
    convert_element_type x12 -> x0, other arithmetic: 18.8 us -> none  [the longest x6 18.8 us: lift(): return jax.nn.relu(total).astype(jnp.bfloat16)]
    concatenate x8 -> x0, other arithmetic: 17 us -> none  [extended(): jnp.concatenate([lax.ppermute(tail, axis, [(i, (i + 1) % count) for i in...]
  transfers between devices with their start and end apart: 18 -> 12, of which waited for: 5 -> 6; matrix products, arithmetic and copies ran while one was open for 44% -> 2% of each run, Pallas kernels for 0% -> 4%
where the time goes in v1:
time: 101 us; the launch traced here: 100 us
  Pallas kernels  56.5 us (56%)
  starting transfers between devices  21 us (21%)
  local copies, waits for them, and re-layouts  10.9 us (11%)
  waiting for transfers between devices  9.92 us (10%)
  other arithmetic  1.4 us (1%)
    pallas_call x1, Pallas kernels, decode(): pl.pallas_call(functools.partial(decode_kernel, grid_rows), in_specs=[SME...  49 us
    unnamed x35, local copies, waits for them, and re-layouts  9.86 us
    ppermute x3, starting transfers between devices, summed(): own = own + lax.ppermute(own, axis, [(i, i ^ k) for i in range(count)])  7.51 us
    ppermute x3, waiting for transfers between devices, summed(): own = own + lax.ppermute(own, axis, [(i, i ^ k) for i in range(count)])  5.64 us
    ppermute x1, starting transfers between devices, body(): down = lax.ppermute(high, 'tile', [(i, i + 1) for i in range(tiles - 1)])  4.87 us
    ppermute x6, starting transfers between devices, gathered(): lax.ppermute(own, axis, [(i, (i + k) % count) for i in range(count)])  3.83 us
    pallas_call x1, Pallas kernels, field_of(): pl.pallas_call(field_kernel, grid=(total // comps,), in_specs=[whole(late...  3.61 us
    all_to_all x1, starting transfers between devices, body(): swapped = lax.all_to_all(press, 'mem', 0, 0)  3.46 us
  transfers between devices with their start and end apart: 12, of which 6 were waited for; matrix products, arithmetic and copies ran while one was open for 2% of the time, Pallas kernels for 4%

profile of v1, /device:TPU:0, one launch (start us, length us, event | category | flops | bytes accessed | tf_op | source)
XLA Modules:
  0.0 100.5 jit_solution(11032231196996313255)
XLA Ops:
  0.6 3.4 %copy-done = bf16[256,2,16,512]{3,2,1,0:T(8,128)(2,1)S(1)} copy-done((bf16[256,2,16,512]{3,2,1,0:T(8,128)(2,1)S(1)}, bf16[256,2,16,512]{3,2,1,0:T(8,128)(2,1)}, u32[]{:S(2)}) %copy-start) | copy-done | bytes 8388632
  4.0 0.8 copy-done.4
  4.9 0.8 copy-done.5
  5.7 0.7 copy-done.7
  6.4 3.6 %shard_map.130 = (f32[2,6,16,512]{3,2,1,0:T(8,128)S(1)}, f32[8,8,512]{2,1,0:T(8,128)S(1)}, f32[8,8,512]{2,1,0:T(8,128)S(1)}) custom-call(f32[6,256]{1,0:T(8,128)S(1)} %copy-done.7, bf16[256,2,16,512]{3,2,1,0:T(8,128)(2,1)S(1)} %copy-done, f32[2,16,512]{2,1,0:T(8,128)S(1)} %copy-done.4, f32[2,16,512]{2,1,0:T(8,128)S(1)} %copy-done.5), custom_call_target="tpu_custom_call" | custom-call | tf_op jit(solution)/shard_map/pallas_call | solution.py:63
  10.1 0.7 copy-done.3
  10.8 4.9 %collective-permute-start = (f32[8,8,512]{2,1,0:T(8,128)S(1)}, f32[8,8,512]{2,1,0:T(8,128)S(1)}, u32[]{:S(2)}, u32[]{:S(2)}) collective-permute-start(f32[8,8,512]{2,1,0:T(8,128)S(1)} %get-tuple-element.13), channel_id=1, source_target_pairs={{0,1},{1,2},{2,3},{3,4},{4,5},{5,6},{6,7},{8,9},{9,10},{10,11},{11... | collective-permute-start | bytes 393224 | tf_op jit(solution)/shard_map/ppermute | solution.py:503
  15.7 1.3 %collective-permute-start.1 = (f32[8,8,512]{2,1,0:T(8,128)S(1)}, f32[8,8,512]{2,1,0:T(8,128)S(1)}, u32[]{:S(2)}, u32[]{:S(2)}) collective-permute-start(f32[8,8,512]{2,1,0:T(8,128)S(1)} %get-tuple-element.14), channel_id=1, source_target_pairs={{1,0},{2,1},{3,2},{4,3},{5,4},{6,5},{7,6},{9,8},{10,9},{11,10},{12... | collective-permute-start | bytes 393224 | tf_op jit(solution)/shard_map/ppermute | solution.py:504
  17.0 0.6 add_select_fusion
  17.7 0.1 copy.14
  18.1 0.6 tile.26.out_ref
  18.7 0.9 shard_map.131
  19.6 1.1 %copy-done.1 = bf16[11,256,256]{2,1,0:T(8,128)(2,1)} copy-done((bf16[11,256,256]{2,1,0:T(8,128)(2,1)}, bf16[11,256,256]{2,1,0:T(8,128)(2,1)S(1)}, u32[]{:S(2)}) %copy-start.1) | copy-done | bytes 1441816
  20.8 0.8 copy-done.2
  21.6 1.0 collective-permute-done.1.up_ref
  22.6 0.7 copy-done.11
  23.2 49.0 %shard_map.132 = (f32[4,6,2,16,128]{4,3,2,1,0:T(8,128)}, f32[12,384]{1,0:T(8,128)}) custom-call(s32[1]{0:T(128)} %bitcast.tile_ref, f32[2,6,16,512]{3,2,1,0:T(8,128)} %copy-done.3, f32[8,8,512]{2,1,0:T(8,128)} %copy-done.10, f32[8,8,512]{2,1,0:T(8,128)} %copy-done.11, f32[2,16,512]{2,1,0:T(8,128)} %prev_ref.3, f32[2,16,512]{2,1,0:T(8,128)} %src_ref.3, ...), custom_call_target="tpu_custom_call" | custom-call | tf_op jit(solution)/shard_map/pallas_call | solution.py:379
  72.2 3.5 %all-to-all-start = ((f32[4,6,2,16,128]{4,3,2,1,0:T(8,128)}), f32[4,6,2,16,128]{4,3,2,1,0:T(8,128)S(1)}, u32[]{:S(2)}, u32[]{:S(2)}) async-start(f32[4,6,2,16,128]{4,3,2,1,0:T(8,128)} %get-tuple-element.17), calls=%async_computation | async-start | bytes 786432 | tf_op jit(solution)/shard_map/all_to_all | solution.py:521
  75.7 2.5 %collective-permute-start.2 = (f32[12,384]{1,0:T(8,128)}, f32[12,384]{1,0:T(8,128)S(1)}, u32[]{:S(2)}, u32[]{:S(2)}) collective-permute-start(f32[12,384]{1,0:T(8,128)} %get-tuple-element.18), channel_id=1, source_target_pairs={{0,1},{1,0},{2,3},{3,2},{4,5},{5,4},{6,7},{7,6},{8,9},{9,8},{10,11... | collective-permute-start | bytes 55304 | tf_op jit(solution)/shard_map/ppermute | solution.py:475
  78.2 2.0 %collective-permute-done.2 = f32[12,384]{1,0:T(8,128)S(1)} collective-permute-done((f32[12,384]{1,0:T(8,128)}, f32[12,384]{1,0:T(8,128)S(1)}, u32[]{:S(2)}, u32[]{:S(2)}) %collective-permute-start.2) | collective-permute-done | bytes 18464 | tf_op jit(solution)/shard_map/ppermute | solution.py:475
  80.2 0.7 add.29
  80.9 2.0 %collective-permute-start.3 = (f32[12,384]{1,0:T(8,128)S(1)}, f32[12,384]{1,0:T(8,128)S(1)}, u32[]{:S(2)}, u32[]{:S(2)}) collective-permute-start(f32[12,384]{1,0:T(8,128)S(1)} %add.29), channel_id=1, source_target_pairs={{0,2},{1,3},{2,0},{3,1},{4,6},{5,7},{6,4},{7,5},{8,10},{9,11},{10,... | collective-permute-start | bytes 55304 | tf_op jit(solution)/shard_map/ppermute | solution.py:475
  82.9 1.8 %collective-permute-done.3 = f32[12,384]{1,0:T(8,128)S(1)} collective-permute-done((f32[12,384]{1,0:T(8,128)S(1)}, f32[12,384]{1,0:T(8,128)S(1)}, u32[]{:S(2)}, u32[]{:S(2)}) %collective-permute-start.3) | collective-permute-done | bytes 18464 | tf_op jit(solution)/shard_map/ppermute | solution.py:475
  84.8 3.0 %collective-permute-start.4 = (f32[12,384]{1,0:T(8,128)S(1)}, f32[12,384]{1,0:T(8,128)S(1)}, u32[]{:S(2)}, u32[]{:S(2)}) collective-permute-start(f32[12,384]{1,0:T(8,128)S(1)} %add.30), channel_id=1, source_target_pairs={{0,4},{1,5},{2,6},{3,7},{4,0},{5,1},{6,2},{7,3},{8,12},{9,13},{10,... | collective-permute-start | bytes 55304 | tf_op jit(solution)/shard_map/ppermute | solution.py:475
  87.8 1.8 %collective-permute-done.4 = f32[12,384]{1,0:T(8,128)S(1)} collective-permute-done((f32[12,384]{1,0:T(8,128)S(1)}, f32[12,384]{1,0:T(8,128)S(1)}, u32[]{:S(2)}, u32[]{:S(2)}) %collective-permute-start.4) | collective-permute-done | bytes 18464 | tf_op jit(solution)/shard_map/ppermute | solution.py:475
  89.7 2.0 %collective-permute-start.6 = (f32[6,384]{1,0:T(8,128)S(1)}, f32[6,384]{1,0:T(8,128)S(1)}, u32[]{:S(2)}, u32[]{:S(2)}) collective-permute-start(f32[6,384]{1,0:T(8,128)S(1)} %slice_divide_fusion.refs_0_), channel_id=1, source_target_pairs={{0,16},{8,24},{16,0},{24,8},{1,17},{9,25},{17,1},{25,9},{2,18},{10... | collective-permute-start | bytes 27656 | tf_op jit(solution)/shard_map/ppermute | solution.py:465
  91.7 1.4 %collective-permute-start.7 = (f32[6,384]{1,0:T(8,128)S(1)}, f32[6,384]{1,0:T(8,128)S(1)}, u32[]{:S(2)}, u32[]{:S(2)}) collective-permute-start(f32[6,384]{1,0:T(8,128)S(1)} %slice_divide_fusion.refs_0_), channel_id=1, source_target_pairs={{0,24},{8,0},{16,8},{24,16},{1,25},{9,1},{17,9},{25,17},{2,26},{10... | collective-permute-start | bytes 27656 | tf_op jit(solution)/shard_map/ppermute | solution.py:465
  93.0 0.4 collective-permute-start.9
  93.5 2.7 %collective-permute-done.8.refs_5_ = f32[6,256]{1,0:T(8,128)S(1)} collective-permute-done((f32[6,256]{1,0:T(8,128)S(1)}, f32[6,256]{1,0:T(8,128)S(1)}, u32[]{:S(2)}, u32[]{:S(2)}) %collective-permute-start.8) | collective-permute-done | bytes 6176 | tf_op jit(solution)/shard_map/ppermute | solution.py:465
  96.1 0.6 collective-permute-done.9.refs_6_
  96.8 3.0 %shard_map.133 = (f32[24,384]{1,0:T(8,128)}, f32[6,256]{1,0:T(8,128)}) custom-call(s32[1]{0:T(128)} %bitcast.5.mem_ref, f32[6,384]{1,0:T(8,128)S(1)} %slice_divide_fusion.refs_0_, f32[6,384]{1,0:T(8,128)S(1)} %collective-permute-done.5.refs_1_, f32[6,384]{1,0:T(8,128)S(1)} %collective-permute-done.6.refs_2_, f32[6,384]{1,0:T(8,128)S(1)} %collective-permute-done.7.refs_3_, ...), custom_call_target="tpu_custom_call" | custom-call | tf_op jit(solution)/shard_map/pallas_call | solution.py:445
  99.7 0.7 copy.16
  (44 shorter events, 0.4 us)
Async XLA Ops:
  0.6 3.4 %copy-start = (bf16[256,2,16,512]{3,2,1,0:T(8,128)(2,1)S(1)}, bf16[256,2,16,512]{3,2,1,0:T(8,128)(2,1)}, u32[]{:S(2)}) copy-start(bf16[256,2,16,512]{3,2,1,0:T(8,128)(2,1)} %basis_ref.1) | copy-start | bytes 25165828
  4.0 0.8 copy-start.4
  4.9 0.8 copy-start.5
  5.7 0.7 copy-start.7
  6.4 10.6 %copy-start.12 = (s32[384,8]{0,1:T(8,128)S(1)}, s32[384,8]{0,1:T(8,128)}, u32[]{:S(2)}) copy-start(s32[384,8]{0,1:T(8,128)} %param.18) | copy-start | bytes 36868
  6.4 10.6 %copy-start.14 = (s32[384]{0:T(512)S(1)}, s32[384]{0:T(512)}, u32[]{:S(2)}) copy-start(s32[384]{0:T(512)} %param.19) | copy-start | bytes 4612
  6.4 11.3 %copy-start.9 = (bf16[9,64,64]{2,1,0:T(8,128)(2,1)S(1)}, bf16[9,64,64]{2,1,0:T(8,128)(2,1)}, u32[]{:S(2)}) copy-start(bf16[9,64,64]{2,1,0:T(8,128)(2,1)} %param.14) | copy-start | bytes 221188
  6.4 11.4 %copy-start.13 = (bf16[9,64]{1,0:T(8,128)(2,1)S(1)}, bf16[9,64]{1,0:T(8,128)(2,1)}, u32[]{:S(2)}) copy-start(bf16[9,64]{1,0:T(8,128)(2,1)} %param.13) | copy-start | bytes 3460
  6.4 11.6 %copy-start.16 = (bf16[64]{0:T(256)(128)(2,1)S(1)}, bf16[64]{0:T(256)(128)(2,1)}, u32[]{:S(2)}) copy-start(bf16[64]{0:T(256)(128)(2,1)} %param.15) | copy-start | bytes 388
  6.4 81.4 %copy-start.8 = (f32[6,256]{1,0:T(8,128)S(1)}, f32[6,256]{1,0:T(8,128)}, u32[]{:S(2)}) copy-start(f32[6,256]{1,0:T(8,128)} %refs_4_.1) | copy-start | bytes 18436
  6.4 87.0 %copy-start.15 = (f32[384]{0:T(512)S(1)}, f32[384]{0:T(512)}, u32[]{:S(2)}) copy-start(f32[384]{0:T(512)} %param.21) | copy-start | bytes 4612
  6.4 90.3 %copy-start.6 = (f32[24,384]{1,0:T(8,128)S(1)}, f32[24,384]{1,0:T(8,128)}, u32[]{:S(2)}) copy-start(f32[24,384]{1,0:T(8,128)} %refs_8_.1) | copy-start | bytes 110596
  10.1 0.7 copy-start.3
  10.8 10.7 %collective-permute-start = (f32[8,8,512]{2,1,0:T(8,128)S(1)}, f32[8,8,512]{2,1,0:T(8,128)S(1)}, u32[]{:S(2)}, u32[]{:S(2)}) collective-permute-start(f32[8,8,512]{2,1,0:T(8,128)S(1)} %get-tuple-element.13), channel_id=1, source_target_pairs={{0,1},{1,2},{2,3},{3,4},{4,5},{5,6},{6,7},{8,9},{9,10},{10,11},{11... | collective-permute-start | bytes 393224 | tf_op jit(solution)/shard_map/ppermute | solution.py:503
  15.7 6.9 %collective-permute-start.1 = (f32[8,8,512]{2,1,0:T(8,128)S(1)}, f32[8,8,512]{2,1,0:T(8,128)S(1)}, u32[]{:S(2)}, u32[]{:S(2)}) collective-permute-start(f32[8,8,512]{2,1,0:T(8,128)S(1)} %get-tuple-element.14), channel_id=1, source_target_pairs={{1,0},{2,1},{3,2},{4,3},{5,4},{6,5},{7,6},{9,8},{10,9},{11,10},{12... | collective-permute-start | bytes 393224 | tf_op jit(solution)/shard_map/ppermute | solution.py:504
  19.6 1.1 %copy-start.1 = (bf16[11,256,256]{2,1,0:T(8,128)(2,1)}, bf16[11,256,256]{2,1,0:T(8,128)(2,1)S(1)}, u32[]{:S(2)}) copy-start(bf16[11,256,256]{2,1,0:T(8,128)(2,1)S(1)} %get-tuple-element.15.win_ref) | copy-start | bytes 4325380
  20.8 0.8 copy-start.2
  21.6 1.0 copy-start.10
  22.5 0.7 copy-start.11
  72.2 27.5 %all-to-all-start = ((f32[4,6,2,16,128]{4,3,2,1,0:T(8,128)}), f32[4,6,2,16,128]{4,3,2,1,0:T(8,128)S(1)}, u32[]{:S(2)}, u32[]{:S(2)}) async-start(f32[4,6,2,16,128]{4,3,2,1,0:T(8,128)} %get-tuple-element.17), calls=%async_computation | async-start | bytes 786432 | tf_op jit(solution)/shard_map/all_to_all | solution.py:521
  75.7 4.5 %collective-permute-start.2 = (f32[12,384]{1,0:T(8,128)}, f32[12,384]{1,0:T(8,128)S(1)}, u32[]{:S(2)}, u32[]{:S(2)}) collective-permute-start(f32[12,384]{1,0:T(8,128)} %get-tuple-element.18), channel_id=1, source_target_pairs={{0,1},{1,0},{2,3},{3,2},{4,5},{5,4},{6,7},{7,6},{8,9},{9,8},{10,11... | collective-permute-start | bytes 55304 | tf_op jit(solution)/shard_map/ppermute | solution.py:475
  80.9 3.8 %collective-permute-start.3 = (f32[12,384]{1,0:T(8,128)S(1)}, f32[12,384]{1,0:T(8,128)S(1)}, u32[]{:S(2)}, u32[]{:S(2)}) collective-permute-start(f32[12,384]{1,0:T(8,128)S(1)} %add.29), channel_id=1, source_target_pairs={{0,2},{1,3},{2,0},{3,1},{4,6},{5,7},{6,4},{7,5},{8,10},{9,11},{10,... | collective-permute-start | bytes 55304 | tf_op jit(solution)/shard_map/ppermute | solution.py:475
  84.8 4.8 %collective-permute-start.4 = (f32[12,384]{1,0:T(8,128)S(1)}, f32[12,384]{1,0:T(8,128)S(1)}, u32[]{:S(2)}, u32[]{:S(2)}) collective-permute-start(f32[12,384]{1,0:T(8,128)S(1)} %add.30), channel_id=1, source_target_pairs={{0,4},{1,5},{2,6},{3,7},{4,0},{5,1},{6,2},{7,3},{8,12},{9,13},{10,... | collective-permute-start | bytes 55304 | tf_op jit(solution)/shard_map/ppermute | solution.py:475
  87.8 5.3 %collective-permute-start.10 = (f32[6,256]{1,0:T(8,128)S(1)}, f32[6,256]{1,0:T(8,128)S(1)}, u32[]{:S(2)}, u32[]{:S(2)}) collective-permute-start(f32[6,256]{1,0:T(8,128)S(1)} %copy-done.8), channel_id=1, source_target_pairs={{0,24},{8,0},{16,8},{24,16},{1,25},{9,1},{17,9},{25,17},{2,26},{10... | collective-permute-start | bytes 18440 | tf_op jit(solution)/shard_map/ppermute | solution.py:465
  89.6 7.1 %collective-permute-start.5 = (f32[6,384]{1,0:T(8,128)S(1)}, f32[6,384]{1,0:T(8,128)S(1)}, u32[]{:S(2)}, u32[]{:S(2)}) collective-permute-start(f32[6,384]{1,0:T(8,128)S(1)} %slice_divide_fusion.refs_0_), channel_id=1, source_target_pairs={{0,8},{8,16},{16,24},{24,0},{1,9},{9,17},{17,25},{25,1},{2,10},{10... | collective-permute-start | bytes 27656 | tf_op jit(solution)/shard_map/ppermute | solution.py:465
  89.7 7.1 %collective-permute-start.6 = (f32[6,384]{1,0:T(8,128)S(1)}, f32[6,384]{1,0:T(8,128)S(1)}, u32[]{:S(2)}, u32[]{:S(2)}) collective-permute-start(f32[6,384]{1,0:T(8,128)S(1)} %slice_divide_fusion.refs_0_), channel_id=1, source_target_pairs={{0,16},{8,24},{16,0},{24,8},{1,17},{9,25},{17,1},{25,9},{2,18},{10... | collective-permute-start | bytes 27656 | tf_op jit(solution)/shard_map/ppermute | solution.py:465
  91.7 5.1 %collective-permute-start.7 = (f32[6,384]{1,0:T(8,128)S(1)}, f32[6,384]{1,0:T(8,128)S(1)}, u32[]{:S(2)}, u32[]{:S(2)}) collective-permute-start(f32[6,384]{1,0:T(8,128)S(1)} %slice_divide_fusion.refs_0_), channel_id=1, source_target_pairs={{0,24},{8,0},{16,8},{24,16},{1,25},{9,1},{17,9},{25,17},{2,26},{10... | collective-permute-start | bytes 27656 | tf_op jit(solution)/shard_map/ppermute | solution.py:465
  93.0 3.1 %collective-permute-start.8 = (f32[6,256]{1,0:T(8,128)S(1)}, f32[6,256]{1,0:T(8,128)S(1)}, u32[]{:S(2)}, u32[]{:S(2)}) collective-permute-start(f32[6,256]{1,0:T(8,128)S(1)} %copy-done.8), channel_id=1, source_target_pairs={{0,8},{8,16},{16,24},{24,0},{1,9},{9,17},{17,25},{25,1},{2,10},{10... | collective-permute-start | bytes 18440 | tf_op jit(solution)/shard_map/ppermute | solution.py:465
  93.0 3.7 %collective-permute-start.9 = (f32[6,256]{1,0:T(8,128)S(1)}, f32[6,256]{1,0:T(8,128)S(1)}, u32[]{:S(2)}, u32[]{:S(2)}) collective-permute-start(f32[6,256]{1,0:T(8,128)S(1)} %copy-done.8), channel_id=1, source_target_pairs={{0,16},{8,24},{16,0},{24,8},{1,17},{9,25},{17,1},{25,9},{2,18},{10... | collective-permute-start | bytes 18440 | tf_op jit(solution)/shard_map/ppermute | solution.py:465

commit v2 on v1

v2 whole, which is shorter than its diff:
```python
import functools
import math

import jax
import jax.numpy as jnp
from jax import lax
from jax.experimental import pallas as pl
from jax.experimental.pallas import tpu as pltpu
from jax.sharding import PartitionSpec as P

SWEEPS = 2
HALO = 4
RING = 24
LIFT_BLOCKS = 11
MIX_BLOCKS = 10
CHUNK_GROUPS = 12
SEG = 16
BF = jnp.bfloat16
F32 = jnp.float32
VMEM = pl.BlockSpec(memory_space=pltpu.VMEM)
SMEM = pl.BlockSpec(memory_space=pltpu.SMEM)


def iota(shape, dim):
    return lax.broadcasted_iota(jnp.int32, shape, dim)


def place_weights(tile, grid_rows, rows, in_ref, mid_ref, out_ref, win_ref, wmix_ref, gain_ref):
    one = lambda mask: jnp.where(mask, 1.0, 0.0).astype(BF)
    dot = functools.partial(jnp.dot, preferred_element_type=F32)
    taps = dot(one(iota((64, 9), 0) & 15 == iota((64, 9), 1)), in_ref[...]).astype(BF)
    taps = dot(taps, one(iota((64, 256), 0) == iota((64, 256), 1) & 63))
    kinds = jnp.where(iota((64, 256), 0) >> 4 == iota((64, 256), 1) >> 6, taps, 0.0).astype(BF)
    k, j = iota((256, 64), 0), iota((256, 64), 1)
    offset, ring = k >> 6, k & 31
    place, tap = j >> 4, j & 15
    xx, yy = place >> 1, place & 1
    a = ((tap * 11) >> 5) - 1
    b = tap - 3 * (a + 1) - 1
    fits = (tap < 9) & (offset == yy + b + 1)
    for block in range(LIFT_BLOCKS):
        row = jnp.where(xx == 0, 18, -3) if block == 0 else 2 * block - HALO + xx
        near = row + a
        near = jnp.where(near < 0, near + RING, near)
        grid_row = tile * rows + row
        pick = fits & (ring == near) & (grid_row >= 0) & (grid_row < grid_rows)
        win_ref[block] = dot(one(pick), kinds).astype(BF)
    o, n = iota((64, 1024), 0), iota((64, 1024), 1)
    put = one(n & 255 == (o >> 5) * 128 + (n >> 8) * 32 + (o & 31))
    placed = [
        lax.dot_general(mid_ref[t], put, (((0,), (0,)), ((), ())), preferred_element_type=F32) for t in range(9)
    ]
    for kind in range(4):
        side, over = kind & 1, kind >> 1
        for place_in in range(4):
            xi, yi = place_in >> 1, place_in & 1
            total = jnp.zeros((64, 256), F32)
            for place_out in range(4):
                xo, yo = place_out >> 1, place_out & 1
                dx = xi - xo + (0 if not over else (2 if xi == 0 else -2))
                dy = yi - yo + (0 if not side else (2 if yi == 0 else -2))
                if abs(dx) <= 1 and abs(dy) <= 1:
                    t = 3 * (dx + 1) + dy + 1
                    total = total + placed[t][:, 256 * place_out : 256 * place_out + 256]
            at = 256 * kind + 64 * place_in
            wmix_ref[at : at + 64, :] = total.astype(BF)
    gains = jnp.broadcast_to(out_ref[...].astype(F32), (8, 64)).astype(BF)
    c, n = iota((64, 128), 0), iota((64, 128), 1)
    gain_ref[0:8] = dot(gains, one(c == n & 31))
    gain_ref[8:16] = dot(gains, one(c == 32 + (n & 31)))


def place_kernel(grid_rows, rows, tile_ref, in_ref, mid_ref, out_ref, win_ref, wmix_ref, gain_ref):
    place_weights(tile_ref[0], grid_rows, rows, in_ref, mid_ref, out_ref, win_ref, wmix_ref, gain_ref)


def placed(tile_vec, grid_rows, rows, conv_in, conv_mid, conv_out):
    return pl.pallas_call(
        functools.partial(place_kernel, grid_rows, rows),
        in_specs=[SMEM] + [VMEM] * 3,
        out_specs=[VMEM] * 3,
        out_shape=[
            jax.ShapeDtypeStruct((LIFT_BLOCKS, 256, 256), BF),
            jax.ShapeDtypeStruct((1024, 256), BF),
            jax.ShapeDtypeStruct((16, 128), F32),
        ],
        compiler_params=pltpu.CompilerParams(vmem_limit_bytes=24 * 2**20),
        cost_estimate=pl.CostEstimate(flops=900_000_000, bytes_accessed=3_000_000, transcendentals=0),
    )(tile_vec, conv_in, conv_mid, conv_out)


def field_kernel(tile_ref, lat_ref, basis_ref, prev_ref, src_ref, field_ref, near_ref, far_ref, held, sems):
    chunks, comps, layers, rows, width = held.shape
    members, total = lat_ref.shape
    span = comps * rows
    copies = [
        pltpu.make_async_copy(basis_ref.at[pl.ds(c * comps, comps)], held.at[c], sems.at[c]) for c in range(chunks)
    ]
    for copy in copies:
        copy.start()
    lat = lat_ref[...].astype(BF)
    own = iota((rows, span), 0) == iota((rows, span), 1) & (rows - 1)
    behind = iota((total, span), 0) - split(iota((total, span), 1), rows)[0]
    for c in range(chunks):
        pick = jnp.where(behind == c * comps, 1.0, 0.0).astype(BF)
        spread = jnp.dot(lat, pick, preferred_element_type=F32)
        left = jnp.where(own[None], spread[:, None, :], 0.0).astype(BF).reshape(members * rows, span)
        copies[c].wait()
        for z in range(layers):
            part = jnp.dot(left, held[c, :, z].reshape(span, width), preferred_element_type=F32)
            part = part.reshape(members, rows, width)
            field_ref[z] = part if c == 0 else field_ref[z] + part
    tiles = [field_ref.at[z, m] for z in range(layers) for m in range(members)]
    tiles += [prev_ref.at[z] for z in range(layers)] + [src_ref.at[z] for z in range(layers)]
    first = iota((8, width), 0) < HALO
    even_tile = tile_ref[0] & 1 == 0
    for pair in range(len(tiles) // 2):
        even, odd = tiles[2 * pair], tiles[2 * pair + 1]
        low = jnp.where(first, even[0:8], pltpu.roll(odd[0:8], HALO, 0))
        high = jnp.where(first, pltpu.roll(odd[rows - 8 : rows], HALO, 0), even[rows - 8 : rows])
        near_ref[pair] = jnp.where(even_tile, high, low)
        far_ref[pair] = jnp.where(even_tile, low, high)


def field_of(tile_vec, latents, basis, prev, src):
    total, layers, rows, width = basis.shape
    members = latents.shape[0]
    comps = 32
    pairs = (layers * members + 2 * layers) // 2
    return pl.pallas_call(
        field_kernel,
        in_specs=[SMEM, VMEM, pl.BlockSpec(memory_space=pl.ANY), VMEM, VMEM],
        out_specs=[VMEM] * 3,
        out_shape=[
            jax.ShapeDtypeStruct((layers, members, rows, width), F32),
            jax.ShapeDtypeStruct((pairs, 8, width), F32),
            jax.ShapeDtypeStruct((pairs, 8, width), F32),
        ],
        scratch_shapes=[
            pltpu.VMEM((total // comps, comps, layers, rows, width), BF),
            pltpu.SemaphoreType.DMA((total // comps,)),
        ],
        compiler_params=pltpu.CompilerParams(vmem_limit_bytes=58 * 2**20),
    )(tile_vec, latents, basis, prev, src)


def target(me, k, count):
    return (me + k) % count if count & (count - 1) else me ^ k


def origin(me, k, count):
    return (me + count - k) % count if count & (count - 1) else me ^ k


def split(value, by):
    if by & (by - 1):
        return value // by, value % by
    return value >> (by.bit_length() - 1), value & (by - 1)


def decode_kernel(
    grid_rows,
    tile_ref,
    mem_ref,
    field_ref,
    near_ref,
    far_ref,
    prev_ref,
    src_ref,
    win_ref,
    wmix_ref,
    gain_ref,
    ids_ref,
    count_ref,
    *refs,

):
    parts = len(refs) - 10
    press_refs, sums_ref = refs[:parts], refs[parts]
    f_scr, t_scr, pt_scr, lift_scr, side_scr, deep_scr, wout_scr, v_scr, press_scr = refs[parts + 1 :]
    layers, members, rows, width = field_ref.shape
    groups = layers * members
    steps = width // (2 * SEG)
    block_rows = width // 2
    tile, mem = tile_ref[0], mem_ref[0]
    even_tile = tile & 1 == 0

    def outer(pair):
        near, far = near_ref[pair], far_ref[pair]
        up, down = jnp.where(even_tile, near, far), jnp.where(even_tile, far, near)
        first = iota(up.shape, 0) < HALO
        return jnp.where(first, up, down), pltpu.roll(jnp.where(first, down, up), HALO, 0)

    def load(pair, _):
        thirds = outer(pair)
        for half in range(2):
            group = 2 * pair + half
            own = field_ref[group // members, lax.rem(group, members)]
            f = jnp.concatenate([own, thirds[half]], axis=0)
            f_scr[group] = f
            hi = f.astype(BF).astype(F32)
            lo = f - hi
            zero = jnp.zeros((32 - RING, width), F32)
            edge = iota((RING, width), 1) == 0
            hi_left = jnp.where(edge, 0.0, pltpu.roll(hi, 1, 1))
            lo_left = jnp.where(edge, 0.0, pltpu.roll(lo, 1, 1))
            tall = jnp.concatenate([hi_left, zero, lo_left, zero, hi, zero, lo, zero], axis=0).T
            t_scr[0:width, :] = tall
            end = pltpu.roll(tall[width - 8 : width], 64, 1)
            end = jnp.where(iota(end.shape, 1) < 64, end, 0.0)
            t_scr[width : width + 8, :] = pltpu.roll(end, 1, 0)
            for q in range(steps + 1):
                part = t_scr[pl.ds(2 * q, SEG, stride=2 * steps), :].astype(BF)
                if q < steps:
                    pt_scr[pl.ds(pl.multiple_of(group * block_rows + q * SEG, SEG), SEG), 0:128] = part
                if q > 0:
                    pt_scr[pl.ds(pl.multiple_of(group * block_rows + (q - 1) * SEG, SEG), SEG), 128:256] = part
        return 0

    lax.fori_loop(0, groups // 2, load, 0)

    chunk = CHUNK_GROUPS * block_rows
    chunks = groups * block_rows // chunk

    def lift(t, _):
        block, part = t // chunks, lax.rem(t, chunks)
        at = pl.multiple_of(part * chunk, chunk)
        wide = jnp.dot(pt_scr[pl.ds(at, chunk), :], win_ref[block], preferred_element_type=F32)
        wide = jnp.maximum(wide, 0.0)
        tight = wide.astype(BF)
        lift_scr[block, pl.ds(at, chunk), :] = tight
        right = iota((SEG, 256), 1) & 64 == 0
        row = iota((SEG, 256), 0)
        for i in range(chunk // block_rows):
            base = i * block_rows
            last = base + block_rows - SEG
            after = jnp.where(row < SEG - 1, pltpu.roll(wide[base : base + SEG], SEG - 1, 0), 0.0)
            before = jnp.where(row > 0, pltpu.roll(wide[last : last + SEG], 1, 0), 0.0)
            for q in range(steps):
                r = base + q * SEG
                nxt = after if q == steps - 1 else wide[r + SEG : r + 2 * SEG]
                prv = before if q == 0 else wide[r - SEG : r]
                side_scr[block, pl.ds(pl.multiple_of(at + r, SEG), SEG), :] = jnp.where(right, nxt, prv).astype(BF)
        return 0


    gain0, gain1 = gain_ref[0:1, :], gain_ref[8:9, :]

    def mix(t, _):
        block, part = t // chunks + 1, lax.rem(t, chunks)
        above = block - 1
        below = jnp.where(block == LIFT_BLOCKS - 1, 0, block + 1)
        at = pl.ds(pl.multiple_of(part * chunk, chunk), chunk)
        x = jnp.concatenate(
            [
                lift_scr[block, at, :],
                side_scr[block, at, :],
                lift_scr[below, at, 0:128],
                lift_scr[above, at, 128:256],
                side_scr[below, at, 0:128],
                side_scr[above, at, 128:256],
            ],
            axis=1,
        )
        deep = jnp.maximum(jnp.dot(x, wmix_ref[...], preferred_element_type=F32), 0.0)
        deep_scr[block - 1, at, :] = (deep[:, :128] * gain0 + deep[:, 128:] * gain1).astype(BF)
        return 0

    def both_steps(t, _):
        mix(t, 0)
        lift(t + 3 * chunks, 0)
        return 0

    lax.fori_loop(0, 3 * chunks, lift, 0)
    lax.fori_loop(0, (LIFT_BLOCKS - 3) * chunks, both_steps, 0)
    lax.fori_loop((LIFT_BLOCKS - 3) * chunks, MIX_BLOCKS * chunks, mix, 0)

    k, n = iota(wout_scr.shape, 0), iota(wout_scr.shape, 1)
    place = (k & 127) >> 5
    row = 2 * ((k >> 7) + 1) - HALO + (place >> 1)
    row = jnp.where(row < 0, row + RING, row)
    wout_scr[...] = jnp.where(n == (place & 1) * 32 + row, 1.0, 0.0).astype(BF)

    def collect(pair, _):
        at = pl.ds(pl.multiple_of(pair * 2 * block_rows, 2 * block_rows), 2 * block_rows)
        x = jnp.concatenate([deep_scr[j, at, :] for j in range(MIX_BLOCKS)], axis=1)
        both = jnp.dot(x, wout_scr[...], preferred_element_type=F32)
        both = both[:block_rows] + pltpu.roll(both[block_rows:], 64, 1)
        for q in range(steps):
            part = both[q * SEG : (q + 1) * SEG]
            t_scr[pl.ds(2 * q, SEG, stride=2 * steps), :] = part
            t_scr[pl.ds(2 * q + 1, SEG, stride=2 * steps), :] = part
        flat = t_scr[0:width, :].T
        even = iota((RING, width), 1) & 1 == 0
        for half in range(2):
            s = 64 * half
            f_scr[2 * pair + half] = f_scr[2 * pair + half] + jnp.where(
                even, flat[s : s + RING], flat[s + 32 : s + 32 + RING]
            )
        return 0

    lax.fori_loop(0, groups // 2, collect, 0)

    full = (RING, width)
    ring = iota(full, 0)
    grid_row = tile * rows + jnp.where(ring < rows + HALO, ring, ring - RING)
    inside = (grid_row >= 0) & (grid_row < grid_rows)
    joined = (grid_row >= 0) & (grid_row < grid_rows - 1)
    not_last = iota(full, 1) < width - 1

    def ring_of(ref, group, z):
        return jnp.concatenate([ref[z], outer(group // 2)[group % 2]], axis=0)

    def row_next(v):
        return pltpu.roll(v, RING - 1, 0)

    def row_prev(v):
        return pltpu.roll(v, 1, 0)

    def col_next(v):
        return pltpu.roll(v, width - 1, 1)

    def col_prev(v):
        return pltpu.roll(v, 1, 1)

    start = [ring_of(prev_ref, groups + z, z) for z in range(layers)]
    base = [start[z] + ring_of(src_ref, groups + layers + z, z) for z in range(layers)]
    around = [[f(start[z]) for f in (row_next, row_prev, col_next, col_prev)] for z in range(layers)]

    def flow(p, q):
        return 2.0 * p * q / (p + q)

    def sweep(member, _):
        perm = [jnp.where(inside, jnp.exp(f_scr[z * members + member]), 1.0) for z in range(layers)]
        between = jnp.where(inside, flow(perm[0], perm[1]), 0.0)
        faces, scale = [], []
        for z in range(layers):
            below = jnp.where(joined, flow(perm[z], row_next(perm[z])), 0.0)
            right = jnp.where(not_last, flow(perm[z], col_next(perm[z])), 0.0)
            right = jnp.where(inside, right, 0.0)
            face = (below, row_prev(below), right, col_prev(right))
            faces.append(face)
            scale.append(1.0 / (1.0 + between + face[0] + face[1] + face[2] + face[3]))
        press, near = start, around
        for turn in range(SWEEPS):
            if turn > 0:
                near = [[f(press[z]) for f in (row_next, row_prev, col_next, col_prev)] for z in range(layers)]
            press = [
                (base[z] + between * press[1 - z] + sum(c * v for c, v in zip(faces[z], near[z]))) * scale[z]
                for z in range(layers)
            ]
        cols = width // parts
        for z in range(layers):
            press_scr[...] = press[z][:rows]
            for k in range(parts):
                at = pl.multiple_of(target(mem, k, parts) * cols, cols)
                press_refs[k][member, z] = press_scr[:, pl.ds(at, cols)]
            weight = perm[z][:rows]
            for kind, value in enumerate((weight * press[z][:rows], weight)):
                hi = value.astype(BF)
                lo = (value - hi.astype(F32)).astype(BF)
                for part, piece in enumerate((hi, lo)):
                    at = (((kind * 2 + part) * members + member) * layers + z) * rows
                    v_scr[pl.ds(pl.multiple_of(at, rows), rows), :] = piece
        return 0

    lax.fori_loop(0, members, sweep, 0)

    slots, wells = ids_ref.shape
    cells = layers * rows
    layer_at, rest = split(ids_ref[...], grid_rows * width)
    row_at, col = split(rest, width)
    row_at = row_at - tile * rows
    used = (iota((slots, wells), 0) < count_ref[...]) & (row_at >= 0) & (row_at < rows)
    sel = jnp.where(used, layer_at * rows + row_at, -1)
    sums = jnp.zeros((4 * members, wells), F32)
    for slot in range(0, slots, 2):
        sel_two = jnp.concatenate([sel[slot : slot + 1], sel[slot + 1 : slot + 2]], axis=1)
        col_two = jnp.concatenate([col[slot : slot + 1], col[slot + 1 : slot + 2]], axis=1)
        here = iota((width, 2 * wells), 0) == col_two
        got = jnp.dot(v_scr[...], jnp.where(here, 1.0, 0.0).astype(BF), preferred_element_type=F32)
        mine = iota((cells, 2 * wells), 0) == sel_two
        picked = jnp.where(mine[None], got.reshape(4 * members, cells, 2 * wells), 0.0)
        both = jnp.sum(picked, axis=1)
        sums = sums + both[:, :wells] + both[:, wells:]
    sums_ref[0:members] = sums[0:members] + sums[members : 2 * members]
    sums_ref[members : 2 * members] = sums[2 * members : 3 * members] + sums[3 * members :]


def decode(parts, tile_vec, mem_vec, grid_rows, field, near, far, prev, src, win, wmix, gains, ids, counts):
    layers, members, rows, width = field.shape
    groups = layers * members
    total = groups * width // 2
    wells = ids.shape[1]
    return pl.pallas_call(
        functools.partial(decode_kernel, grid_rows),
        in_specs=[SMEM] * 2 + [VMEM] * 10,
        out_specs=[VMEM] * (parts + 1),
        out_shape=[jax.ShapeDtypeStruct((members, layers, rows, width // parts), F32)] * parts
        + [jax.ShapeDtypeStruct((2 * members, wells), F32)],
        scratch_shapes=[
            pltpu.VMEM((groups, RING, width), F32),
            pltpu.VMEM((width + 8, 128), F32),
            pltpu.VMEM((total, 256), BF),
            pltpu.VMEM((LIFT_BLOCKS, total, 256), BF),
            pltpu.VMEM((LIFT_BLOCKS, total, 256), BF),
            pltpu.VMEM((MIX_BLOCKS, total, 128), BF),
            pltpu.VMEM((MIX_BLOCKS * 128, 128), BF),
            pltpu.VMEM((4 * groups * rows, width), BF),
            pltpu.VMEM((rows, width), F32),
        ],
        compiler_params=pltpu.CompilerParams(vmem_limit_bytes=52 * 2**20),
    )(tile_vec, mem_vec, field, near, far, prev, src, win, wmix, gains, ids, counts)


def update_kernel(mem_ref, refs, swap_refs, obs_ref, err_ref, press_ref, data_ref, new_ref, all_scr, step_scr):
    count = len(refs)
    own = refs[0].shape[0]
    members, wells = obs_ref.shape
    mem = mem_ref[0]
    for k in range(count):
        source = origin(mem, k, count)
        all_scr[source] = refs[k][...]
        press_ref[source] = swap_refs[k][...]
    every = jnp.concatenate([all_scr[k] for k in range(count)], axis=0)
    data, every = every[:, :wells], every[:, wells:]
    data_ref[...] = data
    scale = 2.0 * err_ref[...]
    root = math.sqrt(members - 1)
    scaled = (data - jnp.mean(data, axis=0, keepdims=True)) / (root * scale)
    innov = (obs_ref[...] - data) / scale
    dims = (((1,), (1,)), ((), ()))
    exact = lax.Precision.HIGHEST
    eye = (iota((members, members), 0) == iota((members, members), 1)).astype(F32)
    gram = eye + lax.dot_general(scaled, scaled, dims, precision=exact, preferred_element_type=F32)
    cross = lax.dot_general(innov, scaled, dims, precision=exact, preferred_element_type=F32)
    right = (every - jnp.mean(every, axis=0, keepdims=True)) / root
    place = iota((members, 1), 0)
    for k in range(members):
        inverse = 1.0 / gram[k : k + 1, k : k + 1]
        factor = jnp.where(place == k, 0.0, gram[:, k : k + 1])
        gram_row = gram[k : k + 1, :] * inverse
        right_row = right[k : k + 1, :] * inverse
        gram = jnp.where(place == k, gram_row, gram - factor * gram_row)
        right = jnp.where(place == k, right_row, right - factor * right_row)
    new = every + jnp.dot(cross, right, precision=exact, preferred_element_type=F32)
    for k in range(count):
        step_scr[k] = new[k * own : (k + 1) * own]
    new_ref[...] = step_scr[mem]


def update(mem_vec, pieces, swaps, obs, err):
    count = len(pieces)
    own, total = pieces[0].shape
    members, wells = obs.shape

    def kernel(mem_ref, *refs):
        update_kernel(mem_ref, refs[:count], refs[count : 2 * count], *refs[2 * count :])

    return pl.pallas_call(
        kernel,
        in_specs=[SMEM] + [VMEM] * (2 * count + 2),
        out_specs=[VMEM] * 3,
        out_shape=[
            jax.ShapeDtypeStruct((count,) + swaps[0].shape, F32),
            jax.ShapeDtypeStruct((members, wells), F32),
            jax.ShapeDtypeStruct((own, total - wells), F32),
        ],
        scratch_shapes=[
            pltpu.VMEM((count, own, total), F32),
            pltpu.VMEM((count, own, total - wells), F32),
        ],
        compiler_params=pltpu.CompilerParams(vmem_limit_bytes=24 * 2**20),
    )(mem_vec, *pieces, *swaps, obs, err)


def gathered(pieces, axis):
    count = lax.axis_size(axis)
    return [pieces[0]] + [
        lax.ppermute(pieces[k], axis, [(i, target(i, k, count)) for i in range(count)]) for k in range(1, count)
    ]


def summed(own, axis):
    count = lax.axis_size(axis)
    if count & (count - 1):
        return lax.psum(own, axis)
    k = 1
    while k < count:
        jumps = (k, 2 * k, 3 * k) if 4 * k <= count else (k,)
        own = own + sum(lax.ppermute(own, axis, [(i, i ^ j) for i in range(count)]) for j in jumps)
        k *= len(jumps) + 1
    return own


def halo(near, far, axis):
    count = lax.axis_size(axis)
    swap = lambda first: [p for i in range(first, count - 1, 2) for p in ((i, i + 1), (i + 1, i))]
    far = lax.ppermute(far, axis, swap(1))
    return lax.ppermute(near, axis, swap(0)), far


def body(
    latents,
    basis,
    conv_in,
    conv_mid,
    conv_out,
    pressure_prev,
    source,
    perf_cells,
    perf_count,
    obs_perturbed,
    obs_error,
):
    members = latents.shape[0]
    layers, rows, width = basis.shape[1:]
    tiles = lax.axis_size("tile")
    parts = lax.axis_size("mem")
    grid_rows = rows * tiles
    tile_vec = lax.axis_index("tile").astype(jnp.int32).reshape(1)
    mem_vec = lax.axis_index("mem").astype(jnp.int32).reshape(1)

    field, near, far = field_of(tile_vec, latents, basis, pressure_prev, source)
    near, far = halo(near, far, "tile")
    win, wmix, gains = placed(tile_vec, grid_rows, rows, conv_in, conv_mid, conv_out.reshape(1, -1))
    *press, sums = decode(
        parts, tile_vec, mem_vec, grid_rows, field, near, far, pressure_prev, source,
        win, wmix, gains, perf_cells.T, perf_count.reshape(1, -1),
    )
    swaps = gathered(press, "mem")
    sums = summed(sums, "tile")
    well = jnp.concatenate([sums[:members] / sums[members:], latents], axis=1)
    pieces = gathered([well] * parts, "mem")
    press, data, new = update(mem_vec, pieces, swaps, obs_perturbed, obs_error.reshape(1, -1))
    return (press.reshape((parts * members,) + press.shape[2:]), data, new)


def solution(mesh):
    return jax.shard_map(
        body,
        mesh=mesh,
        in_specs=(
            P("mem", None),
            P(None, None, "tile", None),
            P(),
            P(),
            P(),
            P(None, "tile", None),
            P(None, "tile", None),
            P(),
            P(),
            P(),
            P(),
        ),
        out_specs=(P(None, None, "tile", "mem"), P(), P("mem", None)),
        check_vma=False,
    )
```

time: 101 us -> 76 us (0.75)
  Pallas kernels: 56.5 us -> 47.5 us
  local copies, waits for them, and re-layouts: 10.9 us -> 2.17 us
  starting transfers between devices: 21 us -> 18 us
  waiting for transfers between devices: 9.92 us -> 7.27 us
  other arithmetic: 1.4 us -> 0.03 us
    pallas_call x1, Pallas kernels: 49 us -> 37.7 us  [decode(): pl.pallas_call(functools.partial(decode_kernel, grid_rows), in_specs=[SME...]
    unnamed x35 -> x24, local copies, waits for them, and re-layouts: 9.86 us -> 2.17 us
    all_to_all x1 -> x0, starting transfers between devices: 3.46 us -> none  [body(): swapped = lax.all_to_all(press, 'mem', 0, 0)]
    ppermute x11 -> x12, waiting for transfers between devices: 9.92 us -> 7.27 us  [the longest x4 4.22 us: summed(): lax.ppermute(own, axis, [(i, i ^ j) for i in range(count)])]
    pallas_call x2, Pallas kernels: 4.5 us -> 6.82 us  [the longest x1 5.69 us: field_of(): pl.pallas_call(field_kernel, in_specs=[SMEM, VMEM, pl.BlockSpec(memory_sp...]
    ppermute x11 -> x12, starting transfers between devices: 17.5 us -> 18 us  [the longest x4 9.59 us: summed(): lax.ppermute(own, axis, [(i, i ^ j) for i in range(count)])]
  transfers between devices with their start and end apart: 12 -> 12, of which waited for: 6 -> 6; matrix products, arithmetic and copies ran while one was open for 2% -> 0% of each run, Pallas kernels for 4% -> 1%
where the time goes in v2:
time: 76 us; the launch traced here: 75.8 us
  Pallas kernels  47.5 us (62%)
  starting transfers between devices  18 us (24%)
  waiting for transfers between devices  7.27 us (10%)
  local copies, waits for them, and re-layouts  2.17 us (3%)
  between operations  0.87 us (1%)
    pallas_call x1, Pallas kernels, decode(): pl.pallas_call(functools.partial(decode_kernel, grid_rows), in_specs=[SME...  37.7 us
    ppermute x4, starting transfers between devices, summed(): lax.ppermute(own, axis, [(i, i ^ j) for i in range(count)])  9.59 us
    pallas_call x1, Pallas kernels, field_of(): pl.pallas_call(field_kernel, in_specs=[SMEM, VMEM, pl.BlockSpec(memory_sp...  5.69 us
    ppermute x6, starting transfers between devices, gathered(): lax.ppermute(pieces[k], axis, [(i, target(i, k, count)) for i in range(co...  4.72 us
    ppermute x4, waiting for transfers between devices, summed(): lax.ppermute(own, axis, [(i, i ^ j) for i in range(count)])  4.22 us
    ppermute x1, starting transfers between devices, halo(): return (lax.ppermute(near, axis, swap(0)), far)  3.03 us
    pallas_call x1, Pallas kernels, update(): pl.pallas_call(kernel, in_specs=[SMEM] + [VMEM] * (2 * count + 2), out_sp...  2.98 us
    ppermute x6, waiting for transfers between devices, gathered(): lax.ppermute(pieces[k], axis, [(i, target(i, k, count)) for i in range(co...  2.34 us
  transfers between devices with their start and end apart: 12, of which 6 were waited for; matrix products, arithmetic and copies ran while one was open for 0% of the time, Pallas kernels for 1%

profile of v2, /device:TPU:0, one launch (start us, length us, event | category | flops | bytes accessed | tf_op | source)
XLA Modules:
  0.0 75.8 jit_solution(403242128024489654)
XLA Ops:
  0.7 5.7 %shard_map.130 = (f32[2,6,16,512]{3,2,1,0:T(8,128)}, f32[8,8,512]{2,1,0:T(8,128)}, f32[8,8,512]{2,1,0:T(8,128)}) custom-call(s32[1]{0:T(128)} %bitcast.1.tile_ref, f32[6,256]{1,0:T(8,128)} %lat_ref.1, bf16[256,2,16,512]{3,2,1,0:T(8,128)(2,1)} %basis_ref.1, f32[2,16,512]{2,1,0:T(8,128)} %prev_ref.3, f32[2,16,512]{2,1,0:T(8,128)} %src_ref.3), custom_call_target="tpu_custom_call" | custom-call | tf_op jit(solution)/shard_map/pallas_call | solution.py:130
  6.4 3.0 %collective-permute-start = (f32[8,8,512]{2,1,0:T(8,128)}, f32[8,8,512]{2,1,0:T(8,128)S(1)}, u32[]{:S(2)}, u32[]{:S(2)}) collective-permute-start(f32[8,8,512]{2,1,0:T(8,128)} %get-tuple-element.18), channel_id=1, source_target_pairs={{0,1},{1,0},{2,3},{3,2},{4,5},{5,4},{6,7},{7,6},{8,9},{9,8},{10,11... | collective-permute-start | bytes 393224 | tf_op jit(solution)/shard_map/ppermute | solution.py:500
  9.5 0.7 collective-permute-start.1
  10.2 1.1 %shard_map.131 = (bf16[11,256,256]{2,1,0:T(8,128)(2,1)S(1)}, bf16[1024,256]{1,0:T(8,128)(2,1)S(1)}, f32[16,128]{1,0:T(8,128)S(1)}) custom-call(s32[1]{0:T(128)} %bitcast.1.tile_ref, bf16[9,64]{1,0:T(8,128)(2,1)S(1)} %copy-done.7, bf16[9,64,64]{2,1,0:T(8,128)(2,1)S(1)} %copy-done.6, bf16[1,64]{1,0:T(2,128)(2,1)S(1)} %bitcast.6), custom_call_target="tpu_custom_call" | custom-call | flops 900000000 | bytes 3000000 | tf_op jit(solution)/shard_map/pallas_call | solution.py:78
  11.3 1.1 %copy-done = bf16[11,256,256]{2,1,0:T(8,128)(2,1)} copy-done((bf16[11,256,256]{2,1,0:T(8,128)(2,1)}, bf16[11,256,256]{2,1,0:T(8,128)(2,1)S(1)}, u32[]{:S(2)}) %copy-start) | copy-done | bytes 1441816
  12.5 0.7 collective-permute-done.near_ref
  13.2 0.0 collective-permute-done.1.far_ref
  13.2 0.0 copy-done.2
  13.2 0.0 copy-start.1
  13.2 1.0 %copy-done.1 = f32[2,6,16,512]{3,2,1,0:T(8,128)S(1)} copy-done((f32[2,6,16,512]{3,2,1,0:T(8,128)S(1)}, f32[2,6,16,512]{3,2,1,0:T(8,128)}, u32[]{:S(2)}) %copy-start.1) | copy-done | bytes 393240
  14.2 37.7 %shard_map.132 = (f32[6,2,16,128]{3,2,1,0:T(8,128)S(1)}, f32[6,2,16,128]{3,2,1,0:T(8,128)S(1)}, f32[6,2,16,128]{3,2,1,0:T(8,128)S(1)}, f32[6,2,16,128]{3,2,1,0:T(8,128)S(1)}, f32[12,384]{1,0:T(8,128)S(1)}) custom-call(s32[1]{0:T(128)} %bitcast.1.tile_ref, s32[1]{0:T(128)} %bitcast.mem_ref, f32[2,6,16,512]{3,2,1,0:T(8,128)S(1)} %copy-done.1, ...), custom_call_target="tpu_custom_call" | custom-call | tf_op jit(solution)/shard_map/pallas_call | solution.py:395
  51.9 4.7 %collective-permute-start.2 = (f32[12,384]{1,0:T(8,128)S(1)}, f32[12,384]{1,0:T(8,128)S(1)}, u32[]{:S(2)}, u32[]{:S(2)}) collective-permute-start(f32[12,384]{1,0:T(8,128)S(1)} %get-tuple-element.23), channel_id=1, source_target_pairs={{0,1},{1,0},{2,3},{3,2},{4,5},{5,4},{6,7},{7,6},{8,9},{9,8},{10,11... | collective-permute-start | bytes 55304 | tf_op jit(solution)/shard_map/ppermute | solution.py:491
  56.6 1.7 %collective-permute-start.3 = (f32[12,384]{1,0:T(8,128)S(1)}, f32[12,384]{1,0:T(8,128)S(1)}, u32[]{:S(2)}, u32[]{:S(2)}) collective-permute-start(f32[12,384]{1,0:T(8,128)S(1)} %get-tuple-element.23), channel_id=1, source_target_pairs={{0,2},{1,3},{2,0},{3,1},{4,6},{5,7},{6,4},{7,5},{8,10},{9,11},{10,... | collective-permute-start | bytes 55304 | tf_op jit(solution)/shard_map/ppermute | solution.py:491
  58.3 1.0 %collective-permute-start.4 = (f32[12,384]{1,0:T(8,128)S(1)}, f32[12,384]{1,0:T(8,128)S(1)}, u32[]{:S(2)}, u32[]{:S(2)}) collective-permute-start(f32[12,384]{1,0:T(8,128)S(1)} %get-tuple-element.23), channel_id=1, source_target_pairs={{0,3},{1,2},{2,1},{3,0},{4,7},{5,6},{6,5},{7,4},{8,11},{9,10},{10,... | collective-permute-start | bytes 55304 | tf_op jit(solution)/shard_map/ppermute | solution.py:491
  59.2 0.0 collective-permute-done.2
  59.2 1.2 %collective-permute-done.3 = f32[12,384]{1,0:T(8,128)S(1)} collective-permute-done((f32[12,384]{1,0:T(8,128)S(1)}, f32[12,384]{1,0:T(8,128)S(1)}, u32[]{:S(2)}, u32[]{:S(2)}) %collective-permute-start.3) | collective-permute-done | bytes 18464 | tf_op jit(solution)/shard_map/ppermute | solution.py:491
  60.4 2.6 %collective-permute-done.4 = f32[12,384]{1,0:T(8,128)S(1)} collective-permute-done((f32[12,384]{1,0:T(8,128)S(1)}, f32[12,384]{1,0:T(8,128)S(1)}, u32[]{:S(2)}, u32[]{:S(2)}) %collective-permute-start.4) | collective-permute-done | bytes 18464 | tf_op jit(solution)/shard_map/ppermute | solution.py:491
  63.0 2.2 %collective-permute-start.5 = (f32[12,384]{1,0:T(8,128)S(1)}, f32[12,384]{1,0:T(8,128)S(1)}, u32[]{:S(2)}, u32[]{:S(2)}) collective-permute-start(f32[12,384]{1,0:T(8,128)S(1)} %add_add_fusion), channel_id=1, source_target_pairs={{0,4},{1,5},{2,6},{3,7},{4,0},{5,1},{6,2},{7,3},{8,12},{9,13},{10,... | collective-permute-start | bytes 55304 | tf_op jit(solution)/shard_map/ppermute | solution.py:491
  65.3 1.5 %collective-permute-start.10 = (f32[6,2,16,128]{3,2,1,0:T(8,128)S(1)}, f32[6,2,16,128]{3,2,1,0:T(8,128)S(1)}, u32[]{:S(2)}, u32[]{:S(2)}) collective-permute-start(f32[6,2,16,128]{3,2,1,0:T(8,128)S(1)} %get-tuple-element.26), channel_id=1, source_target_pairs={{0,16},{8,24},{16,0},{24,8},{1,17},{9,25},{17,1},{25,9},{2,18},{10... | collective-permute-start | bytes 294920 | tf_op jit(solution)/shard_map/ppermute | solution.py:480
  66.7 0.0 collective-permute-start.11
  66.7 0.7 collective-permute-start.9
  67.4 0.5 collective-permute-done.5
  67.9 0.1 collective-permute-start.6
  68.0 1.6 %collective-permute-start.7 = (f32[6,640]{1,0:T(8,128)S(1)}, f32[6,640]{1,0:T(8,128)S(1)}, u32[]{:S(2)}, u32[]{:S(2)}) collective-permute-start(f32[6,640]{1,0:T(8,128)S(1)} %pad_maximum_fusion.refs_0_), channel_id=1, source_target_pairs={{0,16},{8,24},{16,0},{24,8},{1,17},{9,25},{17,1},{25,9},{2,18},{10... | collective-permute-start | bytes 46088 | tf_op jit(solution)/shard_map/ppermute | solution.py:480
  69.6 0.0 collective-permute-done.6.refs_1_
  69.6 0.9 %collective-permute-start.8 = (f32[6,640]{1,0:T(8,128)S(1)}, f32[6,640]{1,0:T(8,128)S(1)}, u32[]{:S(2)}, u32[]{:S(2)}) collective-permute-start(f32[6,640]{1,0:T(8,128)S(1)} %pad_maximum_fusion.refs_0_), channel_id=1, source_target_pairs={{0,24},{8,16},{16,8},{24,0},{1,25},{9,17},{17,9},{25,1},{2,26},{10... | collective-permute-start | bytes 46088 | tf_op jit(solution)/shard_map/ppermute | solution.py:480
  70.5 1.9 %collective-permute-done.7.refs_2_ = f32[6,640]{1,0:T(8,128)S(1)} collective-permute-done((f32[6,640]{1,0:T(8,128)S(1)}, f32[6,640]{1,0:T(8,128)S(1)}, u32[]{:S(2)}, u32[]{:S(2)}) %collective-permute-start.7) | collective-permute-done | bytes 15392 | tf_op jit(solution)/shard_map/ppermute | solution.py:480
  72.4 0.4 collective-permute-done.8.refs_3_
  72.8 0.0 collective-permute-done.10.refs_6_
  72.8 0.0 collective-permute-done.11.refs_7_
  72.8 0.0 collective-permute-done.9.refs_5_
  72.8 3.0 %shard_map.133 = (f32[4,6,2,16,128]{4,3,2,1,0:T(8,128)}, f32[24,384]{1,0:T(8,128)}, f32[6,256]{1,0:T(8,128)}) custom-call(s32[1]{0:T(128)} %bitcast.mem_ref, f32[6,640]{1,0:T(8,128)S(1)} %pad_maximum_fusion.refs_0_, f32[6,640]{1,0:T(8,128)S(1)} %collective-permute-done.6.refs_1_, f32[6,640]{1,0:T(8,128)S(1)} %collective-permute-done.7.refs_2_, ...), custom_call_target="tpu_custom_call" | custom-call | tf_op jit(solution)/shard_map/pallas_call | solution.py:460
  (26 shorter events, 0.1 us)
Async XLA Ops:
  0.6 67.2 %copy-start.9 = (f32[6,256]{1,0:T(8,128)S(1)}, f32[6,256]{1,0:T(8,128)}, u32[]{:S(2)}) copy-start(f32[6,256]{1,0:T(8,128)} %lat_ref.1) | copy-start | bytes 18436
  0.6 12.5 %copy-start.2 = (f32[2,16,512]{2,1,0:T(8,128)S(1)}, f32[2,16,512]{2,1,0:T(8,128)}, u32[]{:S(2)}) copy-start(f32[2,16,512]{2,1,0:T(8,128)} %prev_ref.3) | copy-start | bytes 196612
  0.7 12.5 %copy-start.3 = (f32[2,16,512]{2,1,0:T(8,128)S(1)}, f32[2,16,512]{2,1,0:T(8,128)}, u32[]{:S(2)}) copy-start(f32[2,16,512]{2,1,0:T(8,128)} %src_ref.3) | copy-start | bytes 196612
  0.7 9.5 %copy-start.10 = (s32[384]{0:T(512)S(1)}, s32[384]{0:T(512)}, u32[]{:S(2)}) copy-start(s32[384]{0:T(512)} %param.19) | copy-start | bytes 4612
  0.7 9.5 %copy-start.8 = (bf16[64]{0:T(256)(128)(2,1)S(1)}, bf16[64]{0:T(256)(128)(2,1)}, u32[]{:S(2)}) copy-start(bf16[64]{0:T(256)(128)(2,1)} %param.15) | copy-start | bytes 388
  0.7 9.5 %copy-start.7 = (bf16[9,64]{1,0:T(8,128)(2,1)S(1)}, bf16[9,64]{1,0:T(8,128)(2,1)}, u32[]{:S(2)}) copy-start(bf16[9,64]{1,0:T(8,128)(2,1)} %in_ref.1) | copy-start | bytes 3460
  0.7 9.5 %copy-start.6 = (bf16[9,64,64]{2,1,0:T(8,128)(2,1)S(1)}, bf16[9,64,64]{2,1,0:T(8,128)(2,1)}, u32[]{:S(2)}) copy-start(bf16[9,64,64]{2,1,0:T(8,128)(2,1)} %mid_ref.1) | copy-start | bytes 221188
  0.7 12.5 %copy-start.5 = (s32[384,8]{0,1:T(8,128)S(1)}, s32[384,8]{0,1:T(8,128)}, u32[]{:S(2)}) copy-start(s32[384,8]{0,1:T(8,128)} %param.18) | copy-start | bytes 36868
  0.7 69.8 %copy-start.11 = (f32[384]{0:T(512)S(1)}, f32[384]{0:T(512)}, u32[]{:S(2)}) copy-start(f32[384]{0:T(512)} %param.21) | copy-start | bytes 4612
  0.7 72.1 %copy-start.4 = (f32[24,384]{1,0:T(8,128)S(1)}, f32[24,384]{1,0:T(8,128)}, u32[]{:S(2)}) copy-start(f32[24,384]{1,0:T(8,128)} %refs_8_.1) | copy-start | bytes 110596
  6.4 6.7 %collective-permute-start = (f32[8,8,512]{2,1,0:T(8,128)}, f32[8,8,512]{2,1,0:T(8,128)S(1)}, u32[]{:S(2)}, u32[]{:S(2)}) collective-permute-start(f32[8,8,512]{2,1,0:T(8,128)} %get-tuple-element.18), channel_id=1, source_target_pairs={{0,1},{1,0},{2,3},{3,2},{4,5},{5,4},{6,7},{7,6},{8,9},{9,8},{10,11... | collective-permute-start | bytes 393224 | tf_op jit(solution)/shard_map/ppermute | solution.py:500
  9.5 3.7 %collective-permute-start.1 = (f32[8,8,512]{2,1,0:T(8,128)}, f32[8,8,512]{2,1,0:T(8,128)S(1)}, u32[]{:S(2)}, u32[]{:S(2)}) collective-permute-start(f32[8,8,512]{2,1,0:T(8,128)} %get-tuple-element.19), channel_id=1, source_target_pairs={{1,2},{2,1},{3,4},{4,3},{5,6},{6,5},{9,10},{10,9},{11,12},{12,11},... | collective-permute-start | bytes 393224 | tf_op jit(solution)/shard_map/ppermute | solution.py:499
  11.3 1.1 %copy-start = (bf16[11,256,256]{2,1,0:T(8,128)(2,1)}, bf16[11,256,256]{2,1,0:T(8,128)(2,1)S(1)}, u32[]{:S(2)}) copy-start(bf16[11,256,256]{2,1,0:T(8,128)(2,1)S(1)} %get-tuple-element.20.win_ref) | copy-start | bytes 4325380
  13.2 1.0 %copy-start.1 = (f32[2,6,16,512]{3,2,1,0:T(8,128)S(1)}, f32[2,6,16,512]{3,2,1,0:T(8,128)}, u32[]{:S(2)}) copy-start(f32[2,6,16,512]{3,2,1,0:T(8,128)} %get-tuple-element.17.field_ref) | copy-start | bytes 1179652
  51.9 7.4 %collective-permute-start.2 = (f32[12,384]{1,0:T(8,128)S(1)}, f32[12,384]{1,0:T(8,128)S(1)}, u32[]{:S(2)}, u32[]{:S(2)}) collective-permute-start(f32[12,384]{1,0:T(8,128)S(1)} %get-tuple-element.23), channel_id=1, source_target_pairs={{0,1},{1,0},{2,3},{3,2},{4,5},{5,4},{6,7},{7,6},{8,9},{9,8},{10,11... | collective-permute-start | bytes 55304 | tf_op jit(solution)/shard_map/ppermute | solution.py:491
  56.6 3.8 %collective-permute-start.3 = (f32[12,384]{1,0:T(8,128)S(1)}, f32[12,384]{1,0:T(8,128)S(1)}, u32[]{:S(2)}, u32[]{:S(2)}) collective-permute-start(f32[12,384]{1,0:T(8,128)S(1)} %get-tuple-element.23), channel_id=1, source_target_pairs={{0,2},{1,3},{2,0},{3,1},{4,6},{5,7},{6,4},{7,5},{8,10},{9,11},{10,... | collective-permute-start | bytes 55304 | tf_op jit(solution)/shard_map/ppermute | solution.py:491
  58.3 4.7 %collective-permute-start.4 = (f32[12,384]{1,0:T(8,128)S(1)}, f32[12,384]{1,0:T(8,128)S(1)}, u32[]{:S(2)}, u32[]{:S(2)}) collective-permute-start(f32[12,384]{1,0:T(8,128)S(1)} %get-tuple-element.23), channel_id=1, source_target_pairs={{0,3},{1,2},{2,1},{3,0},{4,7},{5,6},{6,5},{7,4},{8,11},{9,10},{10,... | collective-permute-start | bytes 55304 | tf_op jit(solution)/shard_map/ppermute | solution.py:491
  63.0 4.8 %collective-permute-start.5 = (f32[12,384]{1,0:T(8,128)S(1)}, f32[12,384]{1,0:T(8,128)S(1)}, u32[]{:S(2)}, u32[]{:S(2)}) collective-permute-start(f32[12,384]{1,0:T(8,128)S(1)} %add_add_fusion), channel_id=1, source_target_pairs={{0,4},{1,5},{2,6},{3,7},{4,0},{5,1},{6,2},{7,3},{8,12},{9,13},{10,... | collective-permute-start | bytes 55304 | tf_op jit(solution)/shard_map/ppermute | solution.py:491
  65.3 7.6 %collective-permute-start.10 = (f32[6,2,16,128]{3,2,1,0:T(8,128)S(1)}, f32[6,2,16,128]{3,2,1,0:T(8,128)S(1)}, u32[]{:S(2)}, u32[]{:S(2)}) collective-permute-start(f32[6,2,16,128]{3,2,1,0:T(8,128)S(1)} %get-tuple-element.26), channel_id=1, source_target_pairs={{0,16},{8,24},{16,0},{24,8},{1,17},{9,25},{17,1},{25,9},{2,18},{10... | collective-permute-start | bytes 294920 | tf_op jit(solution)/shard_map/ppermute | solution.py:480
  66.7 6.1 %collective-permute-start.11 = (f32[6,2,16,128]{3,2,1,0:T(8,128)S(1)}, f32[6,2,16,128]{3,2,1,0:T(8,128)S(1)}, u32[]{:S(2)}, u32[]{:S(2)}) collective-permute-start(f32[6,2,16,128]{3,2,1,0:T(8,128)S(1)} %get-tuple-element.27), channel_id=1, source_target_pairs={{0,24},{8,16},{16,8},{24,0},{1,25},{9,17},{17,9},{25,1},{2,26},{10... | collective-permute-start | bytes 294920 | tf_op jit(solution)/shard_map/ppermute | solution.py:480
  66.7 6.1 %collective-permute-start.9 = (f32[6,2,16,128]{3,2,1,0:T(8,128)S(1)}, f32[6,2,16,128]{3,2,1,0:T(8,128)S(1)}, u32[]{:S(2)}, u32[]{:S(2)}) collective-permute-start(f32[6,2,16,128]{3,2,1,0:T(8,128)S(1)} %get-tuple-element.25), channel_id=1, source_target_pairs={{0,8},{8,0},{16,24},{24,16},{1,9},{9,1},{17,25},{25,17},{2,10},{10... | collective-permute-start | bytes 294920 | tf_op jit(solution)/shard_map/ppermute | solution.py:480
  67.9 1.7 %collective-permute-start.6 = (f32[6,640]{1,0:T(8,128)S(1)}, f32[6,640]{1,0:T(8,128)S(1)}, u32[]{:S(2)}, u32[]{:S(2)}) collective-permute-start(f32[6,640]{1,0:T(8,128)S(1)} %pad_maximum_fusion.refs_0_), channel_id=1, source_target_pairs={{0,8},{8,0},{16,24},{24,16},{1,9},{9,1},{17,25},{25,17},{2,10},{10... | collective-permute-start | bytes 46088 | tf_op jit(solution)/shard_map/ppermute | solution.py:480
  68.0 4.4 %collective-permute-start.7 = (f32[6,640]{1,0:T(8,128)S(1)}, f32[6,640]{1,0:T(8,128)S(1)}, u32[]{:S(2)}, u32[]{:S(2)}) collective-permute-start(f32[6,640]{1,0:T(8,128)S(1)} %pad_maximum_fusion.refs_0_), channel_id=1, source_target_pairs={{0,16},{8,24},{16,0},{24,8},{1,17},{9,25},{17,1},{25,9},{2,18},{10... | collective-permute-start | bytes 46088 | tf_op jit(solution)/shard_map/ppermute | solution.py:480
  69.6 3.2 %collective-permute-start.8 = (f32[6,640]{1,0:T(8,128)S(1)}, f32[6,640]{1,0:T(8,128)S(1)}, u32[]{:S(2)}, u32[]{:S(2)}) collective-permute-start(f32[6,640]{1,0:T(8,128)S(1)} %pad_maximum_fusion.refs_0_), channel_id=1, source_target_pairs={{0,24},{8,16},{16,8},{24,0},{1,25},{9,17},{17,9},{25,1},{2,26},{10... | collective-permute-start | bytes 46088 | tf_op jit(solution)/shard_map/ppermute | solution.py:480

commit v3 on v2

--- a/solution.py
+++ b/solution.py
@@ -9,9 +9,11 @@
 from jax.sharding import PartitionSpec as P
 
 SWEEPS = 2
+PACKED = 96
 HALO = 4
 RING = 24
 LIFT_BLOCKS = 11
+HELD = 5
 MIX_BLOCKS = 10
 CHUNK_GROUPS = 12
 SEG = 16
@@ -98,6 +100,9 @@
     ]
     for copy in copies:
         copy.start()
+    even_tile = tile_ref[0] & 1 == 0
+    shape = (PACKED, 2 * (layers * members + 2 * layers) * rows)
+    picks = [packed_from(layers, members, rows, up, shape) for up in (even_tile, jnp.logical_not(even_tile))]
     lat = lat_ref[...].astype(BF)
     own = iota((rows, span), 0) == iota((rows, span), 1) & (rows - 1)
     behind = iota((total, span), 0) - split(iota((total, span), 1), rows)[0]
@@ -110,37 +115,74 @@
             part = jnp.dot(left, held[c, :, z].reshape(span, width), preferred_element_type=F32)
             part = part.reshape(members, rows, width)
             field_ref[z] = part if c == 0 else field_ref[z] + part
-    tiles = [field_ref.at[z, m] for z in range(layers) for m in range(members)]
-    tiles += [prev_ref.at[z] for z in range(layers)] + [src_ref.at[z] for z in range(layers)]
-    first = iota((8, width), 0) < HALO
-    even_tile = tile_ref[0] & 1 == 0
-    for pair in range(len(tiles) // 2):
-        even, odd = tiles[2 * pair], tiles[2 * pair + 1]
-        low = jnp.where(first, even[0:8], pltpu.roll(odd[0:8], HALO, 0))
-        high = jnp.where(first, pltpu.roll(odd[rows - 8 : rows], HALO, 0), even[rows - 8 : rows])
-        near_ref[pair] = jnp.where(even_tile, high, low)
-        far_ref[pair] = jnp.where(even_tile, low, high)
+    exact, rest = [], []
+    for value in (field_ref[...].reshape(-1, width), prev_ref[...].reshape(-1, width), src_ref[...].reshape(-1, width)):
+        hi = value.astype(BF)
+        exact.append(hi)
+        rest.append((value - hi.astype(F32)).astype(BF))
+    pool = jnp.concatenate([exact[0], rest[0], exact[1], rest[1], exact[2], rest[2]], axis=0)
+    for ref, pick in zip((near_ref, far_ref), picks):
+        ref[...] = jnp.dot(pick, pool, preferred_element_type=F32).astype(BF)
+
+
+def packed_from(layers, members, rows, upper, shape):
+    groups = layers * members
+    r, at = iota((shape[0], 1), 0), iota(shape, 1)
+    last = jnp.where(upper, 1, 0)
+    group = (r * 43) >> 8
+    j = r - 6 * group
+    row_hi = jnp.where(last == 1, rows - HALO + j, j)
+    row_lo = jnp.where(last == 1, rows - 2 + j - HALO, j - HALO)
+    field = jnp.where(j < HALO, group * rows + row_hi, (groups + group) * rows + row_lo)
+    p = r - 6 * groups
+    half, j = (p >> 1) & 1, p & 1
+    prev = (2 * groups + half * layers + (p >> 2)) * rows + jnp.where(last == 1, rows - 2 + j, j)
+    s = p - 4 * layers
+    src = (2 * groups + (2 + (s & 1)) * layers + (s >> 1)) * rows + jnp.where(last == 1, rows - 1, 0)
+    wanted = jnp.where(p < 0, field, jnp.where(s < 0, prev, jnp.where(s < 2 * layers, src, -1)))
+    return jnp.where(wanted == at, 1.0, 0.0).astype(BF)
+
+
+def unpacked_to(layers, members, upper, shape):
+    groups = layers * members
+    r, at = iota((shape[0], 1), 0), iota(shape, 1)
+    group, s = r >> 3, r & 7
+    up = jnp.where(upper, 1, 0)
+    j = jnp.where(up == 1, s - HALO, s)
+    mine = (j >= 0) & (j < HALO)
+    near = jnp.where(up == 1, j - 2, j)
+    close = mine & (near >= 0) & (near < 2)
+    z = group - groups
+    hi = jnp.where(z < 0, group * 6 + j, 6 * groups + z * 4 + near)
+    lo = jnp.where(z < 0, group * 6 + HALO + near, 6 * groups + z * 4 + 2 + near)
+    is_src = z >= layers
+    src = 6 * groups + 4 * layers + 2 * (z - layers)
+    edge = close & (jnp.where(up == 1, near, 1 - near) == 1)
+    hi = jnp.where(is_src, src, hi)
+    lo = jnp.where(is_src, src + 1, lo)
+    use_hi = (z < 0) & mine | (z >= 0) & (z < layers) & close | is_src & edge
+    use_lo = (z < layers) & close | is_src & edge
+    return jnp.where(use_hi & (at == hi) | use_lo & (at == lo), 1.0, 0.0).astype(BF)
 
 
 def field_of(tile_vec, latents, basis, prev, src):
     total, layers, rows, width = basis.shape
     members = latents.shape[0]
     comps = 32
-    pairs = (layers * members + 2 * layers) // 2
     return pl.pallas_call(
         field_kernel,
-        in_specs=[SMEM, VMEM, pl.BlockSpec(memory_space=pl.ANY), VMEM, VMEM],
+        in_specs=[SMEM, VMEM, pl.BlockSpec(memory_space=pltpu.HBM), VMEM, VMEM],
         out_specs=[VMEM] * 3,
         out_shape=[
             jax.ShapeDtypeStruct((layers, members, rows, width), F32),
-            jax.ShapeDtypeStruct((pairs, 8, width), F32),
-            jax.ShapeDtypeStruct((pairs, 8, width), F32),
+            jax.ShapeDtypeStruct((PACKED, width), BF),
+            jax.ShapeDtypeStruct((PACKED, width), BF),
         ],
         scratch_shapes=[
             pltpu.VMEM((total // comps, comps, layers, rows, width), BF),
             pltpu.SemaphoreType.DMA((total // comps,)),
         ],
-        compiler_params=pltpu.CompilerParams(vmem_limit_bytes=58 * 2**20),
+        compiler_params=pltpu.CompilerParams(vmem_limit_bytes=57 * 2**20),
     )(tile_vec, latents, basis, prev, src)
 
 
@@ -175,9 +217,9 @@
     *refs,
 
 ):
-    parts = len(refs) - 10
+    parts = len(refs) - 11
     press_refs, sums_ref = refs[:parts], refs[parts]
-    f_scr, t_scr, pt_scr, lift_scr, side_scr, deep_scr, wout_scr, v_scr, press_scr = refs[parts + 1 :]
+    f_scr, t_scr, pt_scr, lift_scr, side_scr, deep_scr, wout_scr, v_scr, press_scr, third_scr = refs[parts + 1 :]
     layers, members, rows, width = field_ref.shape
     groups = layers * members
     steps = width // (2 * SEG)
@@ -185,18 +227,19 @@
     tile, mem = tile_ref[0], mem_ref[0]
     even_tile = tile & 1 == 0
 
-    def outer(pair):
-        near, far = near_ref[pair], far_ref[pair]
-        up, down = jnp.where(even_tile, near, far), jnp.where(even_tile, far, near)
-        first = iota(up.shape, 0) < HALO
-        return jnp.where(first, up, down), pltpu.roll(jnp.where(first, down, up), HALO, 0)
+    shape = ((groups + 2 * layers) * 8, PACKED)
+    from_near = unpacked_to(layers, members, jnp.logical_not(even_tile), shape)
+    from_far = unpacked_to(layers, members, even_tile, shape)
+    third_scr[...] = (
+        jnp.dot(from_near, near_ref[...], preferred_element_type=F32)
+        + jnp.dot(from_far, far_ref[...], preferred_element_type=F32)
+    ).reshape(-1, 8, width)
 
     def load(pair, _):
-        thirds = outer(pair)
         for half in range(2):
             group = 2 * pair + half
             own = field_ref[group // members, lax.rem(group, members)]
-            f = jnp.concatenate([own, thirds[half]], axis=0)
+            f = jnp.concatenate([own, third_scr[group]], axis=0)
             f_scr[group] = f
             hi = f.astype(BF).astype(F32)
             lo = f - hi
@@ -205,12 +248,12 @@
             hi_left = jnp.where(edge, 0.0, pltpu.roll(hi, 1, 1))
             lo_left = jnp.where(edge, 0.0, pltpu.roll(lo, 1, 1))
             tall = jnp.concatenate([hi_left, zero, lo_left, zero, hi, zero, lo, zero], axis=0).T
-            t_scr[0:width, :] = tall
+            t_scr[half, 0:width, :] = tall
             end = pltpu.roll(tall[width - 8 : width], 64, 1)
             end = jnp.where(iota(end.shape, 1) < 64, end, 0.0)
-            t_scr[width : width + 8, :] = pltpu.roll(end, 1, 0)
+            t_scr[half, width : width + 8, :] = pltpu.roll(end, 1, 0)
             for q in range(steps + 1):
-                part = t_scr[pl.ds(2 * q, SEG, stride=2 * steps), :].astype(BF)
+                part = t_scr[half, pl.ds(2 * q, SEG, stride=2 * steps), :].astype(BF)
                 if q < steps:
                     pt_scr[pl.ds(pl.multiple_of(group * block_rows + q * SEG, SEG), SEG), 0:128] = part
                 if q > 0:
@@ -222,13 +265,17 @@
     chunk = CHUNK_GROUPS * block_rows
     chunks = groups * block_rows // chunk
 
+    def slot_of(block):
+        return jnp.where(block == 0, 0, 1 + lax.rem(block + HELD - 1, HELD))
+
     def lift(t, _):
         block, part = t // chunks, lax.rem(t, chunks)
+        slot = slot_of(block)
         at = pl.multiple_of(part * chunk, chunk)
         wide = jnp.dot(pt_scr[pl.ds(at, chunk), :], win_ref[block], preferred_element_type=F32)
         wide = jnp.maximum(wide, 0.0)
         tight = wide.astype(BF)
-        lift_scr[block, pl.ds(at, chunk), :] = tight
+        lift_scr[slot, pl.ds(at, chunk), :] = tight
         right = iota((SEG, 256), 1) & 64 == 0
         row = iota((SEG, 256), 0)
         for i in range(chunk // block_rows):
@@ -240,7 +287,7 @@
                 r = base + q * SEG
                 nxt = after if q == steps - 1 else wide[r + SEG : r + 2 * SEG]
                 prv = before if q == 0 else wide[r - SEG : r]
-                side_scr[block, pl.ds(pl.multiple_of(at + r, SEG), SEG), :] = jnp.where(right, nxt, prv).astype(BF)
+                side_scr[slot, pl.ds(pl.multiple_of(at + r, SEG), SEG), :] = jnp.where(right, nxt, prv).astype(BF)
         return 0
 
 
@@ -248,13 +295,14 @@
 
     def mix(t, _):
         block, part = t // chunks + 1, lax.rem(t, chunks)
-        above = block - 1
-        below = jnp.where(block == LIFT_BLOCKS - 1, 0, block + 1)
+        above = slot_of(block - 1)
+        below = slot_of(jnp.where(block == LIFT_BLOCKS - 1, 0, block + 1))
+        here = slot_of(block)
         at = pl.ds(pl.multiple_of(part * chunk, chunk), chunk)
         x = jnp.concatenate(
             [
-                lift_scr[block, at, :],
-                side_scr[block, at, :],
+                lift_scr[here, at, :],
+                side_scr[here, at, :],
                 lift_scr[below, at, 0:128],
                 lift_scr[above, at, 128:256],
                 side_scr[below, at, 0:128],
@@ -281,25 +329,25 @@
     row = jnp.where(row < 0, row + RING, row)
     wout_scr[...] = jnp.where(n == (place & 1) * 32 + row, 1.0, 0.0).astype(BF)
 
-    def collect(pair, _):
+    def collect(pair, held):
         at = pl.ds(pl.multiple_of(pair * 2 * block_rows, 2 * block_rows), 2 * block_rows)
         x = jnp.concatenate([deep_scr[j, at, :] for j in range(MIX_BLOCKS)], axis=1)
         both = jnp.dot(x, wout_scr[...], preferred_element_type=F32)
         both = both[:block_rows] + pltpu.roll(both[block_rows:], 64, 1)
         for q in range(steps):
             part = both[q * SEG : (q + 1) * SEG]
-            t_scr[pl.ds(2 * q, SEG, stride=2 * steps), :] = part
-            t_scr[pl.ds(2 * q + 1, SEG, stride=2 * steps), :] = part
-        flat = t_scr[0:width, :].T
+            t_scr[held, pl.ds(2 * q, SEG, stride=2 * steps), :] = part
+            t_scr[held, pl.ds(2 * q + 1, SEG, stride=2 * steps), :] = part
+        flat = t_scr[held, 0:width, :].T
         even = iota((RING, width), 1) & 1 == 0
         for half in range(2):
             s = 64 * half
             f_scr[2 * pair + half] = f_scr[2 * pair + half] + jnp.where(
                 even, flat[s : s + RING], flat[s + 32 : s + 32 + RING]
             )
-        return 0
-
-    lax.fori_loop(0, groups // 2, collect, 0)
+
+    for pair in range(groups // 2):
+        collect(pair, pair)
 
     full = (RING, width)
     ring = iota(full, 0)
@@ -309,7 +357,7 @@
     not_last = iota(full, 1) < width - 1
 
     def ring_of(ref, group, z):
-        return jnp.concatenate([ref[z], outer(group // 2)[group % 2]], axis=0)
+        return jnp.concatenate([ref[z], third_scr[group]], axis=0)
 
     def row_next(v):
         return pltpu.roll(v, RING - 1, 0)
@@ -400,16 +448,17 @@
         + [jax.ShapeDtypeStruct((2 * members, wells), F32)],
         scratch_shapes=[
             pltpu.VMEM((groups, RING, width), F32),
-            pltpu.VMEM((width + 8, 128), F32),
+            pltpu.VMEM((groups // 2, width + 8, 128), F32),
             pltpu.VMEM((total, 256), BF),
-            pltpu.VMEM((LIFT_BLOCKS, total, 256), BF),
-            pltpu.VMEM((LIFT_BLOCKS, total, 256), BF),
+            pltpu.VMEM((HELD + 1, total, 256), BF),
+            pltpu.VMEM((HELD + 1, total, 256), BF),
             pltpu.VMEM((MIX_BLOCKS, total, 128), BF),
             pltpu.VMEM((MIX_BLOCKS * 128, 128), BF),
             pltpu.VMEM((4 * groups * rows, width), BF),
             pltpu.VMEM((rows, width), F32),
+            pltpu.VMEM((groups + 2 * layers, 8, width), F32),
         ],
-        compiler_params=pltpu.CompilerParams(vmem_limit_bytes=52 * 2**20),
+        compiler_params=pltpu.CompilerParams(vmem_limit_bytes=40 * 2**20),
     )(tile_vec, mem_vec, field, near, far, prev, src, win, wmix, gains, ids, counts)
 
 
@@ -435,14 +484,18 @@
     gram = eye + lax.dot_general(scaled, scaled, dims, precision=exact, preferred_element_type=F32)
     cross = lax.dot_general(innov, scaled, dims, precision=exact, preferred_element_type=F32)
     right = (every - jnp.mean(every, axis=0, keepdims=True)) / root
-    place = iota((members, 1), 0)
+    place = iota((members, 128), 0)
+    places = iota(right.shape, 0)
+    cols = [jnp.broadcast_to(gram[:, k : k + 1], (members, 128)) for k in range(members)]
     for k in range(members):
-        inverse = 1.0 / gram[k : k + 1, k : k + 1]
-        factor = jnp.where(place == k, 0.0, gram[:, k : k + 1])
-        gram_row = gram[k : k + 1, :] * inverse
-        right_row = right[k : k + 1, :] * inverse
-        gram = jnp.where(place == k, gram_row, gram - factor * gram_row)
-        right = jnp.where(place == k, right_row, right - factor * right_row)
+        inverse = 1.0 / cols[k][k : k + 1]
+        factor = jnp.where(place == k, 0.0, cols[k])
+        for i in range(k + 1, members):
+            row = cols[i][k : k + 1] * inverse
+            cols[i] = jnp.where(place == k, row, cols[i] - factor * row)
+        row = right[k : k + 1] * jnp.concatenate([inverse] * (right.shape[1] // 128), axis=1)
+        wide = jnp.concatenate([factor] * (right.shape[1] // 128), axis=1)
+        right = jnp.where(places == k, row, right - wide * row)
     new = every + jnp.dot(cross, right, precision=exact, preferred_element_type=F32)
     for k in range(count):
         step_scr[k] = new[k * own : (k + 1) * own]

time: 76 us -> 72.6 us (0.955)
  Pallas kernels: 47.5 us -> 44.4 us
  local copies, waits for them, and re-layouts: 2.17 us -> 1.04 us
    pallas_call x1, Pallas kernels: 37.7 us -> 36 us  [decode(): pl.pallas_call(functools.partial(decode_kernel, grid_rows), in_specs=[SME...]
    pallas_call x1, Pallas kernels: 2.98 us -> 1.56 us  [update(): pl.pallas_call(kernel, in_specs=[SMEM] + [VMEM] * (2 * count + 2), out_sp...]
    unnamed x24 -> x22, local copies, waits for them, and re-layouts: 2.17 us -> 1.03 us
  transfers between devices with their start and end apart: 12 -> 12, of which waited for: 6 -> 6; matrix products, arithmetic and copies ran while one was open for 0% -> 0% of each run, Pallas kernels for 1% -> 2%
where the time goes in v3:
time: 72.6 us; the launch traced here: 72.4 us
  Pallas kernels  44.4 us (61%)
  starting transfers between devices  18.4 us (25%)
  waiting for transfers between devices  7.69 us (11%)
  local copies, waits for them, and re-layouts  1.04 us (1%)
  between operations  0.86 us (1%)
    pallas_call x1, Pallas kernels, decode(): pl.pallas_call(functools.partial(decode_kernel, grid_rows), in_specs=[SME...  36 us
    ppermute x4, starting transfers between devices, summed(): lax.ppermute(own, axis, [(i, i ^ j) for i in range(count)])  9.94 us
    pallas_call x1, Pallas kernels, field_of(): pl.pallas_call(field_kernel, in_specs=[SMEM, VMEM, pl.BlockSpec(memory_sp...  5.78 us
    ppermute x6, starting transfers between devices, gathered(): lax.ppermute(pieces[k], axis, [(i, target(i, k, count)) for i in range(co...  4.76 us
    ppermute x4, waiting for transfers between devices, summed(): lax.ppermute(own, axis, [(i, i ^ j) for i in range(count)])  4.2 us
    ppermute x1, starting transfers between devices, halo(): return (lax.ppermute(near, axis, swap(0)), far)  3.03 us
    ppermute x6, waiting for transfers between devices, gathered(): lax.ppermute(pieces[k], axis, [(i, target(i, k, count)) for i in range(co...  2.34 us
    pallas_call x1, Pallas kernels, update(): pl.pallas_call(kernel, in_specs=[SMEM] + [VMEM] * (2 * count + 2), out_sp...  1.56 us
  transfers between devices with their start and end apart: 12, of which 6 were waited for; matrix products, arithmetic and copies ran while one was open for 0% of the time, Pallas kernels for 2%

profile of v3, /device:TPU:0, one launch (start us, length us, event | category | flops | bytes accessed | tf_op | source)
XLA Modules:
  0.0 72.4 jit_solution(8056861352357860500)
XLA Ops:
  0.7 5.8 %shard_map.130 = (f32[2,6,16,512]{3,2,1,0:T(8,128)}, bf16[96,512]{1,0:T(8,128)(2,1)}, bf16[96,512]{1,0:T(8,128)(2,1)}) custom-call(s32[1]{0:T(128)} %bitcast.1.tile_ref, f32[6,256]{1,0:T(8,128)} %lat_ref.1, bf16[256,2,16,512]{3,2,1,0:T(8,128)(2,1)} %basis_ref.1, f32[2,16,512]{2,1,0:T(8,128)} %prev_ref.3, f32[2,16,512]{2,1,0:T(8,128)} %src_ref.3), custom_call_target="tpu_custom_call" | custom-call | tf_op jit(solution)/shard_map/pallas_call | solution.py:172
  6.5 3.0 %collective-permute-start = (bf16[96,512]{1,0:T(8,128)(2,1)}, bf16[96,512]{1,0:T(8,128)(2,1)S(1)}, u32[]{:S(2)}, u32[]{:S(2)}) collective-permute-start(bf16[96,512]{1,0:T(8,128)(2,1)} %get-tuple-element.18), channel_id=1, source_target_pairs={{0,1},{1,0},{2,3},{3,2},{4,5},{5,4},{6,7},{7,6},{8,9},{9,8},{10,11... | collective-permute-start | bytes 294920 | tf_op jit(solution)/shard_map/ppermute | solution.py:553
  9.6 0.7 collective-permute-start.1
  10.2 0.0 copy-done.9
  10.3 1.1 %shard_map.131 = (bf16[11,256,256]{2,1,0:T(8,128)(2,1)S(1)}, bf16[1024,256]{1,0:T(8,128)(2,1)S(1)}, f32[16,128]{1,0:T(8,128)S(1)}) custom-call(s32[1]{0:T(128)} %bitcast.1.tile_ref, bf16[9,64]{1,0:T(8,128)(2,1)S(1)} %copy-done.6, bf16[9,64,64]{2,1,0:T(8,128)(2,1)S(1)} %copy-done.5, bf16[1,64]{1,0:T(2,128)(2,1)S(1)} %bitcast.6), custom_call_target="tpu_custom_call" | custom-call | flops 900000000 | bytes 3000000 | tf_op jit(solution)/shard_map/pallas_call | solution.py:80
  11.4 1.1 %collective-permute-done.near_ref = bf16[96,512]{1,0:T(8,128)(2,1)S(1)} collective-permute-done((bf16[96,512]{1,0:T(8,128)(2,1)}, bf16[96,512]{1,0:T(8,128)(2,1)S(1)}, u32[]{:S(2)}, u32[]{:S(2)}) %collective-permute-start) | collective-permute-done | bytes 98336 | tf_op jit(solution)/shard_map/ppermute | solution.py:553
  12.6 0.0 collective-permute-done.1.far_ref
  12.6 0.0 copy-done.2
  12.6 0.0 copy-start
  12.6 1.0 %copy-done = f32[2,6,16,512]{3,2,1,0:T(8,128)S(1)} copy-done((f32[2,6,16,512]{3,2,1,0:T(8,128)S(1)}, f32[2,6,16,512]{3,2,1,0:T(8,128)}, u32[]{:S(2)}) %copy-start) | copy-done | bytes 393240
  13.6 36.0 %shard_map.132 = (f32[6,2,16,128]{3,2,1,0:T(8,128)S(1)}, f32[6,2,16,128]{3,2,1,0:T(8,128)S(1)}, f32[6,2,16,128]{3,2,1,0:T(8,128)S(1)}, f32[6,2,16,128]{3,2,1,0:T(8,128)S(1)}, f32[12,384]{1,0:T(8,128)S(1)}) custom-call(s32[1]{0:T(128)} %bitcast.1.tile_ref, s32[1]{0:T(128)} %bitcast.mem_ref, f32[2,6,16,512]{3,2,1,0:T(8,128)S(1)} %copy-done, ...), custom_call_target="tpu_custom_call" | custom-call | tf_op jit(solution)/shard_map/pallas_call | solution.py:443
  49.6 4.8 %collective-permute-start.2 = (f32[12,384]{1,0:T(8,128)S(1)}, f32[12,384]{1,0:T(8,128)S(1)}, u32[]{:S(2)}, u32[]{:S(2)}) collective-permute-start(f32[12,384]{1,0:T(8,128)S(1)} %get-tuple-element.23), channel_id=1, source_target_pairs={{0,1},{1,0},{2,3},{3,2},{4,5},{5,4},{6,7},{7,6},{8,9},{9,8},{10,11... | collective-permute-start | bytes 55304 | tf_op jit(solution)/shard_map/ppermute | solution.py:544
  54.4 1.9 %collective-permute-start.3 = (f32[12,384]{1,0:T(8,128)S(1)}, f32[12,384]{1,0:T(8,128)S(1)}, u32[]{:S(2)}, u32[]{:S(2)}) collective-permute-start(f32[12,384]{1,0:T(8,128)S(1)} %get-tuple-element.23), channel_id=1, source_target_pairs={{0,2},{1,3},{2,0},{3,1},{4,6},{5,7},{6,4},{7,5},{8,10},{9,11},{10,... | collective-permute-start | bytes 55304 | tf_op jit(solution)/shard_map/ppermute | solution.py:544
  56.3 1.0 %collective-permute-start.4 = (f32[12,384]{1,0:T(8,128)S(1)}, f32[12,384]{1,0:T(8,128)S(1)}, u32[]{:S(2)}, u32[]{:S(2)}) collective-permute-start(f32[12,384]{1,0:T(8,128)S(1)} %get-tuple-element.23), channel_id=1, source_target_pairs={{0,3},{1,2},{2,1},{3,0},{4,7},{5,6},{6,5},{7,4},{8,11},{9,10},{10,... | collective-permute-start | bytes 55304 | tf_op jit(solution)/shard_map/ppermute | solution.py:544
  57.3 0.0 collective-permute-done.2
  57.3 0.9 %collective-permute-done.3 = f32[12,384]{1,0:T(8,128)S(1)} collective-permute-done((f32[12,384]{1,0:T(8,128)S(1)}, f32[12,384]{1,0:T(8,128)S(1)}, u32[]{:S(2)}, u32[]{:S(2)}) %collective-permute-start.3) | collective-permute-done | bytes 18464 | tf_op jit(solution)/shard_map/ppermute | solution.py:544
  58.2 2.8 %collective-permute-done.4 = f32[12,384]{1,0:T(8,128)S(1)} collective-permute-done((f32[12,384]{1,0:T(8,128)S(1)}, f32[12,384]{1,0:T(8,128)S(1)}, u32[]{:S(2)}, u32[]{:S(2)}) %collective-permute-start.4) | collective-permute-done | bytes 18464 | tf_op jit(solution)/shard_map/ppermute | solution.py:544
  61.0 2.2 %collective-permute-start.5 = (f32[12,384]{1,0:T(8,128)S(1)}, f32[12,384]{1,0:T(8,128)S(1)}, u32[]{:S(2)}, u32[]{:S(2)}) collective-permute-start(f32[12,384]{1,0:T(8,128)S(1)} %add_add_fusion), channel_id=1, source_target_pairs={{0,4},{1,5},{2,6},{3,7},{4,0},{5,1},{6,2},{7,3},{8,12},{9,13},{10,... | collective-permute-start | bytes 55304 | tf_op jit(solution)/shard_map/ppermute | solution.py:544
  63.3 1.5 %collective-permute-start.10 = (f32[6,2,16,128]{3,2,1,0:T(8,128)S(1)}, f32[6,2,16,128]{3,2,1,0:T(8,128)S(1)}, u32[]{:S(2)}, u32[]{:S(2)}) collective-permute-start(f32[6,2,16,128]{3,2,1,0:T(8,128)S(1)} %get-tuple-element.26), channel_id=1, source_target_pairs={{0,16},{8,24},{16,0},{24,8},{1,17},{9,25},{17,1},{25,9},{2,18},{10... | collective-permute-start | bytes 294920 | tf_op jit(solution)/shard_map/ppermute | solution.py:533
  64.8 0.0 collective-permute-start.11
  64.8 0.6 collective-permute-start.9
  65.4 0.5 collective-permute-done.5
  65.9 0.1 collective-permute-start.6
  66.0 1.7 %collective-permute-start.7 = (f32[6,640]{1,0:T(8,128)S(1)}, f32[6,640]{1,0:T(8,128)S(1)}, u32[]{:S(2)}, u32[]{:S(2)}) collective-permute-start(f32[6,640]{1,0:T(8,128)S(1)} %pad_maximum_fusion.refs_0_), channel_id=1, source_target_pairs={{0,16},{8,24},{16,0},{24,8},{1,17},{9,25},{17,1},{25,9},{2,18},{10... | collective-permute-start | bytes 46088 | tf_op jit(solution)/shard_map/ppermute | solution.py:533
  67.7 0.0 collective-permute-done.6.refs_1_
  67.7 0.9 %collective-permute-start.8 = (f32[6,640]{1,0:T(8,128)S(1)}, f32[6,640]{1,0:T(8,128)S(1)}, u32[]{:S(2)}, u32[]{:S(2)}) collective-permute-start(f32[6,640]{1,0:T(8,128)S(1)} %pad_maximum_fusion.refs_0_), channel_id=1, source_target_pairs={{0,24},{8,16},{16,8},{24,0},{1,25},{9,17},{17,9},{25,1},{2,26},{10... | collective-permute-start | bytes 46088 | tf_op jit(solution)/shard_map/ppermute | solution.py:533
  68.5 1.9 %collective-permute-done.7.refs_2_ = f32[6,640]{1,0:T(8,128)S(1)} collective-permute-done((f32[6,640]{1,0:T(8,128)S(1)}, f32[6,640]{1,0:T(8,128)S(1)}, u32[]{:S(2)}, u32[]{:S(2)}) %collective-permute-start.7) | collective-permute-done | bytes 15392 | tf_op jit(solution)/shard_map/ppermute | solution.py:533
  70.4 0.4 collective-permute-done.8.refs_3_
  70.9 0.0 collective-permute-done.10.refs_6_
  70.9 0.0 collective-permute-done.11.refs_7_
  70.9 0.0 collective-permute-done.9.refs_5_
  70.9 1.6 %shard_map.133 = (f32[4,6,2,16,128]{4,3,2,1,0:T(8,128)}, f32[24,384]{1,0:T(8,128)}, f32[6,256]{1,0:T(8,128)}) custom-call(s32[1]{0:T(128)} %bitcast.mem_ref, f32[6,640]{1,0:T(8,128)S(1)} %pad_maximum_fusion.refs_0_, f32[6,640]{1,0:T(8,128)S(1)} %collective-permute-done.6.refs_1_, f32[6,640]{1,0:T(8,128)S(1)} %collective-permute-done.7.refs_2_, ...), custom_call_target="tpu_custom_call" | custom-call | tf_op jit(solution)/shard_map/pallas_call | solution.py:513
  (24 shorter events, 0.1 us)
Async XLA Ops:
  0.6 65.2 %copy-start.8 = (f32[6,256]{1,0:T(8,128)S(1)}, f32[6,256]{1,0:T(8,128)}, u32[]{:S(2)}) copy-start(f32[6,256]{1,0:T(8,128)} %lat_ref.1) | copy-start | bytes 18436
  0.6 11.9 %copy-start.1 = (f32[2,16,512]{2,1,0:T(8,128)S(1)}, f32[2,16,512]{2,1,0:T(8,128)}, u32[]{:S(2)}) copy-start(f32[2,16,512]{2,1,0:T(8,128)} %prev_ref.3) | copy-start | bytes 196612
  0.7 11.9 %copy-start.2 = (f32[2,16,512]{2,1,0:T(8,128)S(1)}, f32[2,16,512]{2,1,0:T(8,128)}, u32[]{:S(2)}) copy-start(f32[2,16,512]{2,1,0:T(8,128)} %src_ref.3) | copy-start | bytes 196612
  0.7 9.6 %copy-start.9 = (s32[384]{0:T(512)S(1)}, s32[384]{0:T(512)}, u32[]{:S(2)}) copy-start(s32[384]{0:T(512)} %param.19) | copy-start | bytes 4612
  0.7 9.6 %copy-start.7 = (bf16[64]{0:T(256)(128)(2,1)S(1)}, bf16[64]{0:T(256)(128)(2,1)}, u32[]{:S(2)}) copy-start(bf16[64]{0:T(256)(128)(2,1)} %param.15) | copy-start | bytes 388
  0.7 9.6 %copy-start.6 = (bf16[9,64]{1,0:T(8,128)(2,1)S(1)}, bf16[9,64]{1,0:T(8,128)(2,1)}, u32[]{:S(2)}) copy-start(bf16[9,64]{1,0:T(8,128)(2,1)} %in_ref.1) | copy-start | bytes 3460
  0.7 9.6 %copy-start.5 = (bf16[9,64,64]{2,1,0:T(8,128)(2,1)S(1)}, bf16[9,64,64]{2,1,0:T(8,128)(2,1)}, u32[]{:S(2)}) copy-start(bf16[9,64,64]{2,1,0:T(8,128)(2,1)} %mid_ref.1) | copy-start | bytes 221188
  0.7 11.9 %copy-start.4 = (s32[384,8]{0,1:T(8,128)S(1)}, s32[384,8]{0,1:T(8,128)}, u32[]{:S(2)}) copy-start(s32[384,8]{0,1:T(8,128)} %param.18) | copy-start | bytes 36868
  0.7 67.8 %copy-start.10 = (f32[384]{0:T(512)S(1)}, f32[384]{0:T(512)}, u32[]{:S(2)}) copy-start(f32[384]{0:T(512)} %param.21) | copy-start | bytes 4612
  0.7 70.2 %copy-start.3 = (f32[24,384]{1,0:T(8,128)S(1)}, f32[24,384]{1,0:T(8,128)}, u32[]{:S(2)}) copy-start(f32[24,384]{1,0:T(8,128)} %refs_8_.1) | copy-start | bytes 110596
  6.5 6.0 %collective-permute-start = (bf16[96,512]{1,0:T(8,128)(2,1)}, bf16[96,512]{1,0:T(8,128)(2,1)S(1)}, u32[]{:S(2)}, u32[]{:S(2)}) collective-permute-start(bf16[96,512]{1,0:T(8,128)(2,1)} %get-tuple-element.18), channel_id=1, source_target_pairs={{0,1},{1,0},{2,3},{3,2},{4,5},{5,4},{6,7},{7,6},{8,9},{9,8},{10,11... | collective-permute-start | bytes 294920 | tf_op jit(solution)/shard_map/ppermute | solution.py:553
  9.6 3.0 %collective-permute-start.1 = (bf16[96,512]{1,0:T(8,128)(2,1)}, bf16[96,512]{1,0:T(8,128)(2,1)S(1)}, u32[]{:S(2)}, u32[]{:S(2)}) collective-permute-start(bf16[96,512]{1,0:T(8,128)(2,1)} %get-tuple-element.19), channel_id=1, source_target_pairs={{1,2},{2,1},{3,4},{4,3},{5,6},{6,5},{9,10},{10,9},{11,12},{12,11},... | collective-permute-start | bytes 294920 | tf_op jit(solution)/shard_map/ppermute | solution.py:552
  12.6 1.0 %copy-start = (f32[2,6,16,512]{3,2,1,0:T(8,128)S(1)}, f32[2,6,16,512]{3,2,1,0:T(8,128)}, u32[]{:S(2)}) copy-start(f32[2,6,16,512]{3,2,1,0:T(8,128)} %get-tuple-element.17.field_ref) | copy-start | bytes 1179652
  49.6 7.7 %collective-permute-start.2 = (f32[12,384]{1,0:T(8,128)S(1)}, f32[12,384]{1,0:T(8,128)S(1)}, u32[]{:S(2)}, u32[]{:S(2)}) collective-permute-start(f32[12,384]{1,0:T(8,128)S(1)} %get-tuple-element.23), channel_id=1, source_target_pairs={{0,1},{1,0},{2,3},{3,2},{4,5},{5,4},{6,7},{7,6},{8,9},{9,8},{10,11... | collective-permute-start | bytes 55304 | tf_op jit(solution)/shard_map/ppermute | solution.py:544
  54.4 3.9 %collective-permute-start.3 = (f32[12,384]{1,0:T(8,128)S(1)}, f32[12,384]{1,0:T(8,128)S(1)}, u32[]{:S(2)}, u32[]{:S(2)}) collective-permute-start(f32[12,384]{1,0:T(8,128)S(1)} %get-tuple-element.23), channel_id=1, source_target_pairs={{0,2},{1,3},{2,0},{3,1},{4,6},{5,7},{6,4},{7,5},{8,10},{9,11},{10,... | collective-permute-start | bytes 55304 | tf_op jit(solution)/shard_map/ppermute | solution.py:544
  56.3 4.7 %collective-permute-start.4 = (f32[12,384]{1,0:T(8,128)S(1)}, f32[12,384]{1,0:T(8,128)S(1)}, u32[]{:S(2)}, u32[]{:S(2)}) collective-permute-start(f32[12,384]{1,0:T(8,128)S(1)} %get-tuple-element.23), channel_id=1, source_target_pairs={{0,3},{1,2},{2,1},{3,0},{4,7},{5,6},{6,5},{7,4},{8,11},{9,10},{10,... | collective-permute-start | bytes 55304 | tf_op jit(solution)/shard_map/ppermute | solution.py:544
  61.0 4.8 %collective-permute-start.5 = (f32[12,384]{1,0:T(8,128)S(1)}, f32[12,384]{1,0:T(8,128)S(1)}, u32[]{:S(2)}, u32[]{:S(2)}) collective-permute-start(f32[12,384]{1,0:T(8,128)S(1)} %add_add_fusion), channel_id=1, source_target_pairs={{0,4},{1,5},{2,6},{3,7},{4,0},{5,1},{6,2},{7,3},{8,12},{9,13},{10,... | collective-permute-start | bytes 55304 | tf_op jit(solution)/shard_map/ppermute | solution.py:544
  63.3 7.6 %collective-permute-start.10 = (f32[6,2,16,128]{3,2,1,0:T(8,128)S(1)}, f32[6,2,16,128]{3,2,1,0:T(8,128)S(1)}, u32[]{:S(2)}, u32[]{:S(2)}) collective-permute-start(f32[6,2,16,128]{3,2,1,0:T(8,128)S(1)} %get-tuple-element.26), channel_id=1, source_target_pairs={{0,16},{8,24},{16,0},{24,8},{1,17},{9,25},{17,1},{25,9},{2,18},{10... | collective-permute-start | bytes 294920 | tf_op jit(solution)/shard_map/ppermute | solution.py:533
  64.8 6.1 %collective-permute-start.11 = (f32[6,2,16,128]{3,2,1,0:T(8,128)S(1)}, f32[6,2,16,128]{3,2,1,0:T(8,128)S(1)}, u32[]{:S(2)}, u32[]{:S(2)}) collective-permute-start(f32[6,2,16,128]{3,2,1,0:T(8,128)S(1)} %get-tuple-element.27), channel_id=1, source_target_pairs={{0,24},{8,16},{16,8},{24,0},{1,25},{9,17},{17,9},{25,1},{2,26},{10... | collective-permute-start | bytes 294920 | tf_op jit(solution)/shard_map/ppermute | solution.py:533
  64.8 6.1 %collective-permute-start.9 = (f32[6,2,16,128]{3,2,1,0:T(8,128)S(1)}, f32[6,2,16,128]{3,2,1,0:T(8,128)S(1)}, u32[]{:S(2)}, u32[]{:S(2)}) collective-permute-start(f32[6,2,16,128]{3,2,1,0:T(8,128)S(1)} %get-tuple-element.25), channel_id=1, source_target_pairs={{0,8},{8,0},{16,24},{24,16},{1,9},{9,1},{17,25},{25,17},{2,10},{10... | collective-permute-start | bytes 294920 | tf_op jit(solution)/shard_map/ppermute | solution.py:533
  65.9 1.8 %collective-permute-start.6 = (f32[6,640]{1,0:T(8,128)S(1)}, f32[6,640]{1,0:T(8,128)S(1)}, u32[]{:S(2)}, u32[]{:S(2)}) collective-permute-start(f32[6,640]{1,0:T(8,128)S(1)} %pad_maximum_fusion.refs_0_), channel_id=1, source_target_pairs={{0,8},{8,0},{16,24},{24,16},{1,9},{9,1},{17,25},{25,17},{2,10},{10... | collective-permute-start | bytes 46088 | tf_op jit(solution)/shard_map/ppermute | solution.py:533
  66.0 4.4 %collective-permute-start.7 = (f32[6,640]{1,0:T(8,128)S(1)}, f32[6,640]{1,0:T(8,128)S(1)}, u32[]{:S(2)}, u32[]{:S(2)}) collective-permute-start(f32[6,640]{1,0:T(8,128)S(1)} %pad_maximum_fusion.refs_0_), channel_id=1, source_target_pairs={{0,16},{8,24},{16,0},{24,8},{1,17},{9,25},{17,1},{25,9},{2,18},{10... | collective-permute-start | bytes 46088 | tf_op jit(solution)/shard_map/ppermute | solution.py:533
  67.7 3.2 %collective-permute-start.8 = (f32[6,640]{1,0:T(8,128)S(1)}, f32[6,640]{1,0:T(8,128)S(1)}, u32[]{:S(2)}, u32[]{:S(2)}) collective-permute-start(f32[6,640]{1,0:T(8,128)S(1)} %pad_maximum_fusion.refs_0_), channel_id=1, source_target_pairs={{0,24},{8,16},{16,8},{24,0},{1,25},{9,17},{17,9},{25,1},{2,26},{10... | collective-permute-start | bytes 46088 | tf_op jit(solution)/shard_map/ppermute | solution.py:533

commit v4 on v3

--- a/solution.py
+++ b/solution.py
@@ -13,9 +13,10 @@
 HALO = 4
 RING = 24
 LIFT_BLOCKS = 11
-HELD = 5
+INNER = (3, 8)
+FIRST = ((4, 0), (5, 1), (6, 2))
+ORDER = ((5, 7, 3), (6, 3, 4), (4, 8, 5), (7, 2, 1), (3, 9, 2), (8, 1, 0), (2, 10, 3), (9, 0, 4), (1, None, None), (10, None, None))
 MIX_BLOCKS = 10
-CHUNK_GROUPS = 12
 SEG = 16
 BF = jnp.bfloat16
 F32 = jnp.float32
@@ -34,7 +35,10 @@
     taps = dot(taps, one(iota((64, 256), 0) == iota((64, 256), 1) & 63))
     kinds = jnp.where(iota((64, 256), 0) >> 4 == iota((64, 256), 1) >> 6, taps, 0.0).astype(BF)
     k, j = iota((256, 64), 0), iota((256, 64), 1)
-    offset, ring = k >> 6, k & 31
+    lane = k & 127
+    own = lane < 64
+    offset = 2 * (k >> 7) + jnp.where(own, lane >> 5, ((lane - 64) >> 4) & 1)
+    ring = jnp.where(own, lane & 15, jnp.where(lane < 96, 16 + (lane & 7), 2 * RING))
     place, tap = j >> 4, j & 15
     xx, yy = place >> 1, place & 1
     a = ((tap * 11) >> 5) - 1
@@ -72,37 +76,132 @@
     gain_ref[8:16] = dot(gains, one(c == 32 + (n & 31)))
 
 
-def place_kernel(grid_rows, rows, tile_ref, in_ref, mid_ref, out_ref, win_ref, wmix_ref, gain_ref):
+def shifted(f):
+    hi = f.astype(BF).astype(F32)
+    lo = f - hi
+    edge = iota(f.shape, 1) == 0
+    return [jnp.where(edge, 0.0, pltpu.roll(v, 1, 1)) for v in (hi, lo)] + [hi, lo]
+
+
+def turned(parts, span, scr):
+    width = parts[0].shape[1]
+    tall = jnp.concatenate(parts, axis=0).T
+    scr[0:width, :] = tall
+    end = pltpu.roll(tall[width - 8 : width], 128 - span // 2, 1)
+    end = jnp.where(iota(end.shape, 1) & (span - 1) < span // 2, end, 0.0)
+    scr[width : width + 8, :] = pltpu.roll(end, 1, 0)
+
+
+def lift_block(pt, win, put_lift, put_side):
+    total = pt.shape[0]
+    wide = jnp.maximum(jnp.dot(pt, win, preferred_element_type=F32), 0.0)
+    put_lift(wide.astype(BF))
+    right = iota((SEG, 256), 1) & 64 == 0
+    row = iota((SEG, 256), 0)
+    steps = SEG
+    for base in range(0, total, steps * SEG):
+        last = base + (steps - 1) * SEG
+        after = jnp.where(row < SEG - 1, pltpu.roll(wide[base : base + SEG], SEG - 1, 0), 0.0)
+        before = jnp.where(row > 0, pltpu.roll(wide[last : last + SEG], 1, 0), 0.0)
+        for q in range(steps):
+            r = base + q * SEG
+            nxt = after if q == steps - 1 else wide[r + SEG : r + 2 * SEG]
+            prv = before if q == 0 else wide[r - SEG : r]
+            put_side(r, jnp.where(right, nxt, prv).astype(BF))
+
+
+def lift_to(pt_ref, win, lift_ref, side_ref, slot):
+    def put_lift(v):
+        lift_ref[slot] = v
+
+    def put_side(r, v):
+        side_ref[slot, r : r + SEG, :] = v
+
+    lift_block(pt_ref[...], win, put_lift, put_side)
+
+
+def early_kernel(
+    grid_rows,
+    tile_ref,
+    field_hbm,
+    in_ref,
+    mid_ref,
+    out_ref,
+    field_ref,
+    win_ref,
+    wmix_ref,
+    gain_ref,
+    pt_ref,
+    t_scr,
+    sem,
+):
+    layers, members, rows, width = field_ref.shape
+    groups = layers * members
+    steps = width // (2 * SEG)
+    block_rows = width // 2
+    copy = pltpu.make_async_copy(field_hbm, field_ref, sem)
+    copy.start()
     place_weights(tile_ref[0], grid_rows, rows, in_ref, mid_ref, out_ref, win_ref, wmix_ref, gain_ref)
-
-
-def placed(tile_vec, grid_rows, rows, conv_in, conv_mid, conv_out):
+    copy.wait()
+
+    def load(pair, _):
+        parts = []
+        for half in range(2):
+            group = 2 * pair + half
+            parts += shifted(field_ref[group // members, lax.rem(group, members)])
+        turned(parts, 4 * rows, t_scr)
+        mine = iota((SEG, 128), 1) < 4 * rows
+        for q in range(steps + 1):
+            part = t_scr[pl.ds(2 * q, SEG, stride=2 * steps), :]
+            for half in range(2):
+                v = jnp.where(mine, part if half == 0 else pltpu.roll(part, 64, 1), 0.0).astype(BF)
+                at = (2 * pair + half) * block_rows + q * SEG
+                if q < steps:
+                    pt_ref[pl.ds(pl.multiple_of(at, SEG), SEG), 0:128] = v
+                if q > 0:
+                    pt_ref[pl.ds(pl.multiple_of(at - SEG, SEG), SEG), 128:256] = v
+        return 0
+
+    lax.fori_loop(0, groups // 2, load, 0)
+
+
+def early(tile_vec, grid_rows, field, conv_in, conv_mid, conv_out):
+    layers, members, rows, width = field.shape
+    total = layers * members * width // 2
     return pl.pallas_call(
-        functools.partial(place_kernel, grid_rows, rows),
-        in_specs=[SMEM] + [VMEM] * 3,
-        out_specs=[VMEM] * 3,
+        functools.partial(early_kernel, grid_rows),
+        in_specs=[SMEM, pl.BlockSpec(memory_space=pltpu.HBM)] + [VMEM] * 3,
+        out_specs=[VMEM] * 5,
         out_shape=[
+            jax.ShapeDtypeStruct(field.shape, F32),
             jax.ShapeDtypeStruct((LIFT_BLOCKS, 256, 256), BF),
             jax.ShapeDtypeStruct((1024, 256), BF),
             jax.ShapeDtypeStruct((16, 128), F32),
+            jax.ShapeDtypeStruct((total, 256), BF),
         ],
-        compiler_params=pltpu.CompilerParams(vmem_limit_bytes=24 * 2**20),
+        scratch_shapes=[pltpu.VMEM((width + 8, 128), F32), pltpu.SemaphoreType.DMA],
+        compiler_params=pltpu.CompilerParams(vmem_limit_bytes=16 * 2**20),
         cost_estimate=pl.CostEstimate(flops=900_000_000, bytes_accessed=3_000_000, transcendentals=0),
-    )(tile_vec, conv_in, conv_mid, conv_out)
-
-
-def field_kernel(tile_ref, lat_ref, basis_ref, prev_ref, src_ref, field_ref, near_ref, far_ref, held, sems):
+    )(tile_vec, field, conv_in, conv_mid, conv_out)
+
+
+def field_kernel(tile_ref, lat_hbm, basis_ref, prev_hbm, src_hbm, field_ref, near_ref, far_ref, held, lat_ref, prev_ref, src_ref, sems):
     chunks, comps, layers, rows, width = held.shape
     members, total = lat_ref.shape
     span = comps * rows
     copies = [
         pltpu.make_async_copy(basis_ref.at[pl.ds(c * comps, comps)], held.at[c], sems.at[c]) for c in range(chunks)
     ]
-    for copy in copies:
+    small = [
+        pltpu.make_async_copy(a, b, sems.at[chunks + i])
+        for i, (a, b) in enumerate(((lat_hbm, lat_ref), (prev_hbm, prev_ref), (src_hbm, src_ref)))
+    ]
+    for copy in small[:1] + copies + small[1:]:
         copy.start()
     even_tile = tile_ref[0] & 1 == 0
     shape = (PACKED, 2 * (layers * members + 2 * layers) * rows)
     picks = [packed_from(layers, members, rows, up, shape) for up in (even_tile, jnp.logical_not(even_tile))]
+    small[0].wait()
     lat = lat_ref[...].astype(BF)
     own = iota((rows, span), 0) == iota((rows, span), 1) & (rows - 1)
     behind = iota((total, span), 0) - split(iota((total, span), 1), rows)[0]
@@ -115,6 +214,8 @@
             part = jnp.dot(left, held[c, :, z].reshape(span, width), preferred_element_type=F32)
             part = part.reshape(members, rows, width)
             field_ref[z] = part if c == 0 else field_ref[z] + part
+    small[1].wait()
+    small[2].wait()
     exact, rest = [], []
     for value in (field_ref[...].reshape(-1, width), prev_ref[...].reshape(-1, width), src_ref[...].reshape(-1, width)):
         hi = value.astype(BF)
@@ -171,7 +272,7 @@
     comps = 32
     return pl.pallas_call(
         field_kernel,
-        in_specs=[SMEM, VMEM, pl.BlockSpec(memory_space=pltpu.HBM), VMEM, VMEM],
+        in_specs=[SMEM] + [pl.BlockSpec(memory_space=pltpu.HBM)] * 4,
         out_specs=[VMEM] * 3,
         out_shape=[
             jax.ShapeDtypeStruct((layers, members, rows, width), F32),
@@ -180,7 +281,10 @@
         ],
         scratch_shapes=[
             pltpu.VMEM((total // comps, comps, layers, rows, width), BF),
-            pltpu.SemaphoreType.DMA((total // comps,)),
+            pltpu.VMEM(latents.shape, F32),
+            pltpu.VMEM(prev.shape, F32),
+            pltpu.VMEM(src.shape, F32),
+            pltpu.SemaphoreType.DMA((total // comps + 3,)),
         ],
         compiler_params=pltpu.CompilerParams(vmem_limit_bytes=57 * 2**20),
     )(tile_vec, latents, basis, prev, src)
@@ -212,6 +316,7 @@
     win_ref,
     wmix_ref,
     gain_ref,
+    early_pt_ref,
     ids_ref,
     count_ref,
     *refs,
@@ -235,103 +340,75 @@
         + jnp.dot(from_far, far_ref[...], preferred_element_type=F32)
     ).reshape(-1, 8, width)
 
-    def load(pair, _):
-        for half in range(2):
-            group = 2 * pair + half
-            own = field_ref[group // members, lax.rem(group, members)]
-            f = jnp.concatenate([own, third_scr[group]], axis=0)
-            f_scr[group] = f
-            hi = f.astype(BF).astype(F32)
-            lo = f - hi
-            zero = jnp.zeros((32 - RING, width), F32)
-            edge = iota((RING, width), 1) == 0
-            hi_left = jnp.where(edge, 0.0, pltpu.roll(hi, 1, 1))
-            lo_left = jnp.where(edge, 0.0, pltpu.roll(lo, 1, 1))
-            tall = jnp.concatenate([hi_left, zero, lo_left, zero, hi, zero, lo, zero], axis=0).T
-            t_scr[half, 0:width, :] = tall
-            end = pltpu.roll(tall[width - 8 : width], 64, 1)
-            end = jnp.where(iota(end.shape, 1) < 64, end, 0.0)
-            t_scr[half, width : width + 8, :] = pltpu.roll(end, 1, 0)
-            for q in range(steps + 1):
-                part = t_scr[half, pl.ds(2 * q, SEG, stride=2 * steps), :].astype(BF)
+    def load(quad):
+        parts = []
+        for j in range(4):
+            parts += shifted(third_scr[4 * quad + j])
+        turned(parts, 32, t_scr.at[quad])
+        lane = iota((SEG, 128), 1)
+        mine = (lane >= 64) & (lane < 96)
+        for q in range(steps + 1):
+            part = t_scr[quad, pl.ds(2 * q, SEG, stride=2 * steps), :]
+            for j in range(4):
+                v = part if j == 2 else pltpu.roll(part, (64 - 32 * j) % 128, 1)
+                v = jnp.where(mine, v, 0.0).astype(BF)
+                at = (4 * quad + j) * block_rows + q * SEG
                 if q < steps:
-                    pt_scr[pl.ds(pl.multiple_of(group * block_rows + q * SEG, SEG), SEG), 0:128] = part
+                    rows_at = pl.ds(pl.multiple_of(at, SEG), SEG)
+                    pt_scr[rows_at, 0:128] = early_pt_ref[rows_at, 0:128] + v
                 if q > 0:
-                    pt_scr[pl.ds(pl.multiple_of(group * block_rows + (q - 1) * SEG, SEG), SEG), 128:256] = part
-        return 0
-
-    lax.fori_loop(0, groups // 2, load, 0)
-
-    chunk = CHUNK_GROUPS * block_rows
-    chunks = groups * block_rows // chunk
-
-    def slot_of(block):
-        return jnp.where(block == 0, 0, 1 + lax.rem(block + HELD - 1, HELD))
-
-    def lift(t, _):
-        block, part = t // chunks, lax.rem(t, chunks)
-        slot = slot_of(block)
-        at = pl.multiple_of(part * chunk, chunk)
-        wide = jnp.dot(pt_scr[pl.ds(at, chunk), :], win_ref[block], preferred_element_type=F32)
-        wide = jnp.maximum(wide, 0.0)
-        tight = wide.astype(BF)
-        lift_scr[slot, pl.ds(at, chunk), :] = tight
-        right = iota((SEG, 256), 1) & 64 == 0
-        row = iota((SEG, 256), 0)
-        for i in range(chunk // block_rows):
-            base = i * block_rows
-            last = base + block_rows - SEG
-            after = jnp.where(row < SEG - 1, pltpu.roll(wide[base : base + SEG], SEG - 1, 0), 0.0)
-            before = jnp.where(row > 0, pltpu.roll(wide[last : last + SEG], 1, 0), 0.0)
-            for q in range(steps):
-                r = base + q * SEG
-                nxt = after if q == steps - 1 else wide[r + SEG : r + 2 * SEG]
-                prv = before if q == 0 else wide[r - SEG : r]
-                side_scr[slot, pl.ds(pl.multiple_of(at + r, SEG), SEG), :] = jnp.where(right, nxt, prv).astype(BF)
-        return 0
-
+                    rows_at = pl.ds(pl.multiple_of(at - SEG, SEG), SEG)
+                    pt_scr[rows_at, 128:256] = early_pt_ref[rows_at, 128:256] + v
 
     gain0, gain1 = gain_ref[0:1, :], gain_ref[8:9, :]
 
-    def mix(t, _):
-        block, part = t // chunks + 1, lax.rem(t, chunks)
-        above = slot_of(block - 1)
-        below = slot_of(jnp.where(block == LIFT_BLOCKS - 1, 0, block + 1))
-        here = slot_of(block)
-        at = pl.ds(pl.multiple_of(part * chunk, chunk), chunk)
+    places = {}
+
+    begun = set()
+
+    def mix(block, here, above, below):
         x = jnp.concatenate(
             [
-                lift_scr[here, at, :],
-                side_scr[here, at, :],
-                lift_scr[below, at, 0:128],
-                lift_scr[above, at, 128:256],
-                side_scr[below, at, 0:128],
-                side_scr[above, at, 128:256],
+                here[0][here[2]],
+                here[1][here[2]],
+                below[0][below[2], :, 0:128],
+                above[0][above[2], :, 128:256],
+                below[1][below[2], :, 0:128],
+                above[1][above[2], :, 128:256],
             ],
             axis=1,
         )
         deep = jnp.maximum(jnp.dot(x, wmix_ref[...], preferred_element_type=F32), 0.0)
-        deep_scr[block - 1, at, :] = (deep[:, :128] * gain0 + deep[:, 128:] * gain1).astype(BF)
-        return 0
-
-    def both_steps(t, _):
-        mix(t, 0)
-        lift(t + 3 * chunks, 0)
-        return 0
-
-    lax.fori_loop(0, 3 * chunks, lift, 0)
-    lax.fori_loop(0, (LIFT_BLOCKS - 3) * chunks, both_steps, 0)
-    lax.fori_loop((LIFT_BLOCKS - 3) * chunks, MIX_BLOCKS * chunks, mix, 0)
+        deep = deep[:, :128] * gain0 + deep[:, 128:] * gain1
+        place, part = divmod(block - 1, 4)
+        deep = deep + pltpu.roll(deep, 16 if part & 2 else 112, 1)
+        deep = deep + pltpu.roll(deep, 8 if part & 1 else 120, 1)
+        deep = jnp.where((iota(deep.shape, 1) & 31) >> 3 == part, deep, 0.0).astype(BF)
+        deep_scr[place] = deep if place not in begun else deep_scr[place] + deep
+        begun.add(place)
+
+    def lift(block, slot):
+        lift_to(early_pt_ref if INNER[0] <= block <= INNER[1] else pt_scr, win_ref[block], lift_scr, side_scr, slot)
+        places[block] = (lift_scr, side_scr, slot)
+
+    for block, slot in FIRST:
+        lift(block, slot)
+    for step, (block, lifted, slot) in enumerate(ORDER):
+        mix(block, places[block], places[block - 1], places[(block + 1) % LIFT_BLOCKS])
+        if step < groups // 4:
+            load(step)
+        if lifted is not None:
+            lift(lifted, slot)
 
     k, n = iota(wout_scr.shape, 0), iota(wout_scr.shape, 1)
     place = (k & 127) >> 5
-    row = 2 * ((k >> 7) + 1) - HALO + (place >> 1)
+    row = 2 * (4 * (k >> 7) + ((k & 31) >> 3) + 1) - HALO + (place >> 1)
     row = jnp.where(row < 0, row + RING, row)
     wout_scr[...] = jnp.where(n == (place & 1) * 32 + row, 1.0, 0.0).astype(BF)
 
     def collect(pair, held):
         at = pl.ds(pl.multiple_of(pair * 2 * block_rows, 2 * block_rows), 2 * block_rows)
-        x = jnp.concatenate([deep_scr[j, at, :] for j in range(MIX_BLOCKS)], axis=1)
+        x = jnp.concatenate([deep_scr[j, at, :] for j in range(deep_scr.shape[0])], axis=1)
         both = jnp.dot(x, wout_scr[...], preferred_element_type=F32)
         both = both[:block_rows] + pltpu.roll(both[block_rows:], 64, 1)
         for q in range(steps):
@@ -342,12 +419,14 @@
         even = iota((RING, width), 1) & 1 == 0
         for half in range(2):
             s = 64 * half
-            f_scr[2 * pair + half] = f_scr[2 * pair + half] + jnp.where(
+            group = 2 * pair + half
+            f = jnp.concatenate([field_ref[group // members, group % members], third_scr[group]], axis=0)
+            f_scr[group] = f + jnp.where(
                 even, flat[s : s + RING], flat[s + 32 : s + 32 + RING]
             )
 
     for pair in range(groups // 2):
-        collect(pair, pair)
+        collect(pair, pair % (groups // 4))
 
     full = (RING, width)
     ring = iota(full, 0)
@@ -435,31 +514,31 @@
     sums_ref[members : 2 * members] = sums[2 * members : 3 * members] + sums[3 * members :]
 
 
-def decode(parts, tile_vec, mem_vec, grid_rows, field, near, far, prev, src, win, wmix, gains, ids, counts):
+def decode(parts, tile_vec, mem_vec, grid_rows, field, near, far, prev, src, weights, ids, counts):
     layers, members, rows, width = field.shape
     groups = layers * members
     total = groups * width // 2
     wells = ids.shape[1]
     return pl.pallas_call(
         functools.partial(decode_kernel, grid_rows),
-        in_specs=[SMEM] * 2 + [VMEM] * 10,
+        in_specs=[SMEM] * 2 + [VMEM] * 11,
         out_specs=[VMEM] * (parts + 1),
         out_shape=[jax.ShapeDtypeStruct((members, layers, rows, width // parts), F32)] * parts
         + [jax.ShapeDtypeStruct((2 * members, wells), F32)],
         scratch_shapes=[
             pltpu.VMEM((groups, RING, width), F32),
-            pltpu.VMEM((groups // 2, width + 8, 128), F32),
+            pltpu.VMEM((groups // 4, width + 8, 128), F32),
             pltpu.VMEM((total, 256), BF),
-            pltpu.VMEM((HELD + 1, total, 256), BF),
-            pltpu.VMEM((HELD + 1, total, 256), BF),
-            pltpu.VMEM((MIX_BLOCKS, total, 128), BF),
-            pltpu.VMEM((MIX_BLOCKS * 128, 128), BF),
+            pltpu.VMEM((1 + max(o[2] for o in ORDER if o[2] is not None), total, 256), BF),
+            pltpu.VMEM((1 + max(o[2] for o in ORDER if o[2] is not None), total, 256), BF),
+            pltpu.VMEM((-(-MIX_BLOCKS // 4), total, 128), BF),
+            pltpu.VMEM((-(-MIX_BLOCKS // 4) * 128, 128), BF),
             pltpu.VMEM((4 * groups * rows, width), BF),
             pltpu.VMEM((rows, width), F32),
             pltpu.VMEM((groups + 2 * layers, 8, width), F32),
         ],
-        compiler_params=pltpu.CompilerParams(vmem_limit_bytes=40 * 2**20),
-    )(tile_vec, mem_vec, field, near, far, prev, src, win, wmix, gains, ids, counts)
+        compiler_params=pltpu.CompilerParams(vmem_limit_bytes=43 * 2**20),
+    )(tile_vec, mem_vec, field, near, far, prev, src, *weights, ids, counts)
 
 
 def update_kernel(mem_ref, refs, swap_refs, obs_ref, err_ref, press_ref, data_ref, new_ref, all_scr, step_scr):
@@ -576,10 +655,10 @@
 
     field, near, far = field_of(tile_vec, latents, basis, pressure_prev, source)
     near, far = halo(near, far, "tile")
-    win, wmix, gains = placed(tile_vec, grid_rows, rows, conv_in, conv_mid, conv_out.reshape(1, -1))
+    field, *weights = early(tile_vec, grid_rows, field, conv_in, conv_mid, conv_out.reshape(1, -1))
     *press, sums = decode(
         parts, tile_vec, mem_vec, grid_rows, field, near, far, pressure_prev, source,
-        win, wmix, gains, perf_cells.T, perf_count.reshape(1, -1),
+        weights, perf_cells.T, perf_count.reshape(1, -1),
     )
     swaps = gathered(press, "mem")
     sums = summed(sums, "tile")

time: 72.6 us -> 66.5 us (0.916)
  Pallas kernels: 44.4 us -> 40.3 us
  starting transfers between devices: 18.4 us -> 15.3 us
  waiting for transfers between devices: 7.69 us -> 8.78 us
    pallas_call x1, Pallas kernels: 36 us -> 30.1 us  [decode(): pl.pallas_call(functools.partial(decode_kernel, grid_rows), in_specs=[SME...]
    ppermute x4, starting transfers between devices: 9.94 us -> 7 us  [summed(): lax.ppermute(own, axis, [(i, i ^ j) for i in range(count)])]
    ppermute x4, waiting for transfers between devices: 4.2 us -> 6.44 us  [summed(): lax.ppermute(own, axis, [(i, i ^ j) for i in range(count)])]
    pallas_call x2, Pallas kernels: 6.91 us -> 8.63 us  [the longest x1 4.97 us: field_of(): pl.pallas_call(field_kernel, in_specs=[SMEM] + [pl.BlockSpec(memory_space...]
    ppermute x1, waiting for transfers between devices: 1.15 us -> 0.01 us  [halo(): return (lax.ppermute(near, axis, swap(0)), far)]
  transfers between devices with their start and end apart: 12 -> 12, of which waited for: 6 -> 6; matrix products, arithmetic and copies ran while one was open for 0% -> 0% of each run, Pallas kernels for 2% -> 6%
where the time goes in v4:
time: 66.5 us; the launch traced here: 66.4 us
  Pallas kernels  40.3 us (61%)
  starting transfers between devices  15.3 us (23%)
  waiting for transfers between devices  8.78 us (13%)
  local copies, waits for them, and re-layouts  1.04 us (2%)
  between operations  0.87 us (1%)
    pallas_call x1, Pallas kernels, decode(): pl.pallas_call(functools.partial(decode_kernel, grid_rows), in_specs=[SME...  30.1 us
    ppermute x4, starting transfers between devices, summed(): lax.ppermute(own, axis, [(i, i ^ j) for i in range(count)])  7 us
    ppermute x4, waiting for transfers between devices, summed(): lax.ppermute(own, axis, [(i, i ^ j) for i in range(count)])  6.44 us
    pallas_call x1, Pallas kernels, field_of(): pl.pallas_call(field_kernel, in_specs=[SMEM] + [pl.BlockSpec(memory_space...  4.97 us
    ppermute x6, starting transfers between devices, gathered(): lax.ppermute(pieces[k], axis, [(i, target(i, k, count)) for i in range(co...  4.63 us
    pallas_call x1, Pallas kernels, early(): pl.pallas_call(functools.partial(early_kernel, grid_rows), in_specs=[SMEM...  3.66 us
    ppermute x1, starting transfers between devices, halo(): return (lax.ppermute(near, axis, swap(0)), far)  3.03 us
    ppermute x6, waiting for transfers between devices, gathered(): lax.ppermute(pieces[k], axis, [(i, target(i, k, count)) for i in range(co...  2.34 us
  transfers between devices with their start and end apart: 12, of which 6 were waited for; matrix products, arithmetic and copies ran while one was open for 0% of the time, Pallas kernels for 6%

profile of v4, /device:TPU:0, one launch (start us, length us, event | category | flops | bytes accessed | tf_op | source)
XLA Modules:
  0.0 66.4 jit_solution(4091605419059489482)
XLA Ops:
  0.7 5.0 %shard_map.130 = (f32[2,6,16,512]{3,2,1,0:T(8,128)}, bf16[96,512]{1,0:T(8,128)(2,1)}, bf16[96,512]{1,0:T(8,128)(2,1)}) custom-call(s32[1]{0:T(128)} %bitcast.1.tile_ref, f32[6,256]{1,0:T(8,128)} %lat_hbm.1, bf16[256,2,16,512]{3,2,1,0:T(8,128)(2,1)} %basis_ref.1, f32[2,16,512]{2,1,0:T(8,128)} %prev_ref.1, f32[2,16,512]{2,1,0:T(8,128)} %src_ref.1), custom_call_target="tpu_custom_call" | custom-call | tf_op jit(solution)/shard_map/pallas_call | solution.py:273
  5.7 3.0 %collective-permute-start = (bf16[96,512]{1,0:T(8,128)(2,1)}, bf16[96,512]{1,0:T(8,128)(2,1)S(1)}, u32[]{:S(2)}, u32[]{:S(2)}) collective-permute-start(bf16[96,512]{1,0:T(8,128)(2,1)} %get-tuple-element.21), channel_id=1, source_target_pairs={{0,1},{1,0},{2,3},{3,2},{4,5},{5,4},{6,7},{7,6},{8,9},{9,8},{10,11... | collective-permute-start | bytes 294920 | tf_op jit(solution)/shard_map/ppermute | solution.py:632
  8.7 0.7 collective-permute-start.1
  9.4 0.0 copy-start.4
  9.4 1.0 %copy-done.4 = f32[2,6,16,512]{3,2,1,0:T(8,128)S(1)} copy-done((f32[2,6,16,512]{3,2,1,0:T(8,128)S(1)}, f32[2,6,16,512]{3,2,1,0:T(8,128)}, u32[]{:S(2)}) %copy-start.4) | copy-done | bytes 393240
  10.4 3.7 %shard_map.131 = (f32[2,6,16,512]{3,2,1,0:T(8,128)S(1)}, bf16[11,256,256]{2,1,0:T(8,128)(2,1)S(1)}, bf16[1024,256]{1,0:T(8,128)(2,1)S(1)}, f32[16,128]{1,0:T(8,128)S(1)}, bf16[3072,256]{1,0:T(8,128)(2,1)S(1)}) custom-call(s32[1]{0:T(128)} %bitcast.1.tile_ref, f32[2,6,16,512]{3,2,1,0:T(8,128)S(1)} %copy-done.4, bf16[9,64]{1,0:T(8,128)(2,1)S(1)} %copy-done.6, ...), custom_call_target="tpu_custom_call" | custom-call | flops 900000000 | bytes 3000000 | tf_op jit(solution)/shard_map/pallas_call | solution.py:171
  14.1 0.0 collective-permute-done.near_ref
  14.1 0.0 collective-permute-done.1.far_ref
  14.1 0.0 copy-start.8
  14.1 0.0 copy-start.10
  14.2 0.0 copy-start.2
  14.2 30.1 %shard_map.132 = (f32[6,2,16,128]{3,2,1,0:T(8,128)S(1)}, f32[6,2,16,128]{3,2,1,0:T(8,128)S(1)}, f32[6,2,16,128]{3,2,1,0:T(8,128)S(1)}, f32[6,2,16,128]{3,2,1,0:T(8,128)S(1)}, f32[12,384]{1,0:T(8,128)S(1)}) custom-call(s32[1]{0:T(128)} %bitcast.1.tile_ref, s32[1]{0:T(128)} %bitcast.mem_ref, f32[2,6,16,512]{3,2,1,0:T(8,128)S(1)} %get-tuple-element.20.field_ref, ...), custom_call_target="tpu_custom_call" | custom-call | tf_op jit(solution)/shard_map/pallas_call | solution.py:522
  44.3 4.3 %collective-permute-start.2 = (f32[12,384]{1,0:T(8,128)S(1)}, f32[12,384]{1,0:T(8,128)S(1)}, u32[]{:S(2)}, u32[]{:S(2)}) collective-permute-start(f32[12,384]{1,0:T(8,128)S(1)} %get-tuple-element.27), channel_id=1, source_target_pairs={{0,1},{1,0},{2,3},{3,2},{4,5},{5,4},{6,7},{7,6},{8,9},{9,8},{10,11... | collective-permute-start | bytes 55304 | tf_op jit(solution)/shard_map/ppermute | solution.py:623
  48.6 1.6 %collective-permute-start.3 = (f32[12,384]{1,0:T(8,128)S(1)}, f32[12,384]{1,0:T(8,128)S(1)}, u32[]{:S(2)}, u32[]{:S(2)}) collective-permute-start(f32[12,384]{1,0:T(8,128)S(1)} %get-tuple-element.27), channel_id=1, source_target_pairs={{0,2},{1,3},{2,0},{3,1},{4,6},{5,7},{6,4},{7,5},{8,10},{9,11},{10,... | collective-permute-start | bytes 55304 | tf_op jit(solution)/shard_map/ppermute | solution.py:623
  50.2 0.0 collective-permute-start.4
  50.2 0.2 collective-permute-done.2
  50.5 2.0 %collective-permute-done.3 = f32[12,384]{1,0:T(8,128)S(1)} collective-permute-done((f32[12,384]{1,0:T(8,128)S(1)}, f32[12,384]{1,0:T(8,128)S(1)}, u32[]{:S(2)}, u32[]{:S(2)}) %collective-permute-start.3) | collective-permute-done | bytes 18464 | tf_op jit(solution)/shard_map/ppermute | solution.py:623
  52.5 2.5 %collective-permute-done.4 = f32[12,384]{1,0:T(8,128)S(1)} collective-permute-done((f32[12,384]{1,0:T(8,128)S(1)}, f32[12,384]{1,0:T(8,128)S(1)}, u32[]{:S(2)}, u32[]{:S(2)}) %collective-permute-start.4) | collective-permute-done | bytes 18464 | tf_op jit(solution)/shard_map/ppermute | solution.py:623
  55.0 1.1 %collective-permute-start.5 = (f32[12,384]{1,0:T(8,128)S(1)}, f32[12,384]{1,0:T(8,128)S(1)}, u32[]{:S(2)}, u32[]{:S(2)}) collective-permute-start(f32[12,384]{1,0:T(8,128)S(1)} %add_add_fusion), channel_id=1, source_target_pairs={{0,4},{1,5},{2,6},{3,7},{4,0},{5,1},{6,2},{7,3},{8,12},{9,13},{10,... | collective-permute-start | bytes 55304 | tf_op jit(solution)/shard_map/ppermute | solution.py:623
  56.0 1.5 %collective-permute-start.10 = (f32[6,2,16,128]{3,2,1,0:T(8,128)S(1)}, f32[6,2,16,128]{3,2,1,0:T(8,128)S(1)}, u32[]{:S(2)}, u32[]{:S(2)}) collective-permute-start(f32[6,2,16,128]{3,2,1,0:T(8,128)S(1)} %get-tuple-element.30), channel_id=1, source_target_pairs={{0,16},{8,24},{16,0},{24,8},{1,17},{9,25},{17,1},{25,9},{2,18},{10... | collective-permute-start | bytes 294920 | tf_op jit(solution)/shard_map/ppermute | solution.py:612
  57.5 0.7 %collective-permute-start.9 = (f32[6,2,16,128]{3,2,1,0:T(8,128)S(1)}, f32[6,2,16,128]{3,2,1,0:T(8,128)S(1)}, u32[]{:S(2)}, u32[]{:S(2)}) collective-permute-start(f32[6,2,16,128]{3,2,1,0:T(8,128)S(1)} %get-tuple-element.29), channel_id=1, source_target_pairs={{0,8},{8,0},{16,24},{24,16},{1,9},{9,1},{17,25},{25,17},{2,10},{10... | collective-permute-start | bytes 294920 | tf_op jit(solution)/shard_map/ppermute | solution.py:612
  58.2 1.7 %collective-permute-done.5 = f32[12,384]{1,0:T(8,128)S(1)} collective-permute-done((f32[12,384]{1,0:T(8,128)S(1)}, f32[12,384]{1,0:T(8,128)S(1)}, u32[]{:S(2)}, u32[]{:S(2)}) %collective-permute-start.5) | collective-permute-done | bytes 18464 | tf_op jit(solution)/shard_map/ppermute | solution.py:623
  59.9 0.1 collective-permute-start.6
  60.0 1.5 %collective-permute-start.7 = (f32[6,640]{1,0:T(8,128)S(1)}, f32[6,640]{1,0:T(8,128)S(1)}, u32[]{:S(2)}, u32[]{:S(2)}) collective-permute-start(f32[6,640]{1,0:T(8,128)S(1)} %pad_maximum_fusion.refs_0_), channel_id=1, source_target_pairs={{0,16},{8,24},{16,0},{24,8},{1,17},{9,25},{17,1},{25,9},{2,18},{10... | collective-permute-start | bytes 46088 | tf_op jit(solution)/shard_map/ppermute | solution.py:612
  61.6 0.0 collective-permute-done.6.refs_1_
  61.6 0.9 %collective-permute-start.8 = (f32[6,640]{1,0:T(8,128)S(1)}, f32[6,640]{1,0:T(8,128)S(1)}, u32[]{:S(2)}, u32[]{:S(2)}) collective-permute-start(f32[6,640]{1,0:T(8,128)S(1)} %pad_maximum_fusion.refs_0_), channel_id=1, source_target_pairs={{0,24},{8,16},{16,8},{24,0},{1,25},{9,17},{17,9},{25,1},{2,26},{10... | collective-permute-start | bytes 46088 | tf_op jit(solution)/shard_map/ppermute | solution.py:612
  62.4 1.4 %collective-permute-done.7.refs_2_ = f32[6,640]{1,0:T(8,128)S(1)} collective-permute-done((f32[6,640]{1,0:T(8,128)S(1)}, f32[6,640]{1,0:T(8,128)S(1)}, u32[]{:S(2)}, u32[]{:S(2)}) %collective-permute-start.7) | collective-permute-done | bytes 15392 | tf_op jit(solution)/shard_map/ppermute | solution.py:612
  63.9 0.9 %collective-permute-done.8.refs_3_ = f32[6,640]{1,0:T(8,128)S(1)} collective-permute-done((f32[6,640]{1,0:T(8,128)S(1)}, f32[6,640]{1,0:T(8,128)S(1)}, u32[]{:S(2)}, u32[]{:S(2)}) %collective-permute-start.8) | collective-permute-done | bytes 15392 | tf_op jit(solution)/shard_map/ppermute | solution.py:612
  64.8 0.0 collective-permute-done.10.refs_6_
  64.8 0.0 collective-permute-done.11.refs_7_
  64.8 0.0 collective-permute-done.9.refs_5_
  64.8 1.6 %shard_map.133 = (f32[4,6,2,16,128]{4,3,2,1,0:T(8,128)}, f32[24,384]{1,0:T(8,128)}, f32[6,256]{1,0:T(8,128)}) custom-call(s32[1]{0:T(128)} %bitcast.mem_ref, f32[6,640]{1,0:T(8,128)S(1)} %pad_maximum_fusion.refs_0_, f32[6,640]{1,0:T(8,128)S(1)} %collective-permute-done.6.refs_1_, f32[6,640]{1,0:T(8,128)S(1)} %collective-permute-done.7.refs_2_, ...), custom_call_target="tpu_custom_call" | custom-call | tf_op jit(solution)/shard_map/pallas_call | solution.py:592
  (24 shorter events, 0.1 us)
Async XLA Ops:
  0.6 8.7 %copy-start.9 = (s32[384]{0:T(512)S(1)}, s32[384]{0:T(512)}, u32[]{:S(2)}) copy-start(s32[384]{0:T(512)} %param.19) | copy-start | bytes 4612
  0.6 8.7 %copy-start.5 = (bf16[9,64,64]{2,1,0:T(8,128)(2,1)S(1)}, bf16[9,64,64]{2,1,0:T(8,128)(2,1)}, u32[]{:S(2)}) copy-start(bf16[9,64,64]{2,1,0:T(8,128)(2,1)} %mid_ref.1) | copy-start | bytes 221188
  0.7 8.7 %copy-start.6 = (bf16[9,64]{1,0:T(8,128)(2,1)S(1)}, bf16[9,64]{1,0:T(8,128)(2,1)}, u32[]{:S(2)}) copy-start(bf16[9,64]{1,0:T(8,128)(2,1)} %in_ref.1) | copy-start | bytes 3460
  0.7 8.7 %copy-start.7 = (bf16[64]{0:T(256)(128)(2,1)S(1)}, bf16[64]{0:T(256)(128)(2,1)}, u32[]{:S(2)}) copy-start(bf16[64]{0:T(256)(128)(2,1)} %param.15) | copy-start | bytes 388
  5.7 8.4 %collective-permute-start = (bf16[96,512]{1,0:T(8,128)(2,1)}, bf16[96,512]{1,0:T(8,128)(2,1)S(1)}, u32[]{:S(2)}, u32[]{:S(2)}) collective-permute-start(bf16[96,512]{1,0:T(8,128)(2,1)} %get-tuple-element.21), channel_id=1, source_target_pairs={{0,1},{1,0},{2,3},{3,2},{4,5},{5,4},{6,7},{7,6},{8,9},{9,8},{10,11... | collective-permute-start | bytes 294920 | tf_op jit(solution)/shard_map/ppermute | solution.py:632
  8.7 5.4 %collective-permute-start.1 = (bf16[96,512]{1,0:T(8,128)(2,1)}, bf16[96,512]{1,0:T(8,128)(2,1)S(1)}, u32[]{:S(2)}, u32[]{:S(2)}) collective-permute-start(bf16[96,512]{1,0:T(8,128)(2,1)} %get-tuple-element.22), channel_id=1, source_target_pairs={{1,2},{2,1},{3,4},{4,3},{5,6},{6,5},{9,10},{10,9},{11,12},{12,11},... | collective-permute-start | bytes 294920 | tf_op jit(solution)/shard_map/ppermute | solution.py:631
  9.4 1.0 %copy-start.4 = (f32[2,6,16,512]{3,2,1,0:T(8,128)S(1)}, f32[2,6,16,512]{3,2,1,0:T(8,128)}, u32[]{:S(2)}) copy-start(f32[2,6,16,512]{3,2,1,0:T(8,128)} %get-tuple-element.19.field_hbm) | copy-start | bytes 1179652
  10.4 3.7 %copy-start = (f32[2,16,512]{2,1,0:T(8,128)S(1)}, f32[2,16,512]{2,1,0:T(8,128)}, u32[]{:S(2)}) copy-start(f32[2,16,512]{2,1,0:T(8,128)} %prev_ref.1) | copy-start | bytes 196612
  10.4 3.7 %copy-start.1 = (f32[2,16,512]{2,1,0:T(8,128)S(1)}, f32[2,16,512]{2,1,0:T(8,128)}, u32[]{:S(2)}) copy-start(f32[2,16,512]{2,1,0:T(8,128)} %src_ref.1) | copy-start | bytes 196612
  10.4 3.7 %copy-start.3 = (s32[384,8]{0,1:T(8,128)S(1)}, s32[384,8]{0,1:T(8,128)}, u32[]{:S(2)}) copy-start(s32[384,8]{0,1:T(8,128)} %param.18) | copy-start | bytes 36868
  14.1 45.8 %copy-start.8 = (f32[6,256]{1,0:T(8,128)S(1)}, f32[6,256]{1,0:T(8,128)}, u32[]{:S(2)}) copy-start(f32[6,256]{1,0:T(8,128)} %lat_hbm.1) | copy-start | bytes 18436
  14.1 48.3 %copy-start.10 = (f32[384]{0:T(512)S(1)}, f32[384]{0:T(512)}, u32[]{:S(2)}) copy-start(f32[384]{0:T(512)} %param.21) | copy-start | bytes 4612
  14.2 50.6 %copy-start.2 = (f32[24,384]{1,0:T(8,128)S(1)}, f32[24,384]{1,0:T(8,128)}, u32[]{:S(2)}) copy-start(f32[24,384]{1,0:T(8,128)} %refs_8_.1) | copy-start | bytes 110596
  44.3 6.1 %collective-permute-start.2 = (f32[12,384]{1,0:T(8,128)S(1)}, f32[12,384]{1,0:T(8,128)S(1)}, u32[]{:S(2)}, u32[]{:S(2)}) collective-permute-start(f32[12,384]{1,0:T(8,128)S(1)} %get-tuple-element.27), channel_id=1, source_target_pairs={{0,1},{1,0},{2,3},{3,2},{4,5},{5,4},{6,7},{7,6},{8,9},{9,8},{10,11... | collective-permute-start | bytes 55304 | tf_op jit(solution)/shard_map/ppermute | solution.py:623
  48.6 3.8 %collective-permute-start.3 = (f32[12,384]{1,0:T(8,128)S(1)}, f32[12,384]{1,0:T(8,128)S(1)}, u32[]{:S(2)}, u32[]{:S(2)}) collective-permute-start(f32[12,384]{1,0:T(8,128)S(1)} %get-tuple-element.27), channel_id=1, source_target_pairs={{0,2},{1,3},{2,0},{3,1},{4,6},{5,7},{6,4},{7,5},{8,10},{9,11},{10,... | collective-permute-start | bytes 55304 | tf_op jit(solution)/shard_map/ppermute | solution.py:623
  50.2 4.7 %collective-permute-start.4 = (f32[12,384]{1,0:T(8,128)S(1)}, f32[12,384]{1,0:T(8,128)S(1)}, u32[]{:S(2)}, u32[]{:S(2)}) collective-permute-start(f32[12,384]{1,0:T(8,128)S(1)} %get-tuple-element.27), channel_id=1, source_target_pairs={{0,3},{1,2},{2,1},{3,0},{4,7},{5,6},{6,5},{7,4},{8,11},{9,10},{10,... | collective-permute-start | bytes 55304 | tf_op jit(solution)/shard_map/ppermute | solution.py:623
  55.0 4.9 %collective-permute-start.5 = (f32[12,384]{1,0:T(8,128)S(1)}, f32[12,384]{1,0:T(8,128)S(1)}, u32[]{:S(2)}, u32[]{:S(2)}) collective-permute-start(f32[12,384]{1,0:T(8,128)S(1)} %add_add_fusion), channel_id=1, source_target_pairs={{0,4},{1,5},{2,6},{3,7},{4,0},{5,1},{6,2},{7,3},{8,12},{9,13},{10,... | collective-permute-start | bytes 55304 | tf_op jit(solution)/shard_map/ppermute | solution.py:623
  56.0 8.7 %collective-permute-start.10 = (f32[6,2,16,128]{3,2,1,0:T(8,128)S(1)}, f32[6,2,16,128]{3,2,1,0:T(8,128)S(1)}, u32[]{:S(2)}, u32[]{:S(2)}) collective-permute-start(f32[6,2,16,128]{3,2,1,0:T(8,128)S(1)} %get-tuple-element.30), channel_id=1, source_target_pairs={{0,16},{8,24},{16,0},{24,8},{1,17},{9,25},{17,1},{25,9},{2,18},{10... | collective-permute-start | bytes 294920 | tf_op jit(solution)/shard_map/ppermute | solution.py:612
  57.5 7.3 %collective-permute-start.11 = (f32[6,2,16,128]{3,2,1,0:T(8,128)S(1)}, f32[6,2,16,128]{3,2,1,0:T(8,128)S(1)}, u32[]{:S(2)}, u32[]{:S(2)}) collective-permute-start(f32[6,2,16,128]{3,2,1,0:T(8,128)S(1)} %get-tuple-element.31), channel_id=1, source_target_pairs={{0,24},{8,16},{16,8},{24,0},{1,25},{9,17},{17,9},{25,1},{2,26},{10... | collective-permute-start | bytes 294920 | tf_op jit(solution)/shard_map/ppermute | solution.py:612
  57.5 7.3 %collective-permute-start.9 = (f32[6,2,16,128]{3,2,1,0:T(8,128)S(1)}, f32[6,2,16,128]{3,2,1,0:T(8,128)S(1)}, u32[]{:S(2)}, u32[]{:S(2)}) collective-permute-start(f32[6,2,16,128]{3,2,1,0:T(8,128)S(1)} %get-tuple-element.29), channel_id=1, source_target_pairs={{0,8},{8,0},{16,24},{24,16},{1,9},{9,1},{17,25},{25,17},{2,10},{10... | collective-permute-start | bytes 294920 | tf_op jit(solution)/shard_map/ppermute | solution.py:612
  59.9 1.6 %collective-permute-start.6 = (f32[6,640]{1,0:T(8,128)S(1)}, f32[6,640]{1,0:T(8,128)S(1)}, u32[]{:S(2)}, u32[]{:S(2)}) collective-permute-start(f32[6,640]{1,0:T(8,128)S(1)} %pad_maximum_fusion.refs_0_), channel_id=1, source_target_pairs={{0,8},{8,0},{16,24},{24,16},{1,9},{9,1},{17,25},{25,17},{2,10},{10... | collective-permute-start | bytes 46088 | tf_op jit(solution)/shard_map/ppermute | solution.py:612
  60.0 3.8 %collective-permute-start.7 = (f32[6,640]{1,0:T(8,128)S(1)}, f32[6,640]{1,0:T(8,128)S(1)}, u32[]{:S(2)}, u32[]{:S(2)}) collective-permute-start(f32[6,640]{1,0:T(8,128)S(1)} %pad_maximum_fusion.refs_0_), channel_id=1, source_target_pairs={{0,16},{8,24},{16,0},{24,8},{1,17},{9,25},{17,1},{25,9},{2,18},{10... | collective-permute-start | bytes 46088 | tf_op jit(solution)/shard_map/ppermute | solution.py:612
  61.6 3.2 %collective-permute-start.8 = (f32[6,640]{1,0:T(8,128)S(1)}, f32[6,640]{1,0:T(8,128)S(1)}, u32[]{:S(2)}, u32[]{:S(2)}) collective-permute-start(f32[6,640]{1,0:T(8,128)S(1)} %pad_maximum_fusion.refs_0_), channel_id=1, source_target_pairs={{0,24},{8,16},{16,8},{24,0},{1,25},{9,17},{17,9},{25,1},{2,26},{10... | collective-permute-start | bytes 46088 | tf_op jit(solution)/shard_map/ppermute | solution.py:612

commit v5 on v4

--- a/solution.py
+++ b/solution.py
@@ -9,7 +9,7 @@
 from jax.sharding import PartitionSpec as P
 
 SWEEPS = 2
-PACKED = 96
+PACKED = 80
 HALO = 4
 RING = 24
 LIFT_BLOCKS = 11
@@ -120,29 +120,11 @@
     lift_block(pt_ref[...], win, put_lift, put_side)
 
 
-def early_kernel(
-    grid_rows,
-    tile_ref,
-    field_hbm,
-    in_ref,
-    mid_ref,
-    out_ref,
-    field_ref,
-    win_ref,
-    wmix_ref,
-    gain_ref,
-    pt_ref,
-    t_scr,
-    sem,
-):
+def early_kernel(field_ref, pt_ref, t_scr):
     layers, members, rows, width = field_ref.shape
     groups = layers * members
     steps = width // (2 * SEG)
     block_rows = width // 2
-    copy = pltpu.make_async_copy(field_hbm, field_ref, sem)
-    copy.start()
-    place_weights(tile_ref[0], grid_rows, rows, in_ref, mid_ref, out_ref, win_ref, wmix_ref, gain_ref)
-    copy.wait()
 
     def load(pair, _):
         parts = []
@@ -165,27 +147,42 @@
     lax.fori_loop(0, groups // 2, load, 0)
 
 
-def early(tile_vec, grid_rows, field, conv_in, conv_mid, conv_out):
+def early(field):
     layers, members, rows, width = field.shape
     total = layers * members * width // 2
     return pl.pallas_call(
-        functools.partial(early_kernel, grid_rows),
-        in_specs=[SMEM, pl.BlockSpec(memory_space=pltpu.HBM)] + [VMEM] * 3,
-        out_specs=[VMEM] * 5,
-        out_shape=[
-            jax.ShapeDtypeStruct(field.shape, F32),
-            jax.ShapeDtypeStruct((LIFT_BLOCKS, 256, 256), BF),
-            jax.ShapeDtypeStruct((1024, 256), BF),
-            jax.ShapeDtypeStruct((16, 128), F32),
-            jax.ShapeDtypeStruct((total, 256), BF),
-        ],
-        scratch_shapes=[pltpu.VMEM((width + 8, 128), F32), pltpu.SemaphoreType.DMA],
+        early_kernel,
+        in_specs=[VMEM],
+        out_specs=VMEM,
+        out_shape=jax.ShapeDtypeStruct((total, 256), BF),
+        scratch_shapes=[pltpu.VMEM((width + 8, 128), F32)],
         compiler_params=pltpu.CompilerParams(vmem_limit_bytes=16 * 2**20),
         cost_estimate=pl.CostEstimate(flops=900_000_000, bytes_accessed=3_000_000, transcendentals=0),
-    )(tile_vec, field, conv_in, conv_mid, conv_out)
-
-
-def field_kernel(tile_ref, lat_hbm, basis_ref, prev_hbm, src_hbm, field_ref, near_ref, far_ref, held, lat_ref, prev_ref, src_ref, sems):
+    )(field)
+
+
+def field_kernel(
+    grid_rows,
+    tile_ref,
+    lat_hbm,
+    basis_ref,
+    prev_hbm,
+    src_hbm,
+    in_ref,
+    mid_ref,
+    out_ref,
+    field_ref,
+    near_ref,
+    far_ref,
+    win_ref,
+    wmix_ref,
+    gain_ref,
+    held,
+    lat_ref,
+    prev_ref,
+    src_ref,
+    sems,
+):
     chunks, comps, layers, rows, width = held.shape
     members, total = lat_ref.shape
     span = comps * rows
@@ -198,6 +195,7 @@
     ]
     for copy in small[:1] + copies + small[1:]:
         copy.start()
+    place_weights(tile_ref[0], grid_rows, rows, in_ref, mid_ref, out_ref, win_ref, wmix_ref, gain_ref)
     even_tile = tile_ref[0] & 1 == 0
     shape = (PACKED, 2 * (layers * members + 2 * layers) * rows)
     picks = [packed_from(layers, members, rows, up, shape) for up in (even_tile, jnp.logical_not(even_tile))]
@@ -230,12 +228,12 @@
     groups = layers * members
     r, at = iota((shape[0], 1), 0), iota(shape, 1)
     last = jnp.where(upper, 1, 0)
-    group = (r * 43) >> 8
-    j = r - 6 * group
+    group = (r * 52) >> 8
+    j = r - 5 * group
     row_hi = jnp.where(last == 1, rows - HALO + j, j)
-    row_lo = jnp.where(last == 1, rows - 2 + j - HALO, j - HALO)
+    row_lo = jnp.where(last == 1, rows - 1, 0)
     field = jnp.where(j < HALO, group * rows + row_hi, (groups + group) * rows + row_lo)
-    p = r - 6 * groups
+    p = r - 5 * groups
     half, j = (p >> 1) & 1, p & 1
     prev = (2 * groups + half * layers + (p >> 2)) * rows + jnp.where(last == 1, rows - 2 + j, j)
     s = p - 4 * layers
@@ -254,30 +252,33 @@
     near = jnp.where(up == 1, j - 2, j)
     close = mine & (near >= 0) & (near < 2)
     z = group - groups
-    hi = jnp.where(z < 0, group * 6 + j, 6 * groups + z * 4 + near)
-    lo = jnp.where(z < 0, group * 6 + HALO + near, 6 * groups + z * 4 + 2 + near)
+    hi = jnp.where(z < 0, group * 5 + j, 5 * groups + z * 4 + near)
+    lo = jnp.where(z < 0, group * 5 + HALO, 5 * groups + z * 4 + 2 + near)
     is_src = z >= layers
-    src = 6 * groups + 4 * layers + 2 * (z - layers)
+    src = 5 * groups + 4 * layers + 2 * (z - layers)
     edge = close & (jnp.where(up == 1, near, 1 - near) == 1)
     hi = jnp.where(is_src, src, hi)
     lo = jnp.where(is_src, src + 1, lo)
     use_hi = (z < 0) & mine | (z >= 0) & (z < layers) & close | is_src & edge
-    use_lo = (z < layers) & close | is_src & edge
+    use_lo = (z >= 0) & (z < layers) & close | (z < 0) & edge | is_src & edge
     return jnp.where(use_hi & (at == hi) | use_lo & (at == lo), 1.0, 0.0).astype(BF)
 
 
-def field_of(tile_vec, latents, basis, prev, src):
+def field_of(tile_vec, grid_rows, latents, basis, prev, src, conv_in, conv_mid, conv_out):
     total, layers, rows, width = basis.shape
     members = latents.shape[0]
     comps = 32
     return pl.pallas_call(
-        field_kernel,
-        in_specs=[SMEM] + [pl.BlockSpec(memory_space=pltpu.HBM)] * 4,
-        out_specs=[VMEM] * 3,
+        functools.partial(field_kernel, grid_rows),
+        in_specs=[SMEM] + [pl.BlockSpec(memory_space=pltpu.HBM)] * 4 + [VMEM] * 3,
+        out_specs=[VMEM] * 6,
         out_shape=[
-            jax.ShapeDtypeStruct((layers, members, rows, width), F32),
-            jax.ShapeDtypeStruct((PACKED, width), BF),
-            jax.ShapeDtypeStruct((PACKED, width), BF),
+            pltpu.VMEM((layers, members, rows, width), F32),
+            pltpu.VMEM((PACKED, width), BF),
+            pltpu.VMEM((PACKED, width), BF),
+            pltpu.VMEM((LIFT_BLOCKS, 256, 256), BF),
+            pltpu.VMEM((1024, 256), BF),
+            pltpu.VMEM((16, 128), F32),
         ],
         scratch_shapes=[
             pltpu.VMEM((total // comps, comps, layers, rows, width), BF),
@@ -287,7 +288,7 @@
             pltpu.SemaphoreType.DMA((total // comps + 3,)),
         ],
         compiler_params=pltpu.CompilerParams(vmem_limit_bytes=57 * 2**20),
-    )(tile_vec, latents, basis, prev, src)
+    )(tile_vec, latents, basis, prev, src, conv_in, conv_mid, conv_out)
 
 
 def target(me, k, count):
@@ -653,9 +654,11 @@
     tile_vec = lax.axis_index("tile").astype(jnp.int32).reshape(1)
     mem_vec = lax.axis_index("mem").astype(jnp.int32).reshape(1)
 
-    field, near, far = field_of(tile_vec, latents, basis, pressure_prev, source)
+    field, near, far, *weights = field_of(
+        tile_vec, grid_rows, latents, basis, pressure_prev, source, conv_in, conv_mid, conv_out.reshape(1, -1)
+    )
     near, far = halo(near, far, "tile")
-    field, *weights = early(tile_vec, grid_rows, field, conv_in, conv_mid, conv_out.reshape(1, -1))
+    weights.append(early(field))
     *press, sums = decode(
         parts, tile_vec, mem_vec, grid_rows, field, near, far, pressure_prev, source,
         weights, perf_cells.T, perf_count.reshape(1, -1),

time: 66.5 us -> 64.9 us (0.976)
  starting transfers between devices: 15.3 us -> 17.9 us
  waiting for transfers between devices: 8.78 us -> 6.54 us
  local copies, waits for them, and re-layouts: 1.04 us -> 0.05 us
  Pallas kernels: 40.3 us -> 39.4 us
    ppermute x4, starting transfers between devices: 7 us -> 9.46 us  [summed(): lax.ppermute(own, axis, [(i, i ^ j) for i in range(count)])]
    ppermute x4, waiting for transfers between devices: 6.44 us -> 4.2 us  [summed(): lax.ppermute(own, axis, [(i, i ^ j) for i in range(count)])]
    unnamed x22 -> x14, local copies, waits for them, and re-layouts: 1.04 us -> 0.04 us
    pallas_call x2, Pallas kernels: 8.63 us -> 7.79 us  [the longest x1 5.47 us: field_of(): pl.pallas_call(functools.partial(field_kernel, grid_rows), in_specs=[SMEM...]
  transfers between devices with their start and end apart: 12 -> 12, of which waited for: 6 -> 5; matrix products, arithmetic and copies ran while one was open for 0% -> 0% of each run, Pallas kernels for 6% -> 4%
where the time goes in v5:
time: 64.9 us; the launch traced here: 64.8 us
  Pallas kernels  39.4 us (61%)
  starting transfers between devices  17.9 us (28%)
  waiting for transfers between devices  6.54 us (10%)
  between operations  0.83 us (1%)
    pallas_call x1, Pallas kernels, decode(): pl.pallas_call(functools.partial(decode_kernel, grid_rows), in_specs=[SME...  30.1 us
    ppermute x4, starting transfers between devices, summed(): lax.ppermute(own, axis, [(i, i ^ j) for i in range(count)])  9.46 us
    pallas_call x1, Pallas kernels, field_of(): pl.pallas_call(functools.partial(field_kernel, grid_rows), in_specs=[SMEM...  5.47 us
    ppermute x6, starting transfers between devices, gathered(): lax.ppermute(pieces[k], axis, [(i, target(i, k, count)) for i in range(co...  4.77 us
    ppermute x4, waiting for transfers between devices, summed(): lax.ppermute(own, axis, [(i, i ^ j) for i in range(count)])  4.2 us
    ppermute x1, starting transfers between devices, halo(): return (lax.ppermute(near, axis, swap(0)), far)  3.03 us
    ppermute x6, waiting for transfers between devices, gathered(): lax.ppermute(pieces[k], axis, [(i, target(i, k, count)) for i in range(co...  2.34 us
    pallas_call x1, Pallas kernels, early(): pl.pallas_call(early_kernel, in_specs=[VMEM], out_specs=VMEM, out_shape=j...  2.33 us
  transfers between devices with their start and end apart: 12, of which 5 were waited for; matrix products, arithmetic and copies ran while one was open for 0% of the time, Pallas kernels for 4%

profile of v5, /device:TPU:0, one launch (start us, length us, event | category | flops | bytes accessed | tf_op | source)
XLA Modules:
  0.0 64.8 jit_solution(2822201610860311053)
XLA Ops:
  0.6 5.5 %shard_map.130 = (f32[2,6,16,512]{3,2,1,0:T(8,128)S(1)}, bf16[80,512]{1,0:T(8,128)(2,1)S(1)}, bf16[80,512]{1,0:T(8,128)(2,1)S(1)}, bf16[11,256,256]{2,1,0:T(8,12...) custom-call(s32[1]{0:T(128)} %bitcast.1.tile_ref, f32[6,256]{1,0:T(8,128)} %lat_hbm.1, ...), custom_call_target="tpu_custom_call" | custom-call | tf_op jit(solution)/shard_map/pallas_call | solution.py:271
  6.1 3.0 %collective-permute-start = (bf16[80,512]{1,0:T(8,128)(2,1)S(1)}, bf16[80,512]{1,0:T(8,128)(2,1)S(1)}, u32[]{:S(2)}, u32[]{:S(2)}) collective-permute-start(bf16[80,512]{1,0:T(8,128)(2,1)S(1)} %get-tuple-element.18), channel_id=1, source_target_pairs={{0,1},{1,0},{2,3},{3,2},{4,5},{5,4},{6,7},{7,6},{8,9},{9,8},{10,11... | collective-permute-start | bytes 245768 | tf_op jit(solution)/shard_map/ppermute | solution.py:633
  9.2 0.7 %collective-permute-start.1 = (bf16[80,512]{1,0:T(8,128)(2,1)S(1)}, bf16[80,512]{1,0:T(8,128)(2,1)S(1)}, u32[]{:S(2)}, u32[]{:S(2)}) collective-permute-start(bf16[80,512]{1,0:T(8,128)(2,1)S(1)} %get-tuple-element.19), channel_id=1, source_target_pairs={{1,2},{2,1},{3,4},{4,3},{5,6},{6,5},{9,10},{10,9},{11,12},{12,11},... | collective-permute-start | bytes 245768 | tf_op jit(solution)/shard_map/ppermute | solution.py:632
  9.8 0.0 copy-start
  9.9 0.0 copy-start.1
  9.9 0.0 copy-start.3
  9.9 2.3 %shard_map.131.early_pt_ref = bf16[3072,256]{1,0:T(8,128)(2,1)S(1)} custom-call(f32[2,6,16,512]{3,2,1,0:T(8,128)S(1)} %get-tuple-element.17.field_ref), custom_call_target="tpu_custom_call" | custom-call | flops 900000000 | bytes 3000000 | tf_op jit(solution)/shard_map/pallas_call | solution.py:153
  12.2 0.0 collective-permute-done.near_ref
  12.2 0.0 collective-permute-done.1.far_ref
  12.3 0.0 copy-start.4
  12.3 0.0 copy-start.6
  12.3 0.0 copy-start.2
  12.3 30.1 %shard_map.132 = (f32[6,2,16,128]{3,2,1,0:T(8,128)S(1)}, f32[6,2,16,128]{3,2,1,0:T(8,128)S(1)}, f32[6,2,16,128]{3,2,1,0:T(8,128)S(1)}, f32[6,2,16,128]{3,2,1,0:T(8,128)S(1)}, f32[12,384]{1,0:T(8,128)S(1)}) custom-call(s32[1]{0:T(128)} %bitcast.1.tile_ref, s32[1]{0:T(128)} %bitcast.mem_ref, f32[2,6,16,512]{3,2,1,0:T(8,128)S(1)} %get-tuple-element.17.field_ref, ...), custom_call_target="tpu_custom_call" | custom-call | tf_op jit(solution)/shard_map/pallas_call | solution.py:523
  42.4 4.4 %collective-permute-start.2 = (f32[12,384]{1,0:T(8,128)S(1)}, f32[12,384]{1,0:T(8,128)S(1)}, u32[]{:S(2)}, u32[]{:S(2)}) collective-permute-start(f32[12,384]{1,0:T(8,128)S(1)} %get-tuple-element.23), channel_id=1, source_target_pairs={{0,1},{1,0},{2,3},{3,2},{4,5},{5,4},{6,7},{7,6},{8,9},{9,8},{10,11... | collective-permute-start | bytes 55304 | tf_op jit(solution)/shard_map/ppermute | solution.py:624
  46.7 1.9 %collective-permute-start.3 = (f32[12,384]{1,0:T(8,128)S(1)}, f32[12,384]{1,0:T(8,128)S(1)}, u32[]{:S(2)}, u32[]{:S(2)}) collective-permute-start(f32[12,384]{1,0:T(8,128)S(1)} %get-tuple-element.23), channel_id=1, source_target_pairs={{0,2},{1,3},{2,0},{3,1},{4,6},{5,7},{6,4},{7,5},{8,10},{9,11},{10,... | collective-permute-start | bytes 55304 | tf_op jit(solution)/shard_map/ppermute | solution.py:624
  48.7 1.0 %collective-permute-start.4 = (f32[12,384]{1,0:T(8,128)S(1)}, f32[12,384]{1,0:T(8,128)S(1)}, u32[]{:S(2)}, u32[]{:S(2)}) collective-permute-start(f32[12,384]{1,0:T(8,128)S(1)} %get-tuple-element.23), channel_id=1, source_target_pairs={{0,3},{1,2},{2,1},{3,0},{4,7},{5,6},{6,5},{7,4},{8,11},{9,10},{10,... | collective-permute-start | bytes 55304 | tf_op jit(solution)/shard_map/ppermute | solution.py:624
  49.6 0.0 collective-permute-done.2
  49.6 1.0 %collective-permute-done.3 = f32[12,384]{1,0:T(8,128)S(1)} collective-permute-done((f32[12,384]{1,0:T(8,128)S(1)}, f32[12,384]{1,0:T(8,128)S(1)}, u32[]{:S(2)}, u32[]{:S(2)}) %collective-permute-start.3) | collective-permute-done | bytes 18464 | tf_op jit(solution)/shard_map/ppermute | solution.py:624
  50.6 2.8 %collective-permute-done.4 = f32[12,384]{1,0:T(8,128)S(1)} collective-permute-done((f32[12,384]{1,0:T(8,128)S(1)}, f32[12,384]{1,0:T(8,128)S(1)}, u32[]{:S(2)}, u32[]{:S(2)}) %collective-permute-start.4) | collective-permute-done | bytes 18464 | tf_op jit(solution)/shard_map/ppermute | solution.py:624
  53.4 2.2 %collective-permute-start.5 = (f32[12,384]{1,0:T(8,128)S(1)}, f32[12,384]{1,0:T(8,128)S(1)}, u32[]{:S(2)}, u32[]{:S(2)}) collective-permute-start(f32[12,384]{1,0:T(8,128)S(1)} %add_add_fusion), channel_id=1, source_target_pairs={{0,4},{1,5},{2,6},{3,7},{4,0},{5,1},{6,2},{7,3},{8,12},{9,13},{10,... | collective-permute-start | bytes 55304 | tf_op jit(solution)/shard_map/ppermute | solution.py:624
  55.6 1.5 %collective-permute-start.10 = (f32[6,2,16,128]{3,2,1,0:T(8,128)S(1)}, f32[6,2,16,128]{3,2,1,0:T(8,128)S(1)}, u32[]{:S(2)}, u32[]{:S(2)}) collective-permute-start(f32[6,2,16,128]{3,2,1,0:T(8,128)S(1)} %get-tuple-element.26), channel_id=1, source_target_pairs={{0,16},{8,24},{16,0},{24,8},{1,17},{9,25},{17,1},{25,9},{2,18},{10... | collective-permute-start | bytes 294920 | tf_op jit(solution)/shard_map/ppermute | solution.py:613
  57.1 0.0 collective-permute-start.11
  57.1 0.7 %collective-permute-start.9 = (f32[6,2,16,128]{3,2,1,0:T(8,128)S(1)}, f32[6,2,16,128]{3,2,1,0:T(8,128)S(1)}, u32[]{:S(2)}, u32[]{:S(2)}) collective-permute-start(f32[6,2,16,128]{3,2,1,0:T(8,128)S(1)} %get-tuple-element.25), channel_id=1, source_target_pairs={{0,8},{8,0},{16,24},{24,16},{1,9},{9,1},{17,25},{25,17},{2,10},{10... | collective-permute-start | bytes 294920 | tf_op jit(solution)/shard_map/ppermute | solution.py:613
  57.8 0.4 collective-permute-done.5
  58.2 0.1 collective-permute-start.6
  58.3 1.7 %collective-permute-start.7 = (f32[6,640]{1,0:T(8,128)S(1)}, f32[6,640]{1,0:T(8,128)S(1)}, u32[]{:S(2)}, u32[]{:S(2)}) collective-permute-start(f32[6,640]{1,0:T(8,128)S(1)} %pad_maximum_fusion.refs_0_), channel_id=1, source_target_pairs={{0,16},{8,24},{16,0},{24,8},{1,17},{9,25},{17,1},{25,9},{2,18},{10... | collective-permute-start | bytes 46088 | tf_op jit(solution)/shard_map/ppermute | solution.py:613
  60.0 0.0 collective-permute-done.6.refs_1_
  60.0 0.9 %collective-permute-start.8 = (f32[6,640]{1,0:T(8,128)S(1)}, f32[6,640]{1,0:T(8,128)S(1)}, u32[]{:S(2)}, u32[]{:S(2)}) collective-permute-start(f32[6,640]{1,0:T(8,128)S(1)} %pad_maximum_fusion.refs_0_), channel_id=1, source_target_pairs={{0,24},{8,16},{16,8},{24,0},{1,25},{9,17},{17,9},{25,1},{2,26},{10... | collective-permute-start | bytes 46088 | tf_op jit(solution)/shard_map/ppermute | solution.py:613
  60.9 1.9 %collective-permute-done.7.refs_2_ = f32[6,640]{1,0:T(8,128)S(1)} collective-permute-done((f32[6,640]{1,0:T(8,128)S(1)}, f32[6,640]{1,0:T(8,128)S(1)}, u32[]{:S(2)}, u32[]{:S(2)}) %collective-permute-start.7) | collective-permute-done | bytes 15392 | tf_op jit(solution)/shard_map/ppermute | solution.py:613
  62.8 0.4 collective-permute-done.8.refs_3_
  63.2 0.0 collective-permute-done.9.refs_5_
  63.2 1.6 %shard_map.133 = (f32[4,6,2,16,128]{4,3,2,1,0:T(8,128)}, f32[24,384]{1,0:T(8,128)}, f32[6,256]{1,0:T(8,128)}) custom-call(s32[1]{0:T(128)} %bitcast.mem_ref, f32[6,640]{1,0:T(8,128)S(1)} %pad_maximum_fusion.refs_0_, f32[6,640]{1,0:T(8,128)S(1)} %collective-permute-done.6.refs_1_, f32[6,640]{1,0:T(8,128)S(1)} %collective-permute-done.7.refs_2_, ...), custom_call_target="tpu_custom_call" | custom-call | tf_op jit(solution)/shard_map/pallas_call | solution.py:593
  (16 shorter events, 0.1 us)
Async XLA Ops:
  0.6 9.2 %copy-start.5 = (s32[384]{0:T(512)S(1)}, s32[384]{0:T(512)}, u32[]{:S(2)}) copy-start(s32[384]{0:T(512)} %param.19) | copy-start | bytes 4612
  6.1 6.1 %collective-permute-start = (bf16[80,512]{1,0:T(8,128)(2,1)S(1)}, bf16[80,512]{1,0:T(8,128)(2,1)S(1)}, u32[]{:S(2)}, u32[]{:S(2)}) collective-permute-start(bf16[80,512]{1,0:T(8,128)(2,1)S(1)} %get-tuple-element.18), channel_id=1, source_target_pairs={{0,1},{1,0},{2,3},{3,2},{4,5},{5,4},{6,7},{7,6},{8,9},{9,8},{10,11... | collective-permute-start | bytes 245768 | tf_op jit(solution)/shard_map/ppermute | solution.py:633
  9.2 3.1 %collective-permute-start.1 = (bf16[80,512]{1,0:T(8,128)(2,1)S(1)}, bf16[80,512]{1,0:T(8,128)(2,1)S(1)}, u32[]{:S(2)}, u32[]{:S(2)}) collective-permute-start(bf16[80,512]{1,0:T(8,128)(2,1)S(1)} %get-tuple-element.19), channel_id=1, source_target_pairs={{1,2},{2,1},{3,4},{4,3},{5,6},{6,5},{9,10},{10,9},{11,12},{12,11},... | collective-permute-start | bytes 245768 | tf_op jit(solution)/shard_map/ppermute | solution.py:632
  9.8 2.4 %copy-start = (f32[2,16,512]{2,1,0:T(8,128)S(1)}, f32[2,16,512]{2,1,0:T(8,128)}, u32[]{:S(2)}) copy-start(f32[2,16,512]{2,1,0:T(8,128)} %prev_ref.1) | copy-start | bytes 196612
  9.9 2.4 %copy-start.1 = (f32[2,16,512]{2,1,0:T(8,128)S(1)}, f32[2,16,512]{2,1,0:T(8,128)}, u32[]{:S(2)}) copy-start(f32[2,16,512]{2,1,0:T(8,128)} %src_ref.1) | copy-start | bytes 196612
  9.9 2.4 %copy-start.3 = (s32[384,8]{0,1:T(8,128)S(1)}, s32[384,8]{0,1:T(8,128)}, u32[]{:S(2)}) copy-start(s32[384,8]{0,1:T(8,128)} %param.18) | copy-start | bytes 36868
  12.3 46.0 %copy-start.4 = (f32[6,256]{1,0:T(8,128)S(1)}, f32[6,256]{1,0:T(8,128)}, u32[]{:S(2)}) copy-start(f32[6,256]{1,0:T(8,128)} %lat_hbm.1) | copy-start | bytes 18436
  12.3 48.6 %copy-start.6 = (f32[384]{0:T(512)S(1)}, f32[384]{0:T(512)}, u32[]{:S(2)}) copy-start(f32[384]{0:T(512)} %param.21) | copy-start | bytes 4612
  12.3 50.9 %copy-start.2 = (f32[24,384]{1,0:T(8,128)S(1)}, f32[24,384]{1,0:T(8,128)}, u32[]{:S(2)}) copy-start(f32[24,384]{1,0:T(8,128)} %refs_8_.1) | copy-start | bytes 110596
  42.4 7.2 %collective-permute-start.2 = (f32[12,384]{1,0:T(8,128)S(1)}, f32[12,384]{1,0:T(8,128)S(1)}, u32[]{:S(2)}, u32[]{:S(2)}) collective-permute-start(f32[12,384]{1,0:T(8,128)S(1)} %get-tuple-element.23), channel_id=1, source_target_pairs={{0,1},{1,0},{2,3},{3,2},{4,5},{5,4},{6,7},{7,6},{8,9},{9,8},{10,11... | collective-permute-start | bytes 55304 | tf_op jit(solution)/shard_map/ppermute | solution.py:624
  46.7 3.8 %collective-permute-start.3 = (f32[12,384]{1,0:T(8,128)S(1)}, f32[12,384]{1,0:T(8,128)S(1)}, u32[]{:S(2)}, u32[]{:S(2)}) collective-permute-start(f32[12,384]{1,0:T(8,128)S(1)} %get-tuple-element.23), channel_id=1, source_target_pairs={{0,2},{1,3},{2,0},{3,1},{4,6},{5,7},{6,4},{7,5},{8,10},{9,11},{10,... | collective-permute-start | bytes 55304 | tf_op jit(solution)/shard_map/ppermute | solution.py:624
  48.7 4.7 %collective-permute-start.4 = (f32[12,384]{1,0:T(8,128)S(1)}, f32[12,384]{1,0:T(8,128)S(1)}, u32[]{:S(2)}, u32[]{:S(2)}) collective-permute-start(f32[12,384]{1,0:T(8,128)S(1)} %get-tuple-element.23), channel_id=1, source_target_pairs={{0,3},{1,2},{2,1},{3,0},{4,7},{5,6},{6,5},{7,4},{8,11},{9,10},{10,... | collective-permute-start | bytes 55304 | tf_op jit(solution)/shard_map/ppermute | solution.py:624
  53.4 4.8 %collective-permute-start.5 = (f32[12,384]{1,0:T(8,128)S(1)}, f32[12,384]{1,0:T(8,128)S(1)}, u32[]{:S(2)}, u32[]{:S(2)}) collective-permute-start(f32[12,384]{1,0:T(8,128)S(1)} %add_add_fusion), channel_id=1, source_target_pairs={{0,4},{1,5},{2,6},{3,7},{4,0},{5,1},{6,2},{7,3},{8,12},{9,13},{10,... | collective-permute-start | bytes 55304 | tf_op jit(solution)/shard_map/ppermute | solution.py:624
  55.6 7.6 %collective-permute-start.10 = (f32[6,2,16,128]{3,2,1,0:T(8,128)S(1)}, f32[6,2,16,128]{3,2,1,0:T(8,128)S(1)}, u32[]{:S(2)}, u32[]{:S(2)}) collective-permute-start(f32[6,2,16,128]{3,2,1,0:T(8,128)S(1)} %get-tuple-element.26), channel_id=1, source_target_pairs={{0,16},{8,24},{16,0},{24,8},{1,17},{9,25},{17,1},{25,9},{2,18},{10... | collective-permute-start | bytes 294920 | tf_op jit(solution)/shard_map/ppermute | solution.py:613
  57.1 6.1 %collective-permute-start.11 = (f32[6,2,16,128]{3,2,1,0:T(8,128)S(1)}, f32[6,2,16,128]{3,2,1,0:T(8,128)S(1)}, u32[]{:S(2)}, u32[]{:S(2)}) collective-permute-start(f32[6,2,16,128]{3,2,1,0:T(8,128)S(1)} %get-tuple-element.27), channel_id=1, source_target_pairs={{0,24},{8,16},{16,8},{24,0},{1,25},{9,17},{17,9},{25,1},{2,26},{10... | collective-permute-start | bytes 294920 | tf_op jit(solution)/shard_map/ppermute | solution.py:613
  57.1 6.1 %collective-permute-start.9 = (f32[6,2,16,128]{3,2,1,0:T(8,128)S(1)}, f32[6,2,16,128]{3,2,1,0:T(8,128)S(1)}, u32[]{:S(2)}, u32[]{:S(2)}) collective-permute-start(f32[6,2,16,128]{3,2,1,0:T(8,128)S(1)} %get-tuple-element.25), channel_id=1, source_target_pairs={{0,8},{8,0},{16,24},{24,16},{1,9},{9,1},{17,25},{25,17},{2,10},{10... | collective-permute-start | bytes 294920 | tf_op jit(solution)/shard_map/ppermute | solution.py:613
  58.2 1.8 %collective-permute-start.6 = (f32[6,640]{1,0:T(8,128)S(1)}, f32[6,640]{1,0:T(8,128)S(1)}, u32[]{:S(2)}, u32[]{:S(2)}) collective-permute-start(f32[6,640]{1,0:T(8,128)S(1)} %pad_maximum_fusion.refs_0_), channel_id=1, source_target_pairs={{0,8},{8,0},{16,24},{24,16},{1,9},{9,1},{17,25},{25,17},{2,10},{10... | collective-permute-start | bytes 46088 | tf_op jit(solution)/shard_map/ppermute | solution.py:613
  58.3 4.5 %collective-permute-start.7 = (f32[6,640]{1,0:T(8,128)S(1)}, f32[6,640]{1,0:T(8,128)S(1)}, u32[]{:S(2)}, u32[]{:S(2)}) collective-permute-start(f32[6,640]{1,0:T(8,128)S(1)} %pad_maximum_fusion.refs_0_), channel_id=1, source_target_pairs={{0,16},{8,24},{16,0},{24,8},{1,17},{9,25},{17,1},{25,9},{2,18},{10... | collective-permute-start | bytes 46088 | tf_op jit(solution)/shard_map/ppermute | solution.py:613
  60.0 3.2 %collective-permute-start.8 = (f32[6,640]{1,0:T(8,128)S(1)}, f32[6,640]{1,0:T(8,128)S(1)}, u32[]{:S(2)}, u32[]{:S(2)}) collective-permute-start(f32[6,640]{1,0:T(8,128)S(1)} %pad_maximum_fusion.refs_0_), channel_id=1, source_target_pairs={{0,24},{8,16},{16,8},{24,0},{1,25},{9,17},{17,9},{25,1},{2,26},{10... | collective-permute-start | bytes 46088 | tf_op jit(solution)/shard_map/ppermute | solution.py:613
